TPU v7x, 32 devices: a whole 2x2x4 slice. The times are simulated.
32 devices in a mesh: dp: 8 (over y, x, core), tensor: 4 (over z).
Axes of the slice: x: 2, y: 2, z: 4, core: 2. Of those that a mesh axis runs over, the one named last changes fastest.
Arguments:
- inputs: bfloat16 [2048, 8192], P('dp', 'tensor'), may hold values from -6 to 6
- output_gradient: bfloat16 [2048, 8192], P('dp', 'tensor'), may hold values from -6 to 6
- frozen_weight: bfloat16 [8192, 8192], P(None, 'tensor'), may hold values from -0.0625 to 0.0625
- shrink_matrix_stack: bfloat16 [8, 8192, 64], P('dp', 'tensor'), may hold values from -0.0625 to 0.0625
- expand_matrix_stack: bfloat16 [8, 64, 8192], P('dp', None, 'tensor'), may hold values from -0.75 to 0.75
- adapter_index_rows: int32 [2048, 1], P('dp'), may hold values from 0 to 7; in each aligned block of 256 rows (0 to 255, 256 to 511, ...) at most 64 rows name the same one
- adapter_slot: int32 [8], replicated, may hold values from 0 to 7, each once
Outputs:
- projected_values: bfloat16 [2048, 8192], P('dp', 'tensor')
- activation_cotangent: bfloat16 [2048, 8192], P('dp', 'tensor')
- shrink_matrix_cotangent: bfloat16 [8, 8192, 64], P('dp', 'tensor')
- expand_matrix_cotangent: bfloat16 [8, 64, 8192], P('dp', None, 'tensor')
Inputs may be any that keep to these rules, and one draw needn't show every extreme that they name: `adapter_index_rows`: among the rows of one index of dp no adapter is named more than 64 times, and in some of these blocks one adapter is named exactly 64 times. `adapter_slot`: each slot holds exactly one adapter; the slot s lies with dp index s.
All inputs are finite; a program needn't handle non-finite values.
Results may differ from a plain program's by a relative error of at most 0.022.
Values may be sent and summed in bfloat16 or wider, within the bound.
No kernel may reach another device: no remote copies, remote signals or barrier semaphores. Data moves between devices by JAX's collectives and lax.ppermute only.
A program may use at most 128 MiB of HBM per device.

v0:
```python
import jax
import jax.numpy as jnp
from jax import lax
from jax.sharding import PartitionSpec as P

adapter_scale = 2.0


def body(
    inputs,
    output_gradient,
    frozen_weight,
    shrink_matrix_stack,
    expand_matrix_stack,
    adapter_index_rows,
    adapter_slot,
):
    tok_rows = inputs.shape[0]
    output_width = frozen_weight.shape[1]
    per_worker = shrink_matrix_stack.shape[0]
    adapter_groups = lax.axis_size("dp")
    slot_total = per_worker * adapter_groups
    frozen_output = jnp.dot(
        lax.all_gather(inputs, "tensor", axis=1, tiled=True),
        frozen_weight,
        preferred_element_type=jnp.float32,
    )
    back_part = lax.dot_general(
        output_gradient, frozen_weight, (((1,), (1,)), ((), ())), preferred_element_type=jnp.float32
    )
    frozen_backward = lax.psum_scatter(
        back_part.astype(jnp.bfloat16), "tensor", scatter_dimension=1, tiled=True
    ).astype(jnp.float32)
    adapter_indices = adapter_index_rows[:, 0]
    adapter_equality = adapter_indices[:, None] == jnp.arange(slot_total, dtype=jnp.int32)[None, :]
    slot_position = jnp.sum(jnp.where(adapter_equality, adapter_slot[None, :], 0), axis=1)
    slot_equality = slot_position[:, None] == jnp.arange(slot_total, dtype=jnp.int32)[None, :]
    slot_capacity = tok_rows // 4
    counted = jnp.cumsum(slot_equality.astype(jnp.int32), axis=0) - 1
    position = jnp.sum(jnp.where(slot_equality, counted, 0), axis=1)
    flattened = slot_position * slot_capacity + position
    outgoing_input = (
        jnp.zeros((slot_total * slot_capacity, output_width), jnp.bfloat16)
        .at[flattened]
        .set(inputs)
    )
    outgoing_output_gradient = (
        jnp.zeros((slot_total * slot_capacity, output_width), jnp.bfloat16)
        .at[flattened]
        .set(output_gradient)
    )
    outgoing_input = outgoing_input.reshape(
        adapter_groups, per_worker * slot_capacity, output_width
    )
    outgoing_output_gradient = outgoing_output_gradient.reshape(
        adapter_groups, per_worker * slot_capacity, output_width
    )
    received_input, received_output_gradient = (
        lax.all_to_all(outgoing_input, "dp", split_axis=0, concat_axis=0, tiled=True),
        lax.all_to_all(outgoing_output_gradient, "dp", split_axis=0, concat_axis=0, tiled=True),
    )
    received_input = received_input.reshape(adapter_groups, per_worker, slot_capacity, output_width)
    received_output_gradient = received_output_gradient.reshape(
        adapter_groups, per_worker, slot_capacity, output_width
    )
    reduced_portion = jnp.einsum(
        "zwki,wit->zwkt", received_input, shrink_matrix_stack, preferred_element_type=jnp.float32
    )
    gradient_portion = jnp.einsum(
        "zfey,fay->zfea",
        received_output_gradient,
        expand_matrix_stack,
        preferred_element_type=jnp.float32,
    )
    reduced_hidden, reduced_gradient = (
        lax.psum(reduced_portion.astype(jnp.bfloat16), "tensor").astype(jnp.float32),
        lax.psum(gradient_portion.astype(jnp.bfloat16), "tensor").astype(jnp.float32),
    )
    reduced_hidden = reduced_hidden.astype(jnp.bfloat16)
    reduced_gradient = (adapter_scale * reduced_gradient).astype(jnp.bfloat16)
    contribution = (
        adapter_scale
        * jnp.einsum(
            "ytqw,twl->ytql",
            reduced_hidden,
            expand_matrix_stack,
            preferred_element_type=jnp.float32,
        )
    ).astype(jnp.bfloat16)
    backward_result = jnp.einsum(
        "xhem,ham->xhea", reduced_gradient, shrink_matrix_stack, preferred_element_type=jnp.float32
    ).astype(jnp.bfloat16)
    expand_matrix_cotangent = (
        adapter_scale
        * jnp.einsum(
            "vitl,vitm->ilm",
            reduced_hidden,
            received_output_gradient,
            preferred_element_type=jnp.float32,
        )
    ).astype(jnp.bfloat16)
    shrink_matrix_cotangent = jnp.einsum(
        "sjcd,sjcr->jdr", received_input, reduced_gradient, preferred_element_type=jnp.float32
    ).astype(jnp.bfloat16)
    returned_contribution, returned_backward = (
        lax.all_to_all(
            contribution.reshape(adapter_groups, per_worker * slot_capacity, output_width),
            "dp",
            split_axis=0,
            concat_axis=0,
            tiled=True,
        ),
        lax.all_to_all(
            backward_result.reshape(adapter_groups, per_worker * slot_capacity, output_width),
            "dp",
            split_axis=0,
            concat_axis=0,
            tiled=True,
        ),
    )
    lowrank_delta_term = returned_contribution.reshape(slot_total * slot_capacity, output_width)[
        flattened
    ]
    lowrank_reverse_pass = returned_backward.reshape(slot_total * slot_capacity, output_width)[
        flattened
    ]
    projected_values = (frozen_output + lowrank_delta_term.astype(jnp.float32)).astype(jnp.bfloat16)
    activation_cotangent = (frozen_backward + lowrank_reverse_pass.astype(jnp.float32)).astype(
        jnp.bfloat16
    )
    return (
        projected_values,
        activation_cotangent,
        shrink_matrix_cotangent,
        expand_matrix_cotangent,
    )


def solution(mesh):
    return jax.shard_map(
        body,
        mesh=mesh,
        in_specs=(
            P("dp", "tensor"),
            P("dp", "tensor"),
            P(None, "tensor"),
            P("dp", "tensor", None),
            P("dp", None, "tensor"),
            P("dp", None),
            P(),
        ),
        out_specs=(
            P("dp", "tensor"),
            P("dp", "tensor"),
            P("dp", "tensor", None),
            P("dp", None, "tensor"),
        ),
        check_vma=False,
    )
```

profile of v0, /device:TPU:0, one launch (start us, length us, event | category | flops | bytes accessed | tf_op | source)
XLA Modules:
  0.0 283.3 jit_solution(16418947527570969068)
XLA Ops:
  7.2 0.0 copy-start
  7.2 0.8 select_reduce_fusion
  8.0 0.6 reduce-window.6
  8.6 0.2 slice_reduce_fusion
  8.8 0.1 fusion.18
  9.0 4.4 %scatter_custom_fusion.1 = bf16[512,2048]{1,0:T(8,128)(2,1)} fusion(s32[256]{0:T(256)S(1)} %bitcast.70, bf16[256,2048]{1,0:T(8,128)(2,1)} %param.8, bf16[]{:T(256)} %constant.6.clone.1), kind=kCustom, calls=%fused_computation.20 | custom fusion | bytes 2097664 | tf_op jit(solution)/shard_map/scatter | solution.py:50
  13.4 5.2 %all-to-all-start.2 = ((bf16[8,64,2048]{2,1,0:T(8,128)(2,1)}), bf16[8,64,2048]{2,1,0:T(8,128)(2,1)S(1)}, u32[]{:S(2)}, u32[]{:S(2)}) async-start(bf16[8,64,2048]{2,1,0:T(8,128)(2,1)} %bitcast.68), calls=%async_computation.3 | async-start | bytes 4194304 | tf_op jit(solution)/shard_map/all_to_all | solution.py:60
  18.5 4.4 %scatter_custom_fusion = bf16[512,2048]{1,0:T(8,128)(2,1)} fusion(s32[256]{0:T(256)S(1)} %bitcast.71, bf16[256,2048]{1,0:T(8,128)(2,1)} %param.7, bf16[]{:T(256)} %constant.6.clone.1), kind=kCustom, calls=%fused_computation.22 | custom fusion | bytes 2097664 | tf_op jit(solution)/shard_map/scatter | solution.py:45
  22.9 22.2 %all-to-all-done.2 = bf16[8,64,2048]{2,1,0:T(8,128)(2,1)S(1)} async-done(((bf16[8,64,2048]{2,1,0:T(8,128)(2,1)}), bf16[8,64,2048]{2,1,0:T(8,128)(2,1)S(1)}, u32[]{:S(2)}, u32[]{:S(2)}) %all-to-all-start.2) | async-done | bytes 2097184 | tf_op jit(solution)/shard_map/all_to_all | solution.py:60
  45.2 0.0 copy-start.2
  45.2 4.4 %all-to-all-start = ((bf16[8,64,2048]{2,1,0:T(8,128)(2,1)}), bf16[8,64,2048]{2,1,0:T(8,128)(2,1)}, u32[]{:S(2)}, u32[]{:S(2)}) async-start(bf16[8,64,2048]{2,1,0:T(8,128)(2,1)} %bitcast.67), calls=%async_computation | async-start | bytes 4194304 | tf_op jit(solution)/shard_map/all_to_all | solution.py:59
  49.6 0.0 copy-start.6
  49.6 0.0 all-reduce.3.cloned.1.call-start
  49.6 0.0 copy-done.2
  49.6 0.0 copy-done
  49.6 1.3 fusion.6
  51.0 0.0 copy-start.7
  51.0 25.2 %all-to-all-done = bf16[8,64,2048]{2,1,0:T(8,128)(2,1)} async-done(((bf16[8,64,2048]{2,1,0:T(8,128)(2,1)}), bf16[8,64,2048]{2,1,0:T(8,128)(2,1)}, u32[]{:S(2)}, u32[]{:S(2)}) %all-to-all-start) | async-done | bytes 2097184 | tf_op jit(solution)/shard_map/all_to_all | solution.py:59
  76.2 0.0 copy-done.6
  76.2 2.9 %convolution_convert_fusion.3 = bf16[8,64,64]{2,1,0:T(8,128)(2,1)} fusion(bf16[8,64,2048]{2,1,0:T(8,128)(2,1)} %all-to-all-done, bf16[1,2048,64]{1,2,0:T(8,128)(2,1)S(1)} %copy-done.6), kind=kOutput, calls=%fused_computation.18 | convolution fusion | flops 134250496 | bytes 2424832 | tf_op jit(solution)/shard_map/zwki,wit->zwkt/dot_general | solution.py:66
  79.2 0.0 all-reduce.3.cloned.1.call-update
  79.2 0.0 all-gather.2.cloned.1.call-start
  79.2 0.7 all-gather.2.cloned.1.call-update
  79.9 0.0 reduce-scatter.2.cloned.1.call-start
  80.0 0.0 copy-done.7
  80.0 16.8 %convolution_convert_fusion = bf16[256,8192]{1,0:T(8,128)(2,1)} fusion(bf16[256,2048]{1,0:T(8,128)(2,1)S(1)} %copy-done.7, bf16[8192,2048]{1,0:T(8,128)(2,1)} %param.9), kind=kOutput, calls=%fused_computation.4 | convolution fusion | flops 8592031744 | bytes 38797312 | tf_op jit(solution)/shard_map/dot_general | solution.py:28
  96.7 0.0 reduce-scatter.2.cloned.1.call-update
  96.8 17.5 %all-reduce.3.cloned.1.call-done = (bf16[8,64,64]{2,1,0:T(8,128)(2,1)}, bf16[8,1,64,64]{3,2,0,1:T(8,128)(2,1)}) async-done(((bf16[8,64,64]{2,1,0:T(8,128)(2,1)}, bf16[8,1,64,64]{3,2,0,1:T(8,128)(2,1)}), (bf16[8,64,64]{2,1,0:T(8,128)(2,1)}, bf16[8,1,64,64]{3,2,0,1:T(8,128)(2,1)})) %all-reduce.3.cloned.1.call-update) | async-done | bytes 131088 | tf_op jit(solution)/shard_map/psum | solution.py:76
  114.3 2.9 %multiply_convert_fusion = bf16[8,64,2048]{2,1,0:T(8,128)(2,1)} fusion(bf16[8,64,64]{2,1,0:T(8,128)(2,1)} %get-tuple-element.4, bf16[1,64,2048]{2,1,0:T(8,128)(2,1)S(1)} %copy-done), kind=kOutput, calls=%fused_computation.5 | convolution fusion | flops 136314880 | bytes 2424832 | tf_op jit(solution)/shard_map/ytqw,twl->ytql/dot_general | solution.py:83
  117.2 0.0 copy-start.5
  117.2 3.8 %all-to-all-start.1 = ((bf16[8,64,2048]{2,1,0:T(8,128)(2,1)}), bf16[8,64,2048]{2,1,0:T(8,128)(2,1)S(1)}, u32[]{:S(2)}, u32[]{:S(2)}) async-start(bf16[8,64,2048]{2,1,0:T(8,128)(2,1)} %multiply_convert_fusion), calls=%async_computation.1 | async-start | bytes 4194304 | tf_op jit(solution)/shard_map/all_to_all | solution.py:106
  121.0 0.0 copy-done.5
  121.0 2.0 convolution_convert_fusion.1
  123.0 24.6 %all-to-all-done.1 = bf16[8,64,2048]{2,1,0:T(8,128)(2,1)S(1)} async-done(((bf16[8,64,2048]{2,1,0:T(8,128)(2,1)}), bf16[8,64,2048]{2,1,0:T(8,128)(2,1)S(1)}, u32[]{:S(2)}, u32[]{:S(2)}) %all-to-all-start.1) | async-done | bytes 2097184 | tf_op jit(solution)/shard_map/all_to_all | solution.py:106
  147.6 4.5 %all-to-all-start.3 = ((bf16[8,64,2048]{2,1,0:T(8,128)(2,1)}), bf16[8,64,2048]{2,1,0:T(8,128)(2,1)}, u32[]{:S(2)}, u32[]{:S(2)}) async-start(bf16[8,64,2048]{2,1,0:T(8,128)(2,1)} %convolution_convert_fusion.1), calls=%async_computation.4 | async-start | bytes 4194304 | tf_op jit(solution)/shard_map/all_to_all | solution.py:113
  152.1 0.0 copy-start.3
  152.2 0.0 copy-start.4
  152.2 3.0 %fusion.5 = bf16[1,2048,64]{1,2,0:T(8,128)(2,1)} fusion(bf16[8,64,2048]{2,1,0:T(8,128)(2,1)} %all-to-all-done, bf16[8,1,64,64]{3,2,0,1:T(8,128)(2,1)S(1)} %copy-done.5), kind=kOutput, calls=%fused_computation.15 | convolution fusion | flops 134447104 | bytes 2424832 | tf_op jit(solution)/shard_map/sjcd,sjcr->jdr/dot_general | solution.py:102
  155.2 0.0 copy-done.3
  155.2 0.0 copy-done.4
  155.2 1.2 fusion.4
  156.4 1.4 gather_fusion
  157.7 20.9 %all-to-all-done.3 = bf16[8,64,2048]{2,1,0:T(8,128)(2,1)} async-done(((bf16[8,64,2048]{2,1,0:T(8,128)(2,1)}), bf16[8,64,2048]{2,1,0:T(8,128)(2,1)}, u32[]{:S(2)}, u32[]{:S(2)}) %all-to-all-start.3) | async-done | bytes 2097184 | tf_op jit(solution)/shard_map/all_to_all | solution.py:113
  178.6 4.2 %gather_fusion.1 = bf16[256,2048]{1,0:T(8,128)(2,1)S(1)} fusion(bf16[512,2048]{1,0:T(8,128)(2,1)} %bitcast.17, s32[1024]{0:T(1024)S(1)} %pad_clamp_fusion), kind=kCustom, calls=%fused_computation.1 | custom fusion | bytes 2098176 | tf_op jit(solution)/shard_map/gather | solution.py:124
  182.8 13.6 %all-gather.2.cloned.1.call-done = bf16[256,8192]{1,0:T(8,128)(2,1)} async-done(((bf16[256,2048]{1,0:T(8,128)(2,1)}), bf16[256,8192]{1,0:T(8,128)(2,1)}) %all-gather.2.cloned.1.call-update) | async-done | bytes 4194320 | tf_op jit(solution)/shard_map/all_gather | solution.py:24
  196.5 0.0 copy-start.1
  196.5 17.8 %fusion = bf16[256,2048]{1,0:T(8,128)(2,1)} fusion(bf16[256,8192]{1,0:T(8,128)(2,1)} %all-gather.2.cloned.1.call-done, bf16[8192,2048]{1,0:T(8,128)(2,1)} %param.9, bf16[256,2048]{1,0:T(8,128)(2,1)S(1)} %gather_fusion), kind=kOutput, calls=%fused_computation.8 | convolution fusion | flops 8591507456 | bytes 39845888 | tf_op jit(solution)/shard_map/dot_general | solution.py:23
  214.3 59.9 %reduce-scatter.2.cloned.1.call-done = bf16[256,2048]{1,0:T(8,128)(2,1)} async-done(((bf16[256,8192]{1,0:T(8,128)(2,1)}), bf16[256,2048]{1,0:T(8,128)(2,1)}) %reduce-scatter.2.cloned.1.call-update) | async-done | bytes 1048592 | tf_op jit(solution)/shard_map/reduce_scatter | solution.py:31
  274.2 2.6 add_convert_fusion
  276.8 0.0 copy-done.1
  (6 shorter events, 0.1 us)
Async XLA Ops:
  7.2 42.5 %copy-start = (bf16[1,64,2048]{2,1,0:T(8,128)(2,1)S(1)}, bf16[1,64,2048]{2,1,0:T(8,128)(2,1)}, u32[]{:S(2)}) copy-start(bf16[1,64,2048]{2,1,0:T(8,128)(2,1)} %param.11) | copy-start | bytes 786436
  13.4 31.8 %all-to-all-start.2 = ((bf16[8,64,2048]{2,1,0:T(8,128)(2,1)}), bf16[8,64,2048]{2,1,0:T(8,128)(2,1)S(1)}, u32[]{:S(2)}, u32[]{:S(2)}) async-start(bf16[8,64,2048]{2,1,0:T(8,128)(2,1)} %bitcast.68), calls=%async_computation.3 | async-start | bytes 4194304 | tf_op jit(solution)/shard_map/all_to_all | solution.py:60
  45.2 4.4 %copy-start.2 = (bf16[8,64,2048]{2,1,0:T(8,128)(2,1)}, bf16[8,64,2048]{2,1,0:T(8,128)(2,1)S(1)}, u32[]{:S(2)}) copy-start(bf16[8,64,2048]{2,1,0:T(8,128)(2,1)S(1)} %all-to-all-done.2) | copy-start | bytes 6291460
  45.2 31.0 %all-to-all-start = ((bf16[8,64,2048]{2,1,0:T(8,128)(2,1)}), bf16[8,64,2048]{2,1,0:T(8,128)(2,1)}, u32[]{:S(2)}, u32[]{:S(2)}) async-start(bf16[8,64,2048]{2,1,0:T(8,128)(2,1)} %bitcast.67), calls=%async_computation | async-start | bytes 4194304 | tf_op jit(solution)/shard_map/all_to_all | solution.py:59
  49.6 26.7 %copy-start.6 = (bf16[1,2048,64]{1,2,0:T(8,128)(2,1)S(1)}, bf16[1,2048,64]{1,2,0:T(8,128)(2,1)}, u32[]{:S(2)}) copy-start(bf16[1,2048,64]{1,2,0:T(8,128)(2,1)} %param.10) | copy-start | bytes 786436
  49.6 64.7 %all-reduce.3.cloned.1.call-start = ((), (), s32[]{:S(2)}) async-start(), calls=%async_computation.7 | async-start | bytes 524288 | tf_op jit(solution)/shard_map/psum | solution.py:76
  51.0 29.0 %copy-start.7 = (bf16[256,2048]{1,0:T(8,128)(2,1)S(1)}, bf16[256,2048]{1,0:T(8,128)(2,1)}, u32[]{:S(2)}) copy-start(bf16[256,2048]{1,0:T(8,128)(2,1)} %param.8) | copy-start | bytes 3145732
  79.2 117.3 %all-gather.2.cloned.1.call-start = ((), (), s32[]{:S(2)}) async-start(), calls=%async_computation.5 | async-start | bytes 5242880 | tf_op jit(solution)/shard_map/all_gather | solution.py:24
  79.9 194.3 %reduce-scatter.2.cloned.1.call-start = ((), (), s32[]{:S(2)}) async-start(), calls=%async_computation.6 | async-start | bytes 5242880 | tf_op jit(solution)/shard_map/reduce_scatter | solution.py:31
  117.2 3.8 %copy-start.5 = (bf16[8,1,64,64]{3,2,0,1:T(8,128)(2,1)S(1)}, bf16[8,1,64,64]{3,2,0,1:T(8,128)(2,1)}, u32[]{:S(2)}) copy-start(bf16[8,1,64,64]{3,2,0,1:T(8,128)(2,1)} %get-tuple-element.5) | copy-start | bytes 196612
  117.2 30.4 %all-to-all-start.1 = ((bf16[8,64,2048]{2,1,0:T(8,128)(2,1)}), bf16[8,64,2048]{2,1,0:T(8,128)(2,1)S(1)}, u32[]{:S(2)}, u32[]{:S(2)}) async-start(bf16[8,64,2048]{2,1,0:T(8,128)(2,1)} %multiply_convert_fusion), calls=%async_computation.1 | async-start | bytes 4194304 | tf_op jit(solution)/shard_map/all_to_all | solution.py:106
  147.6 31.0 %all-to-all-start.3 = ((bf16[8,64,2048]{2,1,0:T(8,128)(2,1)}), bf16[8,64,2048]{2,1,0:T(8,128)(2,1)}, u32[]{:S(2)}, u32[]{:S(2)}) async-start(bf16[8,64,2048]{2,1,0:T(8,128)(2,1)} %convolution_convert_fusion.1), calls=%async_computation.4 | async-start | bytes 4194304 | tf_op jit(solution)/shard_map/all_to_all | solution.py:113
  152.1 3.0 %copy-start.3 = (bf16[8,64,2048]{2,1,0:T(8,128)(2,1)S(1)}, bf16[8,64,2048]{2,1,0:T(8,128)(2,1)}, u32[]{:S(2)}) copy-start(bf16[8,64,2048]{2,1,0:T(8,128)(2,1)} %copy-done.2) | copy-start | bytes 6291460
  152.2 3.0 %copy-start.4 = (bf16[8,64,64]{2,1,0:T(8,128)(2,1)S(1)}, bf16[8,64,64]{2,1,0:T(8,128)(2,1)}, u32[]{:S(2)}) copy-start(bf16[8,64,64]{2,1,0:T(8,128)(2,1)} %get-tuple-element.4) | copy-start | bytes 196612
  196.5 80.3 %copy-start.1 = (bf16[1,64,2048]{2,1,0:T(8,128)(2,1)S(1)}, bf16[1,64,2048]{2,1,0:T(8,128)(2,1)}, u32[]{:S(2)}) copy-start(bf16[1,64,2048]{2,1,0:T(8,128)(2,1)} %param.11) | copy-start | bytes 786436
Sparse Core Ops, SparseCore 0:
  79.3 34.9 all-reduce.2
  115.9 80.5 all-gather.1
  198.9 75.2 reduce-scatter.1
where the time goes:
time: 284 us; the launch traced here: 283 us
  waiting for transfers between devices  185 us (65%)
  matrix products  48 us (17%)
  starting transfers between devices  18 us (6%)
  local copies, waits for them, and re-layouts  14.6 us (5%)
  between operations  13.9 us (5%)
  other arithmetic  4.13 us (1%)
    reduce_scatter x1, waiting for transfers between devices, body(): lax.psum_scatter(back_part.astype(jnp.bfloat16), 'tensor', scatter_dimens...  59.9 us
    all_to_all x1, waiting for transfers between devices, body(): lax.all_to_all(outgoing_input, 'dp', split_axis=0, concat_axis=0, tiled=T...  25.2 us
    all_to_all x1, waiting for transfers between devices, body(): lax.all_to_all(contribution.reshape(adapter_groups, per_worker * slot_cap...  24.6 us
    all_to_all x1, waiting for transfers between devices, body(): lax.all_to_all(outgoing_output_gradient, 'dp', split_axis=0, concat_axis=...  22.2 us
    all_to_all x1, waiting for transfers between devices, body(): lax.all_to_all(backward_result.reshape(adapter_groups, per_worker * slot_...  20.9 us
    dot_general x1, matrix products, body(): jnp.dot(lax.all_gather(inputs, 'tensor', axis=1, tiled=True), frozen_weig...  17.8 us
    psum x1, waiting for transfers between devices, body(): lax.psum(reduced_portion.astype(jnp.bfloat16), 'tensor').astype(jnp.float32)  17.5 us
    dot_general x1, matrix products, body(): lax.dot_general(output_gradient, frozen_weight, (((1,), (1,)), ((), ())),...  16.8 us
  transfers between devices with their start and end apart: 7, of which 7 were waited for; matrix products, arithmetic and copies ran while one was open for 19% of the time, Pallas kernels for 0%

commit v1 on v0

v1 whole, which is shorter than its diff:
```python
import jax
import jax.numpy as jnp
from jax import lax
from jax.sharding import PartitionSpec as P

adapter_scale = 2.0
f32, bf16 = jnp.float32, jnp.bfloat16


def dot(a, b, ca, cb):
    return lax.dot_general(a, b, (((ca,), (cb,)), ((), ())), preferred_element_type=f32)


def exchange(x, axis, offset):
    size = lax.axis_size(axis)
    return lax.ppermute(x, axis, [(i, i ^ offset) for i in range(size)])


def body(X, dY, W, A, B, adapter_rows, adapter_slot):
    rows, width = X.shape
    rank = A.shape[2]
    n, D = lax.axis_size("tensor"), lax.axis_size("dp")
    z, me = lax.axis_index("tensor"), lax.axis_index("dp")
    half = D // 2

    own = jnp.concatenate([A[0].T, B[0]], axis=0)
    evens = [own] + [exchange(own, "dp", 2 * j) for j in range(1, half)]
    even = jnp.concatenate([e[:rank] for e in evens] + [e[rank:] for e in evens], axis=0)
    odd = exchange(even, "dp", 1)
    wide = half * rank

    right = [(i, i + 1) for i in range(n - 1)]
    left = [(i + 1, i) for i in range(n - 1)]
    from_left, from_right = [X], [X]
    for s in range(1, n):
        from_left.append(lax.ppermute(from_left[-1], "tensor", right))
        from_right.append(lax.ppermute(from_right[-1], "tensor", left))

    back = dot(dY, W, 1, 1).astype(bf16)
    base_back = lax.psum_scatter(back, "tensor", scatter_dimension=1, tiled=True)

    names = jnp.arange(adapter_slot.shape[0], dtype=jnp.int32)
    slot = jnp.sum(jnp.where(adapter_rows == names[None, :], adapter_slot[None, :], 0), axis=1, keepdims=True)
    offset = slot ^ me
    place = (offset >> 1) + (offset & 1) * half
    group = jnp.arange(D * rank, dtype=jnp.int32) // rank
    chosen = place == group[None, :]
    spread = (jnp.arange(D * rank)[None, :] % rank == jnp.arange(rank)[:, None]).astype(bf16)

    def pick(e, o):
        both = jnp.concatenate([e, o], axis=1)
        return dot(jnp.where(chosen, both, 0).astype(bf16), spread, 1, 1).astype(bf16)

    low_part = pick(dot(X, even[:wide], 1, 1), dot(X, odd[:wide], 1, 1))
    grad_part = pick(dot(dY, even[wide:], 1, 1), dot(dY, odd[wide:], 1, 1))
    part = jnp.concatenate([low_part, grad_part], axis=1)
    total = part.astype(f32)
    for k in range(1, n):
        total = total + exchange(part, "tensor", k).astype(f32)
    low = total[:, :rank].astype(bf16)
    low_grad = (adapter_scale * total[:, rank:]).astype(bf16)
    low_all = jnp.where(chosen, dot(low, spread, 1, 0), 0).astype(bf16)
    grad_all = jnp.where(chosen, dot(low_grad, spread, 1, 0), 0).astype(bf16)

    def grads(part):
        shrink = dot(grad_all[:, part], X, 0, 0)
        expand = adapter_scale * dot(low_all[:, part], dY, 0, 0)
        return jnp.concatenate([shrink, expand], axis=0).astype(bf16)

    there = exchange(grads(slice(wide, 2 * wide)), "dp", 1)
    here = grads(slice(0, wide)).astype(f32) + there.astype(f32)
    blocks = [
        jnp.concatenate([here[j * rank : (j + 1) * rank], here[wide + j * rank : wide + (j + 1) * rank]], axis=0)
        for j in range(half)
    ]
    mine = blocks[0]
    for j in range(1, half):
        mine = mine + exchange(blocks[j].astype(bf16), "dp", 2 * j).astype(f32)
    mine = mine.astype(bf16)

    lora_term = (adapter_scale * (dot(low_all[:, :wide], even[wide:], 1, 0) + dot(low_all[:, wide:], odd[wide:], 1, 0))).astype(bf16)
    lora_back = (dot(grad_all[:, :wide], even[:wide], 1, 0) + dot(grad_all[:, wide:], odd[:wide], 1, 0)).astype(bf16)

    base = dot(X, lax.dynamic_slice(W, (z * width, 0), (width, W.shape[1])), 1, 0)
    for s in range(1, n):
        block = jnp.where(z >= s, from_left[s], from_right[n - s])
        source = lax.rem(z - s + n, n)
        base = base + dot(block, lax.dynamic_slice(W, (source * width, 0), (width, W.shape[1])), 1, 0)

    projected = (base + lora_term.astype(f32)).astype(bf16)
    activation = (base_back.astype(f32) + lora_back.astype(f32)).astype(bf16)
    return projected, activation, mine[:rank].T[None], mine[rank:][None]


def solution(mesh):
    return jax.shard_map(
        body,
        mesh=mesh,
        in_specs=(
            P("dp", "tensor"),
            P("dp", "tensor"),
            P(None, "tensor"),
            P("dp", "tensor", None),
            P("dp", None, "tensor"),
            P("dp", None),
            P(),
        ),
        out_specs=(
            P("dp", "tensor"),
            P("dp", "tensor"),
            P("dp", "tensor", None),
            P("dp", None, "tensor"),
        ),
        check_vma=False,
    )
```

time: 284 us -> 256 us (0.901)
  waiting for transfers between devices: 185 us -> 110 us
  starting transfers between devices: 18 us -> 48.1 us
  matrix products: 48 us -> 62.1 us
    ppermute x0 -> x17, waiting for transfers between devices: none -> 110 us  [the longest x11 70.4 us: exchange(): return lax.ppermute(x, axis, [(i, i ^ offset) for i in range(size)])]
    all_to_all x4 -> x0, waiting for transfers between devices: 92.9 us -> none  [the longest x1 25.2 us: body(): lax.all_to_all(outgoing_input, 'dp', split_axis=0, concat_axis=0, tiled=T...]
    reduce_scatter x1, waiting for transfers between devices: 59.9 us -> 0.01 us  [body(): lax.psum_scatter(back, 'tensor', scatter_dimension=1, tiled=True)]
    ppermute x0 -> x17, starting transfers between devices: none -> 48.1 us  [the longest x3 30.7 us: body(): from_left.append(lax.ppermute(from_left[-1], 'tensor', right))]
    all_to_all x4 -> x0, starting transfers between devices: 17.9 us -> none  [the longest x1 5.17 us: body(): lax.all_to_all(outgoing_output_gradient, 'dp', split_axis=0, concat_axis=...]
    psum x1 -> x0, waiting for transfers between devices: 17.5 us -> none  [body(): lax.psum(reduced_portion.astype(jnp.bfloat16), 'tensor').astype(jnp.float32)]
    dot_general x8 -> x21, matrix products: 48 us -> 62.1 us  [dot(): lax.dot_general(a, b, (((ca,), (cb,)), ((), ())), preferred_element_type=...]
    all_gather x1 -> x0, waiting for transfers between devices: 13.6 us -> none  [body(): lax.all_gather(inputs, 'tensor', axis=1, tiled=True)]
  transfers between devices with their start and end apart: 7 -> 18, of which waited for: 7 -> 8; matrix products, arithmetic and copies ran while one was open for 19% -> 30% of each run, Pallas kernels for 0% -> 0%
where the time goes in v1:
time: 256 us
  waiting for transfers between devices  110 us (43%)
  matrix products  62.1 us (24%)
  starting transfers between devices  48.1 us (19%)
  between operations  14.5 us (6%)
  local copies, waits for them, and re-layouts  13.8 us (5%)
  other arithmetic  6.64 us (3%)
    ppermute x11, waiting for transfers between devices, exchange(): return lax.ppermute(x, axis, [(i, i ^ offset) for i in range(size)])  70.4 us
    dot_general x21, matrix products, dot(): lax.dot_general(a, b, (((ca,), (cb,)), ((), ())), preferred_element_type=...  62.1 us
    ppermute x3, waiting for transfers between devices, body(): from_left.append(lax.ppermute(from_left[-1], 'tensor', right))  34.8 us
    ppermute x3, starting transfers between devices, body(): from_left.append(lax.ppermute(from_left[-1], 'tensor', right))  30.7 us
    ppermute x11, starting transfers between devices, exchange(): return lax.ppermute(x, axis, [(i, i ^ offset) for i in range(size)])  13.4 us
    unnamed x47, local copies, waits for them, and re-layouts  9.21 us
  transfers between devices with their start and end apart: 18, of which 8 were waited for; matrix products, arithmetic and copies ran while one was open for 30% of the time, Pallas kernels for 0%

profile of v1, /device:TPU:0, one launch (start us, length us, event | category | flops | bytes accessed | tf_op | source)
XLA Modules:
  0.0 255.6 jit_solution(11182663303074896152)
XLA Ops:
  7.2 1.1 pad_maximum_fusion.3
  8.4 3.0 %collective-permute-start.6 = (bf16[128,2048]{1,0:T(8,128)(2,1)S(1)}, bf16[128,2048]{1,0:T(8,128)(2,1)S(1)}, u32[]{:S(2)}, u32[]{:S(2)}) collective-permute-start(bf16[128,2048]{1,0:T(8,128)(2,1)S(1)} %pad_maximum_fusion.3), channel_id=1, source_target_pairs={{0,8},{4,12},{8,0},{12,4},{16,24},{20,28},{24,16},{28,20},{1,9},{5... | collective-permute-start | bytes 1572872 | tf_op jit(solution)/shard_map/ppermute | solution.py:16
  11.4 1.5 collective-permute-start.7
  12.9 4.0 %collective-permute-start = (bf16[256,2048]{1,0:T(8,128)(2,1)}, bf16[256,2048]{1,0:T(8,128)(2,1)S(1)}, u32[]{:S(2)}, u32[]{:S(2)}) collective-permute-start(bf16[256,2048]{1,0:T(8,128)(2,1)} %param.7), channel_id=1, source_target_pairs={{0,1},{1,2},{2,3},{4,5},{5,6},{6,7},{8,9},{9,10},{10,11},{12,13},{... | collective-permute-start | bytes 3145736 | tf_op jit(solution)/shard_map/ppermute | solution.py:36
  16.9 1.3 collective-permute-start.1
  18.2 1.7 constant_dynamic-update-slice_fusion.7
  19.9 4.2 %collective-permute-done.6 = bf16[128,2048]{1,0:T(8,128)(2,1)S(1)} collective-permute-done((bf16[128,2048]{1,0:T(8,128)(2,1)S(1)}, bf16[128,2048]{1,0:T(8,128)(2,1)S(1)}, u32[]{:S(2)}, u32[]{:S(2)}) %collective-permute-start.6) | collective-permute-done | bytes 524320 | tf_op jit(solution)/shard_map/ppermute | solution.py:16
  24.1 0.9 fusion.100
  25.1 10.9 %collective-permute-done.7 = bf16[128,2048]{1,0:T(8,128)(2,1)S(1)} collective-permute-done((bf16[128,2048]{1,0:T(8,128)(2,1)S(1)}, bf16[128,2048]{1,0:T(8,128)(2,1)S(1)}, u32[]{:S(2)}, u32[]{:S(2)}) %collective-permute-start.7) | collective-permute-done | bytes 524320 | tf_op jit(solution)/shard_map/ppermute | solution.py:16
  36.0 0.9 fusion.101
  36.9 0.9 fusion.102
  37.9 0.7 constant_dynamic-update-slice_fusion.3
  38.6 0.7 constant_dynamic-update-slice_fusion.2
  39.3 0.7 constant_dynamic-update-slice_fusion.1
  40.0 0.7 constant_dynamic-update-slice_fusion
  40.8 16.7 %convolution_convert_fusion = bf16[256,8192]{1,0:T(8,128)(2,1)} fusion(bf16[256,2048]{1,0:T(8,128)(2,1)S(1)} %copy-done, bf16[8192,2048]{1,0:T(8,128)(2,1)} %param.9), kind=kOutput, calls=%fused_computation | convolution fusion | flops 8592031744 | bytes 38797312 | tf_op jit(solution)/shard_map/dot_general | solution.py:11
  57.5 0.6 copy-done.18
  58.3 3.7 %collective-permute-start.4 = (bf16[256,2048]{1,0:T(8,128)(2,1)S(1)}, bf16[256,2048]{1,0:T(8,128)(2,1)S(1)}, u32[]{:S(2)}, u32[]{:S(2)}) collective-permute-start(bf16[256,2048]{1,0:T(8,128)(2,1)S(1)} %collective-permute-done), channel_id=1, source_target_pairs={{0,1},{1,2},{2,3},{4,5},{5,6},{6,7},{8,9},{9,10},{10,11},{12,13},{... | collective-permute-start | bytes 3145736 | tf_op jit(solution)/shard_map/ppermute | solution.py:36
  62.0 1.3 collective-permute-start.2
  63.3 6.7 %fusion.8 = f32[256,2048]{0,1:T(8,128)S(1)} fusion(bf16[256,2048]{1,0:T(8,128)(2,1)S(1)} %copy-done.1, bf16[8192,2048]{1,0:T(8,128)(2,1)} %param.9, s32[]{:T(128)S(6)} %select_n.76), kind=kOutput, calls=%fused_computation.10 | convolution fusion | flops 2147483648 | bytes 11534340 | tf_op jit(solution)/shard_map/dot_general | solution.py:11
  70.1 0.5 convolution_bitcast_fusion.3
  70.6 0.4 copy-done.7
  71.2 0.5 convolution_bitcast_fusion.1
  71.7 34.8 %collective-permute-done.4 = bf16[256,2048]{1,0:T(8,128)(2,1)S(1)} collective-permute-done((bf16[256,2048]{1,0:T(8,128)(2,1)S(1)}, bf16[256,2048]{1,0:T(8,128)(2,1)S(1)}, u32[]{:S(2)}, u32[]{:S(2)}) %collective-permute-start.4) | collective-permute-done | bytes 1048608 | tf_op jit(solution)/shard_map/ppermute | solution.py:36
  106.5 23.0 %collective-permute-start.5 = (bf16[256,2048]{1,0:T(8,128)(2,1)S(1)}, bf16[256,2048]{1,0:T(8,128)(2,1)S(1)}, u32[]{:S(2)}, u32[]{:S(2)}) collective-permute-start(bf16[256,2048]{1,0:T(8,128)(2,1)S(1)} %collective-permute-done.4), channel_id=1, source_target_pairs={{0,1},{1,2},{2,3},{4,5},{5,6},{6,7},{8,9},{9,10},{10,11},{12,13},{... | collective-permute-start | bytes 3145736 | tf_op jit(solution)/shard_map/ppermute | solution.py:36
  129.5 5.1 %collective-permute-done.2 = bf16[256,2048]{1,0:T(8,128)(2,1)S(1)} collective-permute-done((bf16[256,2048]{1,0:T(8,128)(2,1)}, bf16[256,2048]{1,0:T(8,128)(2,1)S(1)}, u32[]{:S(2)}, u32[]{:S(2)}) %collective-permute-start.2) | collective-permute-done | bytes 1048608 | tf_op jit(solution)/shard_map/ppermute | solution.py:37
  134.5 1.5 collective-permute-start.3
  136.0 1.7 convolution_bitcast_fusion.2
  137.7 0.3 convolution_convert_fusion.4
  138.0 1.7 convolution_bitcast_fusion
  139.7 0.3 convolution_convert_fusion.3
  140.0 2.7 %collective-permute-start.10 = (bf16[256,128]{0,1:T(8,128)(2,1)S(1)}, bf16[256,128]{0,1:T(8,128)(2,1)S(1)}, u32[]{:S(2)}, u32[]{:S(2)}) collective-permute-start(bf16[256,128]{0,1:T(8,128)(2,1)S(1)} %pad_maximum_fusion.11), channel_id=1, source_target_pairs={{0,1},{1,0},{2,3},{3,2},{4,5},{5,4},{6,7},{7,6},{8,9},{9,8},{10,11... | collective-permute-start | bytes 196616 | tf_op jit(solution)/shard_map/ppermute | solution.py:16
  142.7 0.7 collective-permute-start.11
  143.4 1.8 collective-permute-start.12
  145.1 6.9 %fusion.2 = f32[256,2048]{0,1:T(8,128)S(1)} fusion(bf16[8192,2048]{1,0:T(8,128)(2,1)} %param.9, s32[]{:T(128)S(6)} %select_n.82, bf16[256,2048]{1,0:T(8,128)(2,1)S(1)} %collective-permute-done.4, bf16[256,2048]{1,0:T(8,128)(2,1)S(1)} %collective-permute-done.2, pred[]{:T(512)S(6)} %ge.10), kind=kOutput, calls=%fused_computation.3 | convolution fusion | flops 2148007936 | bytes 12582917 | tf_op jit(solution)/shard_map/dot_general | solution.py:11
  152.1 29.2 %collective-permute-done.10 = bf16[256,128]{0,1:T(8,128)(2,1)S(1)} collective-permute-done((bf16[256,128]{0,1:T(8,128)(2,1)S(1)}, bf16[256,128]{0,1:T(8,128)(2,1)S(1)}, u32[]{:S(2)}, u32[]{:S(2)}) %collective-permute-start.10) | collective-permute-done | bytes 65568 | tf_op jit(solution)/shard_map/ppermute | solution.py:16
  181.3 3.5 %collective-permute-done.12 = bf16[256,128]{0,1:T(8,128)(2,1)S(1)} collective-permute-done((bf16[256,128]{0,1:T(8,128)(2,1)S(1)}, bf16[256,128]{0,1:T(8,128)(2,1)S(1)}, u32[]{:S(2)}, u32[]{:S(2)}) %collective-permute-start.12) | collective-permute-done | bytes 65568 | tf_op jit(solution)/shard_map/ppermute | solution.py:16
  184.8 0.3 fusion.36
  185.1 0.3 fusion.35
  185.4 0.6 convolution_convert_fusion.1
  185.9 0.6 fusion.31
  186.5 1.5 pad_maximum_fusion
  188.0 3.0 %fusion.49 = f32[256,2048]{1,0:T(8,128)} fusion(bf16[512,2048]{1,0:T(8,128)(2,1)} %collective-permute-done.9, bf16[256,512]{1,0:T(8,128)(2,1)S(1)} %fusion.36), kind=kOutput, calls=%fused_computation.59 | convolution fusion | flops 268435456 | bytes 3276800 | tf_op jit(solution)/shard_map/dot_general | solution.py:11
  191.1 1.8 fusion.46
  192.8 0.6 convolution_convert_fusion.2
  193.4 0.6 fusion.30
  194.0 0.6 fusion.25
  194.6 7.3 %fusion = f32[256,2048]{0,1:T(8,128)S(1)} fusion(bf16[8192,2048]{1,0:T(8,128)(2,1)} %param.9, s32[]{:T(128)S(6)} %select_n.85, bf16[256,2048]{1,0:T(8,128)(2,1)S(1)} %collective-permute-done.5, bf16[256,2048]{1,0:T(8,128)(2,1)} %collective-permute-done.1, pred[]{:T(512)S(6)} %ge.11), kind=kOutput, calls=%fused_computation.1 | convolution fusion | flops 2148007936 | bytes 12582917 | tf_op jit(solution)/shard_map/dot_general | solution.py:11
  201.9 8.2 %fusion.32 = bf16[256,2048]{0,1:T(8,128)(2,1)} fusion(f32[256,2048]{0,1:T(8,128)S(1)} %fusion.25, f32[256,2048]{0,1:T(8,128)S(1)} %fusion, f32[256,2048]{0,1:T(8,128)S(1)} %fusion.2, f32[256,2048]{0,1:T(8,128)S(1)} %fusion.8, bf16[8192,2048]{1,0:T(8,128)(2,1)} %param.9, s32[]{:T(128)S(6)} %select_n.79, bf16[256,2048]{1,0:T(8,128)(2,1)S(1)} %copy-done.4, ...), kind=kOutput, calls=%fused_computation.30 | convolution fusion | flops 2150629376 | bytes 19922948 | tf_op jit(solution)/shard_map/dot_general | solution.py:11
  210.1 2.3 copy.32
  212.4 2.4 fusion.97
  214.8 0.8 fusion.99
  215.6 0.3 pad_maximum_fusion.4
  215.9 1.3 collective-permute-start.14
  217.2 0.3 pad_maximum_fusion.5
  217.5 1.8 collective-permute-start.15
  219.3 0.3 pad_maximum_fusion.6
  219.5 0.6 collective-permute-start.16
  220.3 10.4 %collective-permute-done.14 = bf16[128,2048]{0,1:T(8,128)(2,1)S(1)} collective-permute-done((bf16[128,2048]{0,1:T(8,128)(2,1)S(1)}, bf16[128,2048]{0,1:T(8,128)(2,1)S(1)}, u32[]{:S(2)}, u32[]{:S(2)}) %collective-permute-start.14) | collective-permute-done | bytes 524320 | tf_op jit(solution)/shard_map/ppermute | solution.py:16
  230.7 12.2 %collective-permute-done.15 = bf16[128,2048]{0,1:T(8,128)(2,1)S(1)} collective-permute-done((bf16[128,2048]{0,1:T(8,128)(2,1)S(1)}, bf16[128,2048]{0,1:T(8,128)(2,1)S(1)}, u32[]{:S(2)}, u32[]{:S(2)}) %collective-permute-start.15) | collective-permute-done | bytes 524320 | tf_op jit(solution)/shard_map/ppermute | solution.py:16
  242.8 0.5 fusion.39
  243.6 0.9 copy.33
  244.5 0.9 copy.34
  245.5 3.3 %fusion.29 = bf16[256,2048]{1,0:T(8,128)(2,1)} fusion(f32[256,2048]{1,0:T(8,128)} %fusion.49, bf16[256,2048]{1,0:T(8,128)(2,1)} %reduce-scatter.2.cloned.1.call-done, bf16[64,2048]{1,0:T(8,128)(2,1)S(1)} %copy-done.17, bf16[64,2048]{1,0:T(8,128)(2,1)S(1)} %copy-done.15, bf16[64,2048]{1,0:T(8,128)(2,1)S(1)} %copy-done.13, bf16[64,2048]{1,0:T(8,128)(2,1)S(1)} %bitcast.39, ...), kind=kOutput, calls=%fused_computation.25 | convolution fusion | flops 275775488 | bytes 5373952 | tf_op jit(solution)/shard_map/dot_general | solution.py:11
  (60 shorter events, 0.8 us)
Async XLA Ops:
  7.2 33.6 %copy-start = (bf16[256,2048]{1,0:T(8,128)(2,1)S(1)}, bf16[256,2048]{1,0:T(8,128)(2,1)}, u32[]{:S(2)}) copy-start(bf16[256,2048]{1,0:T(8,128)(2,1)} %param.8) | copy-start | bytes 3145732
  7.2 238.3 %reduce-scatter.2.cloned.1.call-start = ((), (), s32[]{:S(2)}) async-start(), calls=%async_computation.1 | async-start | bytes 5242880 | tf_op jit(solution)/shard_map/reduce_scatter | solution.py:40
  8.4 15.8 %collective-permute-start.6 = (bf16[128,2048]{1,0:T(8,128)(2,1)S(1)}, bf16[128,2048]{1,0:T(8,128)(2,1)S(1)}, u32[]{:S(2)}, u32[]{:S(2)}) collective-permute-start(bf16[128,2048]{1,0:T(8,128)(2,1)S(1)} %pad_maximum_fusion.3), channel_id=1, source_target_pairs={{0,8},{4,12},{8,0},{12,4},{16,24},{20,28},{24,16},{28,20},{1,9},{5... | collective-permute-start | bytes 1572872 | tf_op jit(solution)/shard_map/ppermute | solution.py:16
  11.4 24.6 %collective-permute-start.7 = (bf16[128,2048]{1,0:T(8,128)(2,1)S(1)}, bf16[128,2048]{1,0:T(8,128)(2,1)S(1)}, u32[]{:S(2)}, u32[]{:S(2)}) collective-permute-start(bf16[128,2048]{1,0:T(8,128)(2,1)S(1)} %pad_maximum_fusion.3), channel_id=1, source_target_pairs={{0,16},{4,20},{8,24},{12,28},{16,0},{20,4},{24,8},{28,12},{1,17},{... | collective-permute-start | bytes 1572872 | tf_op jit(solution)/shard_map/ppermute | solution.py:16
  12.9 24.0 %collective-permute-start.8 = (bf16[128,2048]{1,0:T(8,128)(2,1)S(1)}, bf16[128,2048]{1,0:T(8,128)(2,1)S(1)}, u32[]{:S(2)}, u32[]{:S(2)}) collective-permute-start(bf16[128,2048]{1,0:T(8,128)(2,1)S(1)} %pad_maximum_fusion.3), channel_id=1, source_target_pairs={{0,24},{4,28},{8,16},{12,20},{16,8},{20,12},{24,0},{28,4},{1,25},{... | collective-permute-start | bytes 1572872 | tf_op jit(solution)/shard_map/ppermute | solution.py:16
  12.9 45.3 %collective-permute-start = (bf16[256,2048]{1,0:T(8,128)(2,1)}, bf16[256,2048]{1,0:T(8,128)(2,1)S(1)}, u32[]{:S(2)}, u32[]{:S(2)}) collective-permute-start(bf16[256,2048]{1,0:T(8,128)(2,1)} %param.7), channel_id=1, source_target_pairs={{0,1},{1,2},{2,3},{4,5},{5,6},{6,7},{8,9},{9,10},{10,11},{12,13},{... | collective-permute-start | bytes 3145736 | tf_op jit(solution)/shard_map/ppermute | solution.py:36
  16.9 45.1 %collective-permute-start.1 = (bf16[256,2048]{1,0:T(8,128)(2,1)}, bf16[256,2048]{1,0:T(8,128)(2,1)}, u32[]{:S(2)}, u32[]{:S(2)}) collective-permute-start(bf16[256,2048]{1,0:T(8,128)(2,1)} %param.7), channel_id=1, source_target_pairs={{1,0},{2,1},{3,2},{5,4},{6,5},{7,6},{9,8},{10,9},{11,10},{13,12},{... | collective-permute-start | bytes 3145736 | tf_op jit(solution)/shard_map/ppermute | solution.py:37
  19.9 18.0 %copy-start.2 = (bf16[1,64,2048]{2,1,0:T(8,128)(2,1)S(1)}, bf16[1,64,2048]{2,1,0:T(8,128)(2,1)}, u32[]{:S(2)}) copy-start(bf16[1,64,2048]{2,1,0:T(8,128)(2,1)} %param.11) | copy-start | bytes 786436
  40.8 95.2 %collective-permute-start.9 = (bf16[512,2048]{1,0:T(8,128)(2,1)}, bf16[512,2048]{1,0:T(8,128)(2,1)}, u32[]{:S(2)}, u32[]{:S(2)}) collective-permute-start(bf16[512,2048]{1,0:T(8,128)(2,1)} %constant_dynamic-update-slice_fusion), channel_id=1, source_target_pairs={{0,4},{4,0},{8,12},{12,8},{16,20},{20,16},{24,28},{28,24},{1,5},{5... | collective-permute-start | bytes 6291464 | tf_op jit(solution)/shard_map/ppermute | solution.py:16
  57.5 0.7 copy-start.18
  57.5 0.7 copy-start.19
  57.5 5.8 %copy-start.1 = (bf16[256,2048]{1,0:T(8,128)(2,1)S(1)}, bf16[256,2048]{1,0:T(8,128)(2,1)}, u32[]{:S(2)}) copy-start(bf16[256,2048]{1,0:T(8,128)(2,1)} %param.7) | copy-start | bytes 3145732
  58.2 11.8 %copy-start.5 = (bf16[1,2048,64]{1,2,0:T(8,128)(2,1)S(1)}, bf16[1,2048,64]{1,2,0:T(8,128)(2,1)}, u32[]{:S(2)}) copy-start(bf16[1,2048,64]{1,2,0:T(8,128)(2,1)} %param.10) | copy-start | bytes 786436
  58.2 11.8 %copy-start.12 = (bf16[64,2048]{1,0:T(8,128)(2,1)S(1)}, bf16[64,2048]{1,0:T(8,128)(2,1)}, u32[]{:S(2)}) copy-start(bf16[64,2048]{1,0:T(8,128)(2,1)} %get-tuple-element.24) | copy-start | bytes 786436
  58.2 11.8 %copy-start.14 = (bf16[64,2048]{1,0:T(8,128)(2,1)S(1)}, bf16[64,2048]{1,0:T(8,128)(2,1)}, u32[]{:S(2)}) copy-start(bf16[64,2048]{1,0:T(8,128)(2,1)} %get-tuple-element.27) | copy-start | bytes 786436
  58.3 11.8 %copy-start.16 = (bf16[64,2048]{1,0:T(8,128)(2,1)S(1)}, bf16[64,2048]{1,0:T(8,128)(2,1)}, u32[]{:S(2)}) copy-start(bf16[64,2048]{1,0:T(8,128)(2,1)} %get-tuple-element.30) | copy-start | bytes 786436
  58.3 11.7 %copy-start.3 = (bf16[256,2048]{1,0:T(8,128)(2,1)}, bf16[256,2048]{1,0:T(8,128)(2,1)S(1)}, u32[]{:S(2)}) copy-start(bf16[256,2048]{1,0:T(8,128)(2,1)S(1)} %collective-permute-done) | copy-start | bytes 3145732
  58.3 48.2 %collective-permute-start.4 = (bf16[256,2048]{1,0:T(8,128)(2,1)S(1)}, bf16[256,2048]{1,0:T(8,128)(2,1)S(1)}, u32[]{:S(2)}, u32[]{:S(2)}) collective-permute-start(bf16[256,2048]{1,0:T(8,128)(2,1)S(1)} %collective-permute-done), channel_id=1, source_target_pairs={{0,1},{1,2},{2,3},{4,5},{5,6},{6,7},{8,9},{9,10},{10,11},{12,13},{... | collective-permute-start | bytes 3145736 | tf_op jit(solution)/shard_map/ppermute | solution.py:36
  62.0 72.5 %collective-permute-start.2 = (bf16[256,2048]{1,0:T(8,128)(2,1)}, bf16[256,2048]{1,0:T(8,128)(2,1)S(1)}, u32[]{:S(2)}, u32[]{:S(2)}) collective-permute-start(bf16[256,2048]{1,0:T(8,128)(2,1)} %collective-permute-done.1), channel_id=1, source_target_pairs={{1,0},{2,1},{3,2},{5,4},{6,5},{7,6},{9,8},{10,9},{11,10},{13,12},{... | collective-permute-start | bytes 3145736 | tf_op jit(solution)/shard_map/ppermute | solution.py:37
  70.1 1.0 copy-start.7
  70.1 1.0 copy-start.8
  70.1 1.1 copy-start.9
  106.5 88.1 %collective-permute-start.5 = (bf16[256,2048]{1,0:T(8,128)(2,1)S(1)}, bf16[256,2048]{1,0:T(8,128)(2,1)S(1)}, u32[]{:S(2)}, u32[]{:S(2)}) collective-permute-start(bf16[256,2048]{1,0:T(8,128)(2,1)S(1)} %collective-permute-done.4), channel_id=1, source_target_pairs={{0,1},{1,2},{2,3},{4,5},{5,6},{6,7},{8,9},{9,10},{10,11},{12,13},{... | collective-permute-start | bytes 3145736 | tf_op jit(solution)/shard_map/ppermute | solution.py:36
  134.5 67.4 %collective-permute-start.3 = (bf16[256,2048]{1,0:T(8,128)(2,1)S(1)}, bf16[256,2048]{1,0:T(8,128)(2,1)S(1)}, u32[]{:S(2)}, u32[]{:S(2)}) collective-permute-start(bf16[256,2048]{1,0:T(8,128)(2,1)S(1)} %collective-permute-done.2), channel_id=1, source_target_pairs={{1,0},{2,1},{3,2},{5,4},{6,5},{7,6},{9,8},{10,9},{11,10},{13,12},{... | collective-permute-start | bytes 3145736 | tf_op jit(solution)/shard_map/ppermute | solution.py:37
  140.0 41.3 %collective-permute-start.10 = (bf16[256,128]{0,1:T(8,128)(2,1)S(1)}, bf16[256,128]{0,1:T(8,128)(2,1)S(1)}, u32[]{:S(2)}, u32[]{:S(2)}) collective-permute-start(bf16[256,128]{0,1:T(8,128)(2,1)S(1)} %pad_maximum_fusion.11), channel_id=1, source_target_pairs={{0,1},{1,0},{2,3},{3,2},{4,5},{5,4},{6,7},{7,6},{8,9},{9,8},{10,11... | collective-permute-start | bytes 196616 | tf_op jit(solution)/shard_map/ppermute | solution.py:16
  142.7 38.6 %collective-permute-start.11 = (bf16[256,128]{0,1:T(8,128)(2,1)S(1)}, bf16[256,128]{0,1:T(8,128)(2,1)S(1)}, u32[]{:S(2)}, u32[]{:S(2)}) collective-permute-start(bf16[256,128]{0,1:T(8,128)(2,1)S(1)} %pad_maximum_fusion.11), channel_id=1, source_target_pairs={{0,2},{1,3},{2,0},{3,1},{4,6},{5,7},{6,4},{7,5},{8,10},{9,11},{10,... | collective-permute-start | bytes 196616 | tf_op jit(solution)/shard_map/ppermute | solution.py:16
  143.4 41.4 %collective-permute-start.12 = (bf16[256,128]{0,1:T(8,128)(2,1)S(1)}, bf16[256,128]{0,1:T(8,128)(2,1)S(1)}, u32[]{:S(2)}, u32[]{:S(2)}) collective-permute-start(bf16[256,128]{0,1:T(8,128)(2,1)S(1)} %pad_maximum_fusion.11), channel_id=1, source_target_pairs={{0,3},{1,2},{2,1},{3,0},{4,7},{5,6},{6,5},{7,4},{8,11},{9,10},{10,... | collective-permute-start | bytes 196616 | tf_op jit(solution)/shard_map/ppermute | solution.py:16
  185.1 7.7 %copy-start.10 = (bf16[256,512]{1,0:T(8,128)(2,1)}, bf16[256,512]{1,0:T(8,128)(2,1)S(1)}, u32[]{:S(2)}) copy-start(bf16[256,512]{1,0:T(8,128)(2,1)S(1)} %fusion.36) | copy-start | bytes 786436
  188.0 24.4 %collective-permute-start.13 = (bf16[512,2048]{0,1:T(8,128)(2,1)}, bf16[512,2048]{0,1:T(8,128)(2,1)}, u32[]{:S(2)}, u32[]{:S(2)}) collective-permute-start(bf16[512,2048]{0,1:T(8,128)(2,1)} %pad_maximum_fusion), channel_id=1, source_target_pairs={{0,4},{4,0},{8,12},{12,8},{16,20},{20,16},{24,28},{28,24},{1,5},{5... | collective-permute-start | bytes 6291464 | tf_op jit(solution)/shard_map/ppermute | solution.py:16
  194.5 7.4 %copy-start.4 = (bf16[256,2048]{1,0:T(8,128)(2,1)S(1)}, bf16[256,2048]{1,0:T(8,128)(2,1)}, u32[]{:S(2)}) copy-start(bf16[256,2048]{1,0:T(8,128)(2,1)} %copy-done.3) | copy-start | bytes 3145732
  215.9 14.8 %collective-permute-start.14 = (bf16[128,2048]{0,1:T(8,128)(2,1)S(1)}, bf16[128,2048]{0,1:T(8,128)(2,1)S(1)}, u32[]{:S(2)}, u32[]{:S(2)}) collective-permute-start(bf16[128,2048]{0,1:T(8,128)(2,1)S(1)} %pad_maximum_fusion.4), channel_id=1, source_target_pairs={{0,8},{4,12},{8,0},{12,4},{16,24},{20,28},{24,16},{28,20},{1,9},{5... | collective-permute-start | bytes 1572872 | tf_op jit(solution)/shard_map/ppermute | solution.py:16
  217.5 25.4 %collective-permute-start.15 = (bf16[128,2048]{0,1:T(8,128)(2,1)S(1)}, bf16[128,2048]{0,1:T(8,128)(2,1)S(1)}, u32[]{:S(2)}, u32[]{:S(2)}) collective-permute-start(bf16[128,2048]{0,1:T(8,128)(2,1)S(1)} %pad_maximum_fusion.5), channel_id=1, source_target_pairs={{0,16},{4,20},{8,24},{12,28},{16,0},{20,4},{24,8},{28,12},{1,17},{... | collective-permute-start | bytes 1572872 | tf_op jit(solution)/shard_map/ppermute | solution.py:16
  219.5 23.3 %collective-permute-start.16 = (bf16[128,2048]{0,1:T(8,128)(2,1)S(1)}, bf16[128,2048]{0,1:T(8,128)(2,1)S(1)}, u32[]{:S(2)}, u32[]{:S(2)}) collective-permute-start(bf16[128,2048]{0,1:T(8,128)(2,1)S(1)} %pad_maximum_fusion.6), channel_id=1, source_target_pairs={{0,24},{4,28},{8,16},{12,20},{16,8},{20,12},{24,0},{28,4},{1,25},{... | collective-permute-start | bytes 1572872 | tf_op jit(solution)/shard_map/ppermute | solution.py:16
  243.4 2.1 copy-start.6
  243.4 2.1 copy-start.11
  243.4 2.1 copy-start.13
  243.4 2.0 copy-start.15
  243.4 2.0 copy-start.17
Sparse Core Ops, SparseCore 0:
  57.6 121.4 reduce-scatter.1

commit v2 on v1

v2 whole, which is shorter than its diff:
```python
import jax
import jax.numpy as jnp
from jax import lax
from jax.experimental import pallas as pl
from jax.experimental.pallas import tpu as pltpu
from jax.sharding import PartitionSpec as P

adapter_scale = 2.0
f32, bf16 = jnp.float32, jnp.bfloat16
HBM = pl.BlockSpec(memory_space=pltpu.HBM)
LATE = 10**9


def dot(a, b, ca, cb):
    return lax.dot_general(a, b, (((ca,), (cb,)), ((), ())), preferred_element_type=f32)


def exchange(x, axis, offset):
    size = lax.axis_size(axis)
    return lax.ppermute(x, axis, [(i, i ^ offset) for i in range(size)])


def swap(x, axis, groups):
    return lax.all_to_all(x, axis, 0, 0, axis_index_groups=groups, tiled=True)


def after(x, *earlier):
    return lax.optimization_barrier((x,) + earlier)[0]


def call(kernel, grid, prefetch, ins, outs, shapes, scratch, mib=20, cost=1):
    return pl.pallas_call(
        kernel,
        grid_spec=pltpu.PrefetchScalarGridSpec(
            num_scalar_prefetch=prefetch, grid=grid, in_specs=ins, out_specs=outs, scratch_shapes=list(scratch)
        ),
        out_shape=shapes,
        cost_estimate=pl.CostEstimate(flops=cost * 1000, bytes_accessed=cost, transcendentals=0),
        compiler_params=pltpu.CompilerParams(vmem_limit_bytes=mib * 2**20),
    )


def array(*shape):
    return pltpu.HBM(shape, bf16)


def far(*xs):
    return [pltpu.with_memory_space_constraint(x, pltpu.HBM) for x in xs]


def vmem(*shape):
    return pltpu.VMEM(shape, bf16)


def sems(count):
    return pltpu.SemaphoreType.DMA((count,))


def fetch(copies, sem, first=0):
    copies = [pltpu.make_async_copy(a, b, sem.at[first + i]) for i, (a, b) in enumerate(copies)]
    for c in copies:
        c.start()
    return copies


def wait(copies):
    for c in copies:
        c.wait()


def own_adapter(A, B, half):
    rank, width = B.shape

    def kernel(A, B, out, both, sem):
        wait(fetch([(A, both.at[pl.ds(0, rank)]), (B, both.at[pl.ds(rank, rank)])], sem))
        wait(fetch([(both, out.at[j]) for j in range(half)], sem, 2))

    return call(
        kernel, (1,), 0, [HBM, HBM], HBM, array(half, 2 * rank, width), [vmem(2 * rank, width), sems(2 + half)], mib=4
    )(*far(A, B))


def backward(dY, W, n):
    rows, width = dY.shape
    size = W.shape[0] // n

    def kernel(dY, W, out, y, block, sem, out_sem):
        i = pl.program_id(0)
        slot = lax.rem(i, 2)

        def leave(step, slot):
            return pltpu.make_async_copy(block.at[slot], out.at[step], out_sem.at[slot])

        @pl.when(i == 0)
        def _():
            wait(fetch([(dY, y)], sem))

        @pl.when(i >= 2)
        def _():
            leave(i - 2, slot).wait()

        block[slot] = dot(y[...], W[...], 1, 1).astype(bf16)
        leave(i, slot).start()

        @pl.when(i == n - 1)
        def _():
            if n > 1:
                leave(i - 1, 1 - slot).wait()
            leave(i, slot).wait()

    return call(
        kernel,
        (n,),
        0,
        [HBM, pl.BlockSpec((size, width), lambda i: (i, 0))],
        HBM,
        array(n, rows, size),
        [vmem(rows, width), vmem(2, rows, size), sems(1), sems(2)],
        mib=32,
    )(*far(dY, W))


def add_on(plan, at, arrived, back, cost):
    rows, width = arrived.shape
    steps = 4
    size = rows // steps

    def kernel(plan, arrived, back, out, a, b, sem):
        parts = [pl.ds(i * size, size) for i in range(steps)]
        add = plan[at + 1] == 1
        ins = [pltpu.make_async_copy(arrived.at[p], a.at[p], sem.at[i]) for i, p in enumerate(parts)]
        adds = [pltpu.make_async_copy(back.at[plan[at], p], b.at[p], sem.at[steps + i]) for i, p in enumerate(parts)]
        outs = [pltpu.make_async_copy(a.at[p], out.at[p], sem.at[2 * steps + i]) for i, p in enumerate(parts)]
        for i in range(steps):
            ins[i].start()
            pl.when(add)(adds[i].start)
        for i, p in enumerate(parts):
            ins[i].wait()

            @pl.when(add)
            def _():
                adds[i].wait()
                a[p] = (a[p].astype(f32) + b[p].astype(f32)).astype(bf16)

            outs[i].start()
        wait(outs)

    return call(
        kernel,
        (1,),
        1,
        [HBM, HBM],
        HBM,
        array(rows, width),
        [vmem(rows, width), vmem(rows, width), sems(3 * steps)],
        mib=8,
        cost=cost,
    )(plan, *far(arrived, back))


def finish(plan, arrived, back, own, other):
    rows, width = own.shape
    steps = 4
    size = rows // steps

    def kernel(plan, one, two, back, own, other, out, held, done, sem):
        refs = [one, two, back.at[plan[0]], own, other.at[pl.ds(rows, rows)]]
        parts = [pl.ds(i * size, size) for i in range(steps)]
        ins = [
            fetch([(r.at[p], held.at[k, p]) for k, r in enumerate(refs)], sem, i * len(refs))
            for i, p in enumerate(parts)
        ]
        outs = []
        for i, p in enumerate(parts):
            wait(ins[i])
            one, two, base, own, other = (held[k, p].astype(f32) for k in range(len(refs)))
            done[p] = ((one + two + base) + (own + other)).astype(bf16)
            outs += fetch([(done.at[p], out.at[p])], sem, steps * len(refs) + i)
        wait(outs)

    return call(
        kernel,
        (1,),
        1,
        [HBM] * 5,
        HBM,
        array(rows, width),
        [vmem(5, rows, width), vmem(rows, width), sems(6 * steps)],
        mib=16,
    )(plan, *far(arrived[0], arrived[1], back, own, other))


def forward(plan, at, n, W, blocks, term, other):
    rows, width = blocks[0].shape
    columns = W.shape[1]
    split = 2 if columns % 256 == 0 else 1
    part = columns // split

    def kernel(plan, *refs):
        blocks, (W, term, other, out, held, total, terms, sem) = refs[:-8], refs[-8:]
        own, ones, others = blocks[0], blocks[1:n], blocks[n:]
        h, s = pl.program_id(0), pl.program_id(1)

        def copy(ref, i):
            return pltpu.make_async_copy(ref, held.at[i], sem.at[i])

        lora = [
            pltpu.make_async_copy(term, terms.at[0], sem.at[n]),
            pltpu.make_async_copy(other.at[pl.ds(0, rows)], terms.at[1], sem.at[n + 1]),
        ]

        @pl.when((h == 0) & (s == 0))
        def _():
            copy(own, 0).start()
            for i in range(1, n):
                pl.when(plan[at + n + i] == 1)(copy(ones[i - 1], i).start)
                pl.when(plan[at + n + i] == 0)(copy(others[i - 1], i).start)
            for c in lora:
                c.start()

        for i in range(n):
            pl.when((h == 0) & (s == i))(copy(own, i).wait)

        product = jnp.dot(held[s], W[...], preferred_element_type=f32)

        @pl.when(s == 0)
        def _():
            total[...] = product

        @pl.when((s > 0) & (s < n - 1))
        def _():
            total[...] += product

        @pl.when((h == 0) & (s == n - 1))
        def _():
            wait(lora)

        for i in range(split):

            @pl.when((h == i) & (s == n - 1))
            def _():
                mine = slice(i * part, (i + 1) * part)
                added = terms[0, :, mine].astype(f32) + terms[1, :, mine].astype(f32)
                out[...] = (total[...] + product + added).astype(bf16)

    return call(
        kernel,
        (split, n),
        1,
        [HBM] * len(blocks) + [pl.BlockSpec((width, part), lambda h, s, plan: (plan[at + s], h)), HBM, HBM],
        pl.BlockSpec((rows, part), lambda h, s, plan: (0, h)),
        array(rows, columns),
        [vmem(n, rows, width), pltpu.VMEM((rows, part), f32), vmem(2, rows, columns), sems(n + 2)],
        mib=32,
    )(plan, *far(*blocks, W, term, other))


def chosen_of(plan, slots, ids, rank, half):
    slot = jnp.zeros(ids.shape, jnp.int32)
    for a in range(slots.shape[0]):
        slot = jnp.where(ids == a, slots[a], slot)
    column = lax.broadcasted_iota(jnp.int32, (ids.shape[0], half * rank), 1) // rank
    return slot == 2 * column + (plan[1] & 1)


def pieces(gathered, downs, ups, rank):
    half = gathered.shape[0]
    return [(gathered.at[j, pl.ds(0, rank)], downs.at[pl.ds(j * rank, rank)]) for j in range(half)] + [
        (gathered.at[j, pl.ds(rank, rank)], ups.at[pl.ds(j * rank, rank)]) for j in range(half)
    ]


def low_parts(plan, slots, ids, Xs, dYs, gathered, rank, n):
    rows, width = Xs[0].shape
    half = gathered.shape[0]

    def kernel(plan, slots, ids, X, X_other, dY, dY_other, gathered, out, x, y, downs, ups, part, sem):
        top, bottom = pl.ds(0, rows), pl.ds(rows, rows)
        adapters = pieces(gathered, downs, ups, rank)
        ins = fetch([(X, x.at[top]), (X_other, x.at[bottom])] + adapters[:half], sem)
        more = fetch([(dY, y.at[top]), (dY_other, y.at[bottom])] + adapters[half:], sem, 2 + half)
        chosen = chosen_of(plan, slots, ids[...], rank, half)

        def pick(a, b):
            both = jnp.where(chosen, dot(a[...], b[...], 1, 1), 0)
            return sum(both[:, j * rank : (j + 1) * rank] for j in range(half))

        wait(ins)
        low = pick(x, downs)
        wait(more)
        part[...] = jnp.concatenate([low, pick(y, ups)], axis=1).astype(bf16)
        wait(fetch([(part, out.at[k]) for k in range(n)], sem, 4 + 2 * half))

    return call(
        kernel,
        (1,),
        2,
        [pl.BlockSpec((2 * rows, 1), lambda i, *_: (0, 0))] + [HBM] * 5,
        HBM,
        array(n, 2 * rows, 2 * rank),
        [vmem(2 * rows, width)] * 2
        + [vmem(half * rank, width)] * 2
        + [vmem(2 * rows, 2 * rank), sems(4 + 2 * half + n)],
    )(plan, slots, ids, *far(*Xs, *dYs, gathered))


def spread(parts, chosen, rank, half):
    total = sum(parts[k].astype(f32) for k in range(parts.shape[0]))
    low, grad = total[:, :rank].astype(bf16), (adapter_scale * total[:, rank:]).astype(bf16)
    zero = jnp.zeros((), bf16)
    return [jnp.where(chosen, jnp.concatenate([v] * half, axis=1), zero) for v in (low, grad)]


def adapter_grads(plan, slots, ids, parts, Xs, dYs, rank, half):
    rows, width = Xs[0].shape

    def kernel(plan, slots, ids, parts, X, X_other, dY, dY_other, out, held, x, y, grads, sem):
        top, bottom = pl.ds(0, rows), pl.ds(rows, rows)
        ins = fetch(
            [(parts, held), (X, x.at[top]), (X_other, x.at[bottom]), (dY, y.at[top]), (dY_other, y.at[bottom])], sem
        )
        chosen = chosen_of(plan, slots, ids[...], rank, half)
        ins[0].wait()
        low, grad = spread(held, chosen, rank, half)
        wait(ins[1:3])
        shrink = dot(grad, x[...], 0, 0).astype(bf16)
        for j in range(half):
            grads[j, :rank] = shrink[j * rank : (j + 1) * rank]
        wait(ins[3:])
        expand = (adapter_scale * dot(low, y[...], 0, 0)).astype(bf16)
        for j in range(half):
            grads[j, rank:] = expand[j * rank : (j + 1) * rank]
        wait(fetch([(grads, out)], sem, 5))

    return call(
        kernel,
        (1,),
        2,
        [pl.BlockSpec((2 * rows, 1), lambda i, *_: (0, 0))] + [HBM] * 5,
        HBM,
        array(half, 2 * rank, width),
        [vmem(*parts.shape)] + [vmem(2 * rows, width)] * 2 + [vmem(half, 2 * rank, width), sems(6)],
    )(plan, slots, ids, *far(parts, *Xs, *dYs))


def lora_terms(plan, slots, ids, parts, gathered, rank):
    half, width = gathered.shape[0], gathered.shape[2]
    rows = ids.shape[0] // 2

    def kernel(plan, slots, ids, parts, gathered, term, back, other, held, downs, ups, terms, sem):
        ins = fetch([(parts, held)] + pieces(gathered, downs, ups, rank), sem)
        chosen = chosen_of(plan, slots, ids[...], rank, half)
        ins[0].wait()
        low, grad = spread(held, chosen, rank, half)
        wait(ins[1:])
        top, bottom = pl.ds(0, rows), pl.ds(rows, rows)
        terms[0] = (adapter_scale * dot(low, ups[...], 1, 0)).astype(bf16)
        outs = fetch([(terms.at[0, top], term), (terms.at[0, bottom], other.at[top])], sem, 1 + 2 * half)
        terms[1] = dot(grad, downs[...], 1, 0).astype(bf16)
        wait(outs + fetch([(terms.at[1, top], back), (terms.at[1, bottom], other.at[bottom])], sem, 3 + 2 * half))

    return call(
        kernel,
        (1,),
        2,
        [pl.BlockSpec((2 * rows, 1), lambda i, *_: (0, 0)), HBM, HBM],
        [HBM] * 3,
        [array(rows, width), array(rows, width), array(2 * rows, width)],
        [vmem(*parts.shape)] + [vmem(half * rank, width)] * 2 + [vmem(2, 2 * rows, width), sems(5 + 2 * half)],
    )(plan, slots, ids, *far(parts, gathered))


def add_up(blocks, rank):
    half, _, width = blocks.shape

    def kernel(blocks, shrink, expand, held, total, sem):
        wait(fetch([(blocks, held)], sem))
        total[...] = sum(held[j].astype(f32) for j in range(half)).astype(bf16)
        wait(fetch([(total.at[pl.ds(0, rank)], shrink), (total.at[pl.ds(rank, rank)], expand)], sem, 1))

    return call(
        kernel,
        (1,),
        0,
        [HBM],
        [HBM] * 2,
        [array(rank, width)] * 2,
        [vmem(*blocks.shape), vmem(2 * rank, width), sems(3)],
        mib=8,
    )(*far(blocks))


def body(X, dY, W, A, B, adapter_rows, adapter_slot):
    rows, width = X.shape
    rank = A.shape[2]
    n, D = lax.axis_size("tensor"), lax.axis_size("dp")
    z, me = lax.axis_index("tensor"), lax.axis_index("dp")
    half = D // 2
    chips = [list(range(k, D, 2)) for k in (0, 1)]

    odd = me & 1
    place = [jnp.where(odd == 0, z, n - 1 - z), jnp.where(odd == 0, n - 1 - z, z)]
    up = [(d * n + i, d * n + i + 1) for d in range(D) for i in range(n - 1)]
    pairs = [[(a, b) if (a // n) % 2 == k else (b, a) for a, b in up] for k in (0, 1)]

    def along(x, k):
        return lax.ppermute(x, ("dp", "tensor"), pairs[k])

    def z_of(position, k):
        return jnp.where(odd == k, position, n - 1 - position)

    plan = [z, me]
    for s in range(1, n):
        for k in (0, 1):
            plan += [jnp.clip(z_of(n - s + place[k], k), 0, n - 1), place[k] < s]
    plan += [z_of(lax.rem(place[0] - s + n, n), 0) for s in range(n)] + [place[0] >= s for s in range(n)]
    plan = jnp.stack([v.astype(jnp.int32) for v in plan])

    arrived = [[X], [X]]
    arrived[0].append(along(X, 0))

    X_other, dY_other, rows_other = (exchange(v, "dp", 1) for v in (X, dY, adapter_rows))
    others = (X_other, dY_other, rows_other)
    own = own_adapter(A[0].T, after(B, *others)[0], half)
    gathered = swap(own, "dp", chips)
    arrived[1].append(along(after(X, *others), 1))

    ids = jnp.concatenate([adapter_rows, rows_other], axis=0)
    back = backward(after(dY, own, ids), W, n)

    def onward(s, k, *earlier):
        cost = 1 if s < n - 1 else LATE
        payload = add_on(plan, 2 + 4 * (s - 1) + 2 * k, after(arrived[k][s], *earlier), back, cost)
        arrived[k].append(along(payload, k))
        return payload

    payload = onward(1, 0)
    payload = onward(1, 1, payload)

    gathered = after(gathered, payload)
    part = low_parts(plan, adapter_slot, ids, (X, X_other), (dY, dY_other), gathered, rank, n)
    parts = swap(part, "tensor", None)

    payload = onward(2, 0, part)
    payload = onward(2, 1, payload)

    parts = after(parts, payload)
    mine = adapter_grads(plan, adapter_slot, ids, parts, (X, X_other), (dY, dY_other), rank, half)
    arriving = swap(mine, "dp", chips)
    term, back_term, send = lora_terms(plan, adapter_slot, ids, after(parts, mine), gathered, rank)
    other = exchange(send, "dp", 1)

    for s in range(3, n):
        payload = onward(s, 0, payload, send)
        payload = onward(s, 1, payload, send)

    blocks = [after(X, payload)] + arrived[0][1:n] + [arrived[1][n - s] for s in range(1, n)]
    projected = forward(plan, 2 + 4 * (n - 1), n, W, blocks, term, other)

    shrink, expand = add_up(after(arriving, projected), rank)
    activation = finish(plan, (arrived[0][n], arrived[1][n]), back, after(back_term, expand), other)
    return projected, activation, shrink.T[None], expand[None]


def solution(mesh):
    return jax.shard_map(
        body,
        mesh=mesh,
        in_specs=(
            P("dp", "tensor"),
            P("dp", "tensor"),
            P(None, "tensor"),
            P("dp", "tensor", None),
            P("dp", None, "tensor"),
            P("dp", None),
            P(),
        ),
        out_specs=(
            P("dp", "tensor"),
            P("dp", "tensor"),
            P("dp", "tensor", None),
            P("dp", None, "tensor"),
        ),
        check_vma=False,
    )
```

time: 256 us -> 159 us (0.62)
  Pallas kernels: 0 us -> 80.7 us
  waiting for transfers between devices: 110 us -> 30.2 us
  matrix products: 62.1 us -> 0 us
  between operations: 14.5 us -> 1.14 us
  local copies, waits for them, and re-layouts: 13.8 us -> 5.42 us
  starting transfers between devices: 48.1 us -> 40.6 us
  other arithmetic: 6.64 us -> 0 us
    pallas_call x0 -> x14, Pallas kernels: none -> 80.7 us  [the longest x1 19.5 us: forward(): call(kernel, (split, n), 1, [HBM] * len(blocks) + [pl.BlockSpec((width, p...]
    ppermute x11 -> x4, waiting for transfers between devices: 70.4 us -> 1.35 us  [exchange(): return lax.ppermute(x, axis, [(i, i ^ offset) for i in range(size)])]
    dot_general x21 -> x0, matrix products: 62.1 us -> none  [dot(): lax.dot_general(a, b, (((ca,), (cb,)), ((), ())), preferred_element_type=...]
    ppermute x6 -> x8, waiting for transfers between devices: 39.9 us -> 5.54 us  [along(): return lax.ppermute(x, ('dp', 'tensor'), pairs[k])]
    all_to_all x0 -> x3, waiting for transfers between devices: none -> 23.3 us  [swap(): return lax.all_to_all(x, axis, 0, 0, axis_index_groups=groups, tiled=True)]
    ppermute x11 -> x4, starting transfers between devices: 13.4 us -> 0.67 us  [exchange(): return lax.ppermute(x, axis, [(i, i ^ offset) for i in range(size)])]
    all_to_all x0 -> x3, starting transfers between devices: none -> 11.8 us  [swap(): return lax.all_to_all(x, axis, 0, 0, axis_index_groups=groups, tiled=True)]
    ppermute x6 -> x8, starting transfers between devices: 34.7 us -> 28.1 us  [along(): return lax.ppermute(x, ('dp', 'tensor'), pairs[k])]
  transfers between devices with their start and end apart: 18 -> 15, of which waited for: 8 -> 3; matrix products, arithmetic and copies ran while one was open for 30% -> 0% of each run, Pallas kernels for 0% -> 48%
where the time goes in v2:
time: 159 us; the launch traced here: 158 us
  Pallas kernels  80.7 us (51%)
  starting transfers between devices  40.6 us (26%)
  waiting for transfers between devices  30.2 us (19%)
  local copies, waits for them, and re-layouts  5.42 us (3%)
    ppermute x8, starting transfers between devices, along(): return lax.ppermute(x, ('dp', 'tensor'), pairs[k])  28.1 us
    all_to_all x3, waiting for transfers between devices, swap(): return lax.all_to_all(x, axis, 0, 0, axis_index_groups=groups, tiled=True)  23.3 us
    pallas_call x1, Pallas kernels, forward(): call(kernel, (split, n), 1, [HBM] * len(blocks) + [pl.BlockSpec((width, p...  19.5 us
    pallas_call x1, Pallas kernels, backward(): call(kernel, (n,), 0, [HBM, pl.BlockSpec((size, width), lambda i: (i, 0))...  18.7 us
    pallas_call x6, Pallas kernels, add_on(): call(kernel, (1,), 1, [HBM, HBM], HBM, array(rows, width), [vmem(rows, wi...  16.4 us
    all_to_all x3, starting transfers between devices, swap(): return lax.all_to_all(x, axis, 0, 0, axis_index_groups=groups, tiled=True)  11.8 us
    pallas_call x1, Pallas kernels, low_parts(): call(kernel, (1,), 2, [pl.BlockSpec((2 * rows, 1), lambda i, *_: (0, 0))]...  6.08 us
    ppermute x8, waiting for transfers between devices, along(): return lax.ppermute(x, ('dp', 'tensor'), pairs[k])  5.54 us
  transfers between devices with their start and end apart: 15, of which 3 were waited for; matrix products, arithmetic and copies ran while one was open for 0% of the time, Pallas kernels for 48%

profile of v2, /device:TPU:0, one launch (start us, length us, event | category | flops | bytes accessed | tf_op | source)
XLA Modules:
  0.0 158.0 jit_solution(1251777009372539918)
XLA Ops:
  0.6 0.5 collective-permute-start.1
  1.1 0.1 collective-permute-start
  1.2 5.9 %collective-permute-start.4 = (bf16[256,2048]{1,0:T(8,128)(2,1)}, bf16[256,2048]{1,0:T(8,128)(2,1)}, u32[]{:S(2)}, u32[]{:S(2)}) collective-permute-start(bf16[256,2048]{1,0:T(8,128)(2,1)} %refs_0_), channel_id=1, source_target_pairs={{0,1},{1,2},{2,3},{5,4},{6,5},{7,6},{8,9},{9,10},{10,11},{13,12},{... | collective-permute-start | bytes 3145736 | tf_op jit(solution)/shard_map/ppermute | solution.py:407
  7.1 0.0 collective-permute-start.2
  7.2 1.3 collective-permute-done.2
  8.5 0.0 collective-permute-done.1.dY_other
  8.5 0.0 copy-start.5
  8.5 0.0 collective-permute-done.X_other
  8.5 0.0 copy-start.6
  8.5 2.8 %shard_map.102 = bf16[4,128,2048]{2,1,0:T(8,128)(2,1)} custom-call(bf16[64,2048]{1,0:T(8,128)(2,1)} %bitcast.30, bf16[64,2048]{1,0:T(8,128)(2,1)} %bitcast.31), custom_call_target="tpu_custom_call" | custom-call | flops 1000 | bytes 1 | tf_op jit(solution)/shard_map/pallas_call | solution.py:78
  11.4 0.0 copy-start.9
  11.4 0.0 copy-start.2
  11.4 0.0 copy-done.5
  11.4 0.0 copy-done.6
  11.4 3.9 %all-to-all-start = ((bf16[4,128,2048]{2,1,0:T(8,128)(2,1)}), bf16[4,128,2048]{2,1,0:T(8,128)(2,1)S(1)}, u32[]{:S(2)}, u32[]{:S(2)}) async-start(bf16[4,128,2048]{2,1,0:T(8,128)(2,1)} %shard_map.102), calls=%async_computation | async-start | bytes 4194304 | tf_op jit(solution)/shard_map/all_to_all | solution.py:24
  15.3 0.1 stack.131.plan
  15.4 0.0 copy-done.9
  15.4 0.0 copy-done.2
  15.4 1.3 collective-permute-start.3
  16.7 18.7 %shard_map.103.back = bf16[4,256,2048]{2,1,0:T(8,128)(2,1)} custom-call(bf16[256,2048]{1,0:T(8,128)(2,1)} %dY.4, bf16[8192,2048]{1,0:T(8,128)(2,1)} %refs_7_.1), custom_call_target="tpu_custom_call" | custom-call | flops 1000 | bytes 1 | tf_op jit(solution)/shard_map/pallas_call | solution.py:111
  35.5 0.0 collective-permute-done.4.arrived.refs_1_
  35.5 2.9 %shard_map.104 = bf16[256,2048]{1,0:T(8,128)(2,1)} custom-call(s32[22]{0:T(128)S(1)} %stack.131.plan, bf16[256,2048]{1,0:T(8,128)(2,1)} %collective-permute-done.4.arrived.refs_1_, bf16[4,256,2048]{2,1,0:T(8,128)(2,1)} %shard_map.103.back), custom_call_target="tpu_custom_call" | custom-call | flops 1000 | bytes 1 | tf_op jit(solution)/shard_map/pallas_call | solution.py:148
  38.4 0.0 copy-start
  38.4 5.2 %collective-permute-start.6 = (bf16[256,2048]{1,0:T(8,128)(2,1)}, bf16[256,2048]{1,0:T(8,128)(2,1)}, u32[]{:S(2)}, u32[]{:S(2)}) collective-permute-start(bf16[256,2048]{1,0:T(8,128)(2,1)} %shard_map.104), channel_id=1, source_target_pairs={{0,1},{1,2},{2,3},{5,4},{6,5},{7,6},{8,9},{9,10},{10,11},{13,12},{... | collective-permute-start | bytes 3145736 | tf_op jit(solution)/shard_map/ppermute | solution.py:407
  43.6 0.0 collective-permute-done.3.arrived.refs_6_
  43.6 1.0 copy-done.4
  44.6 2.6 %shard_map.105 = bf16[256,2048]{1,0:T(8,128)(2,1)} custom-call(s32[22]{0:T(128)S(1)} %stack.131.plan, bf16[256,2048]{1,0:T(8,128)(2,1)} %copy-done.4, bf16[4,256,2048]{2,1,0:T(8,128)(2,1)} %shard_map.103.back), custom_call_target="tpu_custom_call" | custom-call | flops 1000 | bytes 1 | tf_op jit(solution)/shard_map/pallas_call | solution.py:148
  47.1 1.3 collective-permute-start.5
  48.4 0.1 copy.13.ids
  48.6 0.0 all-to-all-done.gathered
  48.6 0.0 copy-start.1
  48.6 1.4 copy-done.1
  50.0 0.0 copy-done
  50.0 6.1 %shard_map.106 = bf16[4,512,128]{2,1,0:T(8,128)(2,1)} custom-call(s32[22]{0:T(128)S(1)} %stack.131.plan, s32[8]{0:T(128)S(1)} %copy-done, s32[512,1]{1,0:T(8,128)S(1)} %copy.13.ids, bf16[256,2048]{1,0:T(8,128)(2,1)} %refs_0_, bf16[256,2048]{1,0:T(8,128)(2,1)} %copy-done.6, bf16[256,2048]{1,0:T(8,128)(2,1)} %dY.4, bf16[256,2048]{1,0:T(8,128)(2,1)} %copy-done.5, ...), custom_call_target="tpu_custom_call" | custom-call | flops 1000 | bytes 1 | tf_op jit(solution)/shard_map/pallas_call | solution.py:294
  56.1 5.5 %collective-permute-done.6.arrived.refs_2_ = bf16[256,2048]{1,0:T(8,128)(2,1)} collective-permute-done((bf16[256,2048]{1,0:T(8,128)(2,1)}, bf16[256,2048]{1,0:T(8,128)(2,1)}, u32[]{:S(2)}, u32[]{:S(2)}) %collective-permute-start.6) | collective-permute-done | bytes 1048608 | tf_op jit(solution)/shard_map/ppermute | solution.py:407
  61.6 2.9 %shard_map.107 = bf16[256,2048]{1,0:T(8,128)(2,1)} custom-call(s32[22]{0:T(128)S(1)} %stack.131.plan, bf16[256,2048]{1,0:T(8,128)(2,1)} %collective-permute-done.6.arrived.refs_2_, bf16[4,256,2048]{2,1,0:T(8,128)(2,1)} %shard_map.103.back), custom_call_target="tpu_custom_call" | custom-call | flops 1000 | bytes 1 | tf_op jit(solution)/shard_map/pallas_call | solution.py:148
  64.5 4.5 %collective-permute-start.8 = (bf16[256,2048]{1,0:T(8,128)(2,1)}, bf16[256,2048]{1,0:T(8,128)(2,1)S(1)}, u32[]{:S(2)}, u32[]{:S(2)}) collective-permute-start(bf16[256,2048]{1,0:T(8,128)(2,1)} %shard_map.107), channel_id=1, source_target_pairs={{0,1},{1,2},{2,3},{5,4},{6,5},{7,6},{8,9},{9,10},{10,11},{13,12},{... | collective-permute-start | bytes 3145736 | tf_op jit(solution)/shard_map/ppermute | solution.py:407
  69.0 3.5 %all-to-all-start.1 = ((bf16[4,512,128]{2,1,0:T(8,128)(2,1)}), bf16[4,512,128]{2,1,0:T(8,128)(2,1)S(1)}, u32[]{:S(2)}, u32[]{:S(2)}) async-start(bf16[4,512,128]{2,1,0:T(8,128)(2,1)} %shard_map.106), calls=%async_computation.1 | async-start | bytes 1048576 | tf_op jit(solution)/shard_map/all_to_all | solution.py:24
  72.4 0.0 collective-permute-done.5.arrived.refs_5_
  72.5 2.6 %shard_map.108 = bf16[256,2048]{1,0:T(8,128)(2,1)} custom-call(s32[22]{0:T(128)S(1)} %stack.131.plan, bf16[256,2048]{1,0:T(8,128)(2,1)} %collective-permute-done.5.arrived.refs_5_, bf16[4,256,2048]{2,1,0:T(8,128)(2,1)} %shard_map.103.back), custom_call_target="tpu_custom_call" | custom-call | flops 1000 | bytes 1 | tf_op jit(solution)/shard_map/pallas_call | solution.py:148
  75.0 1.3 collective-permute-start.7
  76.3 23.3 %all-to-all-done.1.parts = bf16[4,512,128]{2,1,0:T(8,128)(2,1)S(1)} async-done(((bf16[4,512,128]{2,1,0:T(8,128)(2,1)}), bf16[4,512,128]{2,1,0:T(8,128)(2,1)S(1)}, u32[]{:S(2)}, u32[]{:S(2)}) %all-to-all-start.1) | async-done | bytes 524320 | tf_op jit(solution)/shard_map/all_to_all | solution.py:24
  99.6 0.8 copy-done.3
  100.4 5.3 %shard_map.109 = bf16[4,128,2048]{2,1,0:T(8,128)(2,1)} custom-call(s32[22]{0:T(128)S(1)} %stack.131.plan, s32[8]{0:T(128)S(1)} %copy-done, s32[512,1]{1,0:T(8,128)S(1)} %copy.13.ids, bf16[4,512,128]{2,1,0:T(8,128)(2,1)} %copy-done.3, bf16[256,2048]{1,0:T(8,128)(2,1)} %refs_0_, bf16[256,2048]{1,0:T(8,128)(2,1)} %copy-done.6, bf16[256,2048]{1,0:T(8,128)(2,1)} %dY.4, ...), custom_call_target="tpu_custom_call" | custom-call | flops 1000 | bytes 1 | tf_op jit(solution)/shard_map/pallas_call | solution.py:335
  105.7 4.5 %all-to-all-start.2 = ((bf16[4,128,2048]{2,1,0:T(8,128)(2,1)}), bf16[4,128,2048]{2,1,0:T(8,128)(2,1)}, u32[]{:S(2)}, u32[]{:S(2)}) async-start(bf16[4,128,2048]{2,1,0:T(8,128)(2,1)} %shard_map.109), calls=%async_computation.2 | async-start | bytes 4194304 | tf_op jit(solution)/shard_map/all_to_all | solution.py:24
  110.2 5.0 %shard_map.110 = (bf16[256,2048]{1,0:T(8,128)(2,1)}, bf16[256,2048]{1,0:T(8,128)(2,1)}, bf16[512,2048]{1,0:T(8,128)(2,1)}) custom-call(s32[22]{0:T(128)S(1)} %stack.131.plan, s32[8]{0:T(128)S(1)} %copy-done, s32[512,1]{1,0:T(8,128)S(1)} %copy.13.ids, bf16[4,512,128]{2,1,0:T(8,128)(2,1)} %copy-done.3, bf16[4,128,2048]{2,1,0:T(8,128)(2,1)} %copy-done.1), custom_call_target="tpu_custom_call" | custom-call | flops 1000 | bytes 1 | tf_op jit(solution)/shard_map/pallas_call | solution.py:362
  115.2 0.1 collective-permute-start.9
  115.3 0.0 collective-permute-done.8.arrived.refs_3_
  115.3 0.0 copy-start.7
  115.3 1.0 copy-done.7
  116.3 2.9 %shard_map.111 = bf16[256,2048]{1,0:T(8,128)(2,1)} custom-call(s32[22]{0:T(128)S(1)} %stack.131.plan, bf16[256,2048]{1,0:T(8,128)(2,1)} %copy-done.7, bf16[4,256,2048]{2,1,0:T(8,128)(2,1)} %shard_map.103.back), custom_call_target="tpu_custom_call" | custom-call | flops 999999995904 | bytes 1000000000 | tf_op jit(solution)/shard_map/pallas_call | solution.py:148
  119.2 7.2 %collective-permute-start.10 = (bf16[256,2048]{1,0:T(8,128)(2,1)}, bf16[256,2048]{1,0:T(8,128)(2,1)}, u32[]{:S(2)}, u32[]{:S(2)}) collective-permute-start(bf16[256,2048]{1,0:T(8,128)(2,1)} %shard_map.111), channel_id=1, source_target_pairs={{0,1},{1,2},{2,3},{5,4},{6,5},{7,6},{8,9},{9,10},{10,11},{13,12},{... | collective-permute-start | bytes 3145736 | tf_op jit(solution)/shard_map/ppermute | solution.py:407
  126.4 0.0 collective-permute-done.7.arrived.refs_4_
  126.4 2.6 %shard_map.112 = bf16[256,2048]{1,0:T(8,128)(2,1)} custom-call(s32[22]{0:T(128)S(1)} %stack.131.plan, bf16[256,2048]{1,0:T(8,128)(2,1)} %collective-permute-done.7.arrived.refs_4_, bf16[4,256,2048]{2,1,0:T(8,128)(2,1)} %shard_map.103.back), custom_call_target="tpu_custom_call" | custom-call | flops 999999995904 | bytes 1000000000 | tf_op jit(solution)/shard_map/pallas_call | solution.py:148
  129.0 1.5 collective-permute-start.11
  130.4 0.0 collective-permute-done.9.refs_9_.other
  130.5 19.5 %shard_map.113 = bf16[256,2048]{1,0:T(8,128)(2,1)} custom-call(s32[22]{0:T(128)S(1)} %stack.131.plan, bf16[256,2048]{1,0:T(8,128)(2,1)} %refs_0_, bf16[256,2048]{1,0:T(8,128)(2,1)} %collective-permute-done.4.arrived.refs_1_, bf16[256,2048]{1,0:T(8,128)(2,1)} %collective-permute-done.6.arrived.refs_2_, bf16[256,2048]{1,0:T(8,128)(2,1)} %copy-done.7, ...), custom_call_target="tpu_custom_call" | custom-call | flops 1000 | bytes 1 | tf_op jit(solution)/shard_map/pallas_call | solution.py:246
  150.0 0.0 all-to-all-done.2.blocks
  150.0 2.7 %shard_map.114 = (bf16[64,2048]{1,0:T(8,128)(2,1)}, bf16[64,2048]{1,0:T(8,128)(2,1)}) custom-call(bf16[4,128,2048]{2,1,0:T(8,128)(2,1)} %all-to-all-done.2.blocks), custom_call_target="tpu_custom_call" | custom-call | flops 1000 | bytes 1 | tf_op jit(solution)/shard_map/pallas_call | solution.py:381
  152.6 0.0 collective-permute-done.10.one
  152.7 0.0 collective-permute-done.11.two
  152.7 0.0 copy-start.8
  152.7 1.0 copy-done.8
  153.7 4.2 %shard_map.115 = bf16[256,2048]{1,0:T(8,128)(2,1)} custom-call(s32[22]{0:T(128)S(1)} %stack.131.plan, bf16[256,2048]{1,0:T(8,128)(2,1)} %collective-permute-done.10.one, bf16[256,2048]{1,0:T(8,128)(2,1)} %copy-done.8, bf16[4,256,2048]{2,1,0:T(8,128)(2,1)} %shard_map.103.back, bf16[256,2048]{1,0:T(8,128)(2,1)} %get-tuple-element.40.own, ...), custom_call_target="tpu_custom_call" | custom-call | flops 1000 | bytes 1 | tf_op jit(solution)/shard_map/pallas_call | solution.py:181
  (4 shorter events, 0.0 us)
Async XLA Ops:
  0.6 7.9 %collective-permute-start.1 = (bf16[256,2048]{1,0:T(8,128)(2,1)}, bf16[256,2048]{1,0:T(8,128)(2,1)S(1)}, u32[]{:S(2)}, u32[]{:S(2)}) collective-permute-start(bf16[256,2048]{1,0:T(8,128)(2,1)} %dY.4), channel_id=1, source_target_pairs={{0,4},{4,0},{8,12},{12,8},{16,20},{20,16},{24,28},{28,24},{1,5},{5... | collective-permute-start | bytes 3145736 | tf_op jit(solution)/shard_map/ppermute | solution.py:20
  1.1 7.4 %collective-permute-start = (bf16[256,2048]{1,0:T(8,128)(2,1)}, bf16[256,2048]{1,0:T(8,128)(2,1)S(1)}, u32[]{:S(2)}, u32[]{:S(2)}) collective-permute-start(bf16[256,2048]{1,0:T(8,128)(2,1)} %refs_0_), channel_id=1, source_target_pairs={{0,4},{4,0},{8,12},{12,8},{16,20},{20,16},{24,28},{28,24},{1,5},{5... | collective-permute-start | bytes 3145736 | tf_op jit(solution)/shard_map/ppermute | solution.py:20
  1.2 34.2 %collective-permute-start.4 = (bf16[256,2048]{1,0:T(8,128)(2,1)}, bf16[256,2048]{1,0:T(8,128)(2,1)}, u32[]{:S(2)}, u32[]{:S(2)}) collective-permute-start(bf16[256,2048]{1,0:T(8,128)(2,1)} %refs_0_), channel_id=1, source_target_pairs={{0,1},{1,2},{2,3},{5,4},{6,5},{7,6},{8,9},{9,10},{10,11},{13,12},{... | collective-permute-start | bytes 3145736 | tf_op jit(solution)/shard_map/ppermute | solution.py:407
  7.1 1.4 collective-permute-start.2
  8.5 2.9 %copy-start.5 = (bf16[256,2048]{1,0:T(8,128)(2,1)}, bf16[256,2048]{1,0:T(8,128)(2,1)S(1)}, u32[]{:S(2)}) copy-start(bf16[256,2048]{1,0:T(8,128)(2,1)S(1)} %collective-permute-done.1.dY_other) | copy-start | bytes 3145732
  8.5 2.9 %copy-start.6 = (bf16[256,2048]{1,0:T(8,128)(2,1)}, bf16[256,2048]{1,0:T(8,128)(2,1)S(1)}, u32[]{:S(2)}) copy-start(bf16[256,2048]{1,0:T(8,128)(2,1)S(1)} %collective-permute-done.X_other) | copy-start | bytes 3145732
  11.4 4.0 %copy-start.9 = (s32[256,1]{0,1:T(1,128)S(1)}, s32[256,1]{0,1:T(1,128)}, u32[]{:S(2)}) copy-start(s32[256,1]{0,1:T(1,128)} %param.12) | copy-start | bytes 3076
  11.4 4.0 %copy-start.2 = (bf16[256,2048]{1,0:T(8,128)(2,1)S(1)}, bf16[256,2048]{1,0:T(8,128)(2,1)}, u32[]{:S(2)}) copy-start(bf16[256,2048]{1,0:T(8,128)(2,1)} %refs_0_) | copy-start | bytes 3145732
  11.4 37.2 %all-to-all-start = ((bf16[4,128,2048]{2,1,0:T(8,128)(2,1)}), bf16[4,128,2048]{2,1,0:T(8,128)(2,1)S(1)}, u32[]{:S(2)}, u32[]{:S(2)}) async-start(bf16[4,128,2048]{2,1,0:T(8,128)(2,1)} %shard_map.102), calls=%async_computation | async-start | bytes 4194304 | tf_op jit(solution)/shard_map/all_to_all | solution.py:24
  15.4 28.2 %collective-permute-start.3 = (bf16[256,2048]{1,0:T(8,128)(2,1)S(1)}, bf16[256,2048]{1,0:T(8,128)(2,1)S(1)}, u32[]{:S(2)}, u32[]{:S(2)}) collective-permute-start(bf16[256,2048]{1,0:T(8,128)(2,1)S(1)} %copy-done.2), channel_id=1, source_target_pairs={{1,0},{2,1},{3,2},{4,5},{5,6},{6,7},{9,8},{10,9},{11,10},{12,13},{... | collective-permute-start | bytes 3145736 | tf_op jit(solution)/shard_map/ppermute | solution.py:407
  38.4 11.6 %copy-start = (s32[8]{0:T(128)S(1)}, s32[8]{0:T(128)}, u32[]{:S(2)}) copy-start(s32[8]{0:T(128)} %slots.5) | copy-start | bytes 100
  38.4 23.2 %collective-permute-start.6 = (bf16[256,2048]{1,0:T(8,128)(2,1)}, bf16[256,2048]{1,0:T(8,128)(2,1)}, u32[]{:S(2)}, u32[]{:S(2)}) collective-permute-start(bf16[256,2048]{1,0:T(8,128)(2,1)} %shard_map.104), channel_id=1, source_target_pairs={{0,1},{1,2},{2,3},{5,4},{6,5},{7,6},{8,9},{9,10},{10,11},{13,12},{... | collective-permute-start | bytes 3145736 | tf_op jit(solution)/shard_map/ppermute | solution.py:407
  43.6 1.0 copy-start.4
  47.1 25.3 %collective-permute-start.5 = (bf16[256,2048]{1,0:T(8,128)(2,1)}, bf16[256,2048]{1,0:T(8,128)(2,1)}, u32[]{:S(2)}, u32[]{:S(2)}) collective-permute-start(bf16[256,2048]{1,0:T(8,128)(2,1)} %shard_map.105), channel_id=1, source_target_pairs={{1,0},{2,1},{3,2},{4,5},{5,6},{6,7},{9,8},{10,9},{11,10},{12,13},{... | collective-permute-start | bytes 3145736 | tf_op jit(solution)/shard_map/ppermute | solution.py:407
  48.6 1.4 copy-start.1
  64.5 50.8 %collective-permute-start.8 = (bf16[256,2048]{1,0:T(8,128)(2,1)}, bf16[256,2048]{1,0:T(8,128)(2,1)S(1)}, u32[]{:S(2)}, u32[]{:S(2)}) collective-permute-start(bf16[256,2048]{1,0:T(8,128)(2,1)} %shard_map.107), channel_id=1, source_target_pairs={{0,1},{1,2},{2,3},{5,4},{6,5},{7,6},{8,9},{9,10},{10,11},{13,12},{... | collective-permute-start | bytes 3145736 | tf_op jit(solution)/shard_map/ppermute | solution.py:407
  69.0 30.6 %all-to-all-start.1 = ((bf16[4,512,128]{2,1,0:T(8,128)(2,1)}), bf16[4,512,128]{2,1,0:T(8,128)(2,1)S(1)}, u32[]{:S(2)}, u32[]{:S(2)}) async-start(bf16[4,512,128]{2,1,0:T(8,128)(2,1)} %shard_map.106), calls=%async_computation.1 | async-start | bytes 1048576 | tf_op jit(solution)/shard_map/all_to_all | solution.py:24
  75.0 51.4 %collective-permute-start.7 = (bf16[256,2048]{1,0:T(8,128)(2,1)}, bf16[256,2048]{1,0:T(8,128)(2,1)}, u32[]{:S(2)}, u32[]{:S(2)}) collective-permute-start(bf16[256,2048]{1,0:T(8,128)(2,1)} %shard_map.108), channel_id=1, source_target_pairs={{1,0},{2,1},{3,2},{4,5},{5,6},{6,7},{9,8},{10,9},{11,10},{12,13},{... | collective-permute-start | bytes 3145736 | tf_op jit(solution)/shard_map/ppermute | solution.py:407
  99.6 0.8 copy-start.3
  105.7 44.3 %all-to-all-start.2 = ((bf16[4,128,2048]{2,1,0:T(8,128)(2,1)}), bf16[4,128,2048]{2,1,0:T(8,128)(2,1)}, u32[]{:S(2)}, u32[]{:S(2)}) async-start(bf16[4,128,2048]{2,1,0:T(8,128)(2,1)} %shard_map.109), calls=%async_computation.2 | async-start | bytes 4194304 | tf_op jit(solution)/shard_map/all_to_all | solution.py:24
  115.2 15.2 %collective-permute-start.9 = (bf16[512,2048]{1,0:T(8,128)(2,1)}, bf16[512,2048]{1,0:T(8,128)(2,1)}, u32[]{:S(2)}, u32[]{:S(2)}) collective-permute-start(bf16[512,2048]{1,0:T(8,128)(2,1)} %get-tuple-element.32), channel_id=1, source_target_pairs={{0,4},{4,0},{8,12},{12,8},{16,20},{20,16},{24,28},{28,24},{1,5},{5... | collective-permute-start | bytes 6291464 | tf_op jit(solution)/shard_map/ppermute | solution.py:20
  115.3 1.0 copy-start.7
  119.2 33.5 %collective-permute-start.10 = (bf16[256,2048]{1,0:T(8,128)(2,1)}, bf16[256,2048]{1,0:T(8,128)(2,1)}, u32[]{:S(2)}, u32[]{:S(2)}) collective-permute-start(bf16[256,2048]{1,0:T(8,128)(2,1)} %shard_map.111), channel_id=1, source_target_pairs={{0,1},{1,2},{2,3},{5,4},{6,5},{7,6},{8,9},{9,10},{10,11},{13,12},{... | collective-permute-start | bytes 3145736 | tf_op jit(solution)/shard_map/ppermute | solution.py:407
  129.0 23.7 %collective-permute-start.11 = (bf16[256,2048]{1,0:T(8,128)(2,1)}, bf16[256,2048]{1,0:T(8,128)(2,1)S(1)}, u32[]{:S(2)}, u32[]{:S(2)}) collective-permute-start(bf16[256,2048]{1,0:T(8,128)(2,1)} %shard_map.112), channel_id=1, source_target_pairs={{1,0},{2,1},{3,2},{4,5},{5,6},{6,7},{9,8},{10,9},{11,10},{12,13},{... | collective-permute-start | bytes 3145736 | tf_op jit(solution)/shard_map/ppermute | solution.py:407
  152.7 1.0 copy-start.8

commit v3 on v2

--- a/solution.py
+++ b/solution.py
@@ -8,7 +8,10 @@
 adapter_scale = 2.0
 f32, bf16 = jnp.float32, jnp.bfloat16
 HBM = pl.BlockSpec(memory_space=pltpu.HBM)
-LATE = 10**9
+LATE = 10**12
+GRADS = 10**10
+BIG = 63
+BACK = 10**10
 
 
 def dot(a, b, ca, cb):
@@ -28,14 +31,14 @@
     return lax.optimization_barrier((x,) + earlier)[0]
 
 
-def call(kernel, grid, prefetch, ins, outs, shapes, scratch, mib=20, cost=1):
+def call(kernel, grid, prefetch, ins, outs, shapes, scratch, mib=BIG, cost=10**3):
     return pl.pallas_call(
         kernel,
         grid_spec=pltpu.PrefetchScalarGridSpec(
             num_scalar_prefetch=prefetch, grid=grid, in_specs=ins, out_specs=outs, scratch_shapes=list(scratch)
         ),
         out_shape=shapes,
-        cost_estimate=pl.CostEstimate(flops=cost * 1000, bytes_accessed=cost, transcendentals=0),
+        cost_estimate=pl.CostEstimate(flops=cost, bytes_accessed=1, transcendentals=0),
         compiler_params=pltpu.CompilerParams(vmem_limit_bytes=mib * 2**20),
     )
 
@@ -80,82 +83,94 @@
     )(*far(A, B))
 
 
-def backward(dY, W, n):
+def backward(plan, at, blocks, dY, W, n, cost):
     rows, width = dY.shape
     size = W.shape[0] // n
-
-    def kernel(dY, W, out, y, block, sem, out_sem):
-        i = pl.program_id(0)
-        slot = lax.rem(i, 2)
-
-        def leave(step, slot):
-            return pltpu.make_async_copy(block.at[slot], out.at[step], out_sem.at[slot])
-
-        @pl.when(i == 0)
-        def _():
-            wait(fetch([(dY, y)], sem))
-
-        @pl.when(i >= 2)
-        def _():
-            leave(i - 2, slot).wait()
-
-        block[slot] = dot(y[...], W[...], 1, 1).astype(bf16)
-        leave(i, slot).start()
-
-        @pl.when(i == n - 1)
-        def _():
-            if n > 1:
-                leave(i - 1, 1 - slot).wait()
-            leave(i, slot).wait()
-
-    return call(
-        kernel,
-        (n,),
-        0,
-        [HBM, pl.BlockSpec((size, width), lambda i: (i, 0))],
+    fine = 4 if size % 512 == 0 else 1
+    coarse = 2 if fine == 4 else 1
+    tile, chunk = size // coarse, size // fine
+
+    def kernel(plan, dY, W, out, y, w, done, sem, out_sem):
+        ins = fetch([(dY, y)], sem)
+        for b in range(blocks):
+            for i in range(fine):
+                source = pl.multiple_of(plan[at + b] * size + i * chunk, chunk)
+                to = pl.ds(b * size + i * chunk, chunk)
+                ins += fetch([(W.at[pl.ds(source, chunk)], w.at[to])], sem, 1 + b * fine + i)
+        ins[0].wait()
+        outs = []
+        for b in range(blocks):
+            for i in range(coarse):
+                per = fine // coarse
+                first = 1 + b * fine + i * per
+                wait(ins[first : first + per])
+                span = pl.ds(i * tile, tile)
+                done[b, :, span] = dot(y[...], w[pl.ds(b * size + i * tile, tile)], 1, 1).astype(bf16)
+                outs += fetch([(done.at[b, :, span], out.at[b, :, span])], out_sem, b * coarse + i)
+        wait(outs)
+
+    return call(
+        kernel,
+        (1,),
+        1,
+        [HBM, HBM],
         HBM,
-        array(n, rows, size),
-        [vmem(rows, width), vmem(2, rows, size), sems(1), sems(2)],
-        mib=32,
-    )(*far(dY, W))
-
-
-def add_on(plan, at, arrived, back, cost):
+        array(blocks, rows, size),
+        [
+            vmem(rows, width),
+            vmem(blocks * size, width),
+            vmem(blocks, rows, size),
+            sems(1 + blocks * fine),
+            sems(blocks * coarse),
+        ],
+        mib=BIG,
+        cost=cost,
+    )(plan, *far(dY, W))
+
+
+def add_on(plan, at, arrived, backs, cost):
     rows, width = arrived.shape
     steps = 4
     size = rows // steps
-
-    def kernel(plan, arrived, back, out, a, b, sem):
+    count = backs[0].shape[0]
+
+    def kernel(plan, arrived, *refs):
+        backs, (out, a, b, sem) = refs[: len(backs_)], refs[len(backs_) :]
         parts = [pl.ds(i * size, size) for i in range(steps)]
         add = plan[at + 1] == 1
         ins = [pltpu.make_async_copy(arrived.at[p], a.at[p], sem.at[i]) for i, p in enumerate(parts)]
-        adds = [pltpu.make_async_copy(back.at[plan[at], p], b.at[p], sem.at[steps + i]) for i, p in enumerate(parts)]
+        adds = [
+            [pltpu.make_async_copy(r.at[lax.rem(plan[at], count), p], b.at[p], sem.at[steps + i]) for r in backs]
+            for i, p in enumerate(parts)
+        ]
         outs = [pltpu.make_async_copy(a.at[p], out.at[p], sem.at[2 * steps + i]) for i, p in enumerate(parts)]
         for i in range(steps):
             ins[i].start()
-            pl.when(add)(adds[i].start)
+            for k in range(len(backs)):
+                pl.when(add & (lax.div(plan[at], count) == k))(adds[i][k].start)
         for i, p in enumerate(parts):
             ins[i].wait()
 
             @pl.when(add)
             def _():
-                adds[i].wait()
+                adds[i][0].wait()
                 a[p] = (a[p].astype(f32) + b[p].astype(f32)).astype(bf16)
 
             outs[i].start()
         wait(outs)
 
+    backs_ = backs
     return call(
         kernel,
         (1,),
         1,
-        [HBM, HBM],
+        [HBM] * (1 + len(backs)),
         HBM,
         array(rows, width),
         [vmem(rows, width), vmem(rows, width), sems(3 * steps)],
         mib=8,
         cost=cost,
-    )(plan, *far(arrived, back))
+    )(plan, *far(arrived, *backs))
 
 
 def finish(plan, arrived, back, own, other):
@@ -164,7 +179,7 @@
     size = rows // steps
 
     def kernel(plan, one, two, back, own, other, out, held, done, sem):
-        refs = [one, two, back.at[plan[0]], own, other.at[pl.ds(rows, rows)]]
+        refs = [one, two, back.at[back.shape[0] - 1], own, other.at[pl.ds(rows, rows)]]
         parts = [pl.ds(i * size, size) for i in range(steps)]
         ins = [
             fetch([(r.at[p], held.at[k, p]) for k, r in enumerate(refs)], sem, i * len(refs))
@@ -190,69 +205,69 @@
     )(plan, *far(arrived[0], arrived[1], back, own, other))
 
 
-def forward(plan, at, n, W, blocks, term, other):
-    rows, width = blocks[0].shape
+def forward(plan, at, n, W, blocks, rest=()):
+    rows, width = blocks[0][0].shape
     columns = W.shape[1]
-    split = 2 if columns % 256 == 0 else 1
-    part = columns // split
+    fine = 4 if width % 512 == 0 else 1
+    coarse = 2 if fine == 4 else 1
+    tile, chunk = width // coarse, width // fine
+    count = len(blocks)
+    arrays = [b for block in blocks for b in block]
 
     def kernel(plan, *refs):
-        blocks, (W, term, other, out, held, total, terms, sem) = refs[:-8], refs[-8:]
-        own, ones, others = blocks[0], blocks[1:n], blocks[n:]
-        h, s = pl.program_id(0), pl.program_id(1)
-
-        def copy(ref, i):
-            return pltpu.make_async_copy(ref, held.at[i], sem.at[i])
-
-        lora = [
-            pltpu.make_async_copy(term, terms.at[0], sem.at[n]),
-            pltpu.make_async_copy(other.at[pl.ds(0, rows)], terms.at[1], sem.at[n + 1]),
-        ]
-
-        @pl.when((h == 0) & (s == 0))
-        def _():
-            copy(own, 0).start()
-            for i in range(1, n):
-                pl.when(plan[at + n + i] == 1)(copy(ones[i - 1], i).start)
-                pl.when(plan[at + n + i] == 0)(copy(others[i - 1], i).start)
-            for c in lora:
-                c.start()
-
-        for i in range(n):
-            pl.when((h == 0) & (s == i))(copy(own, i).wait)
-
-        product = jnp.dot(held[s], W[...], preferred_element_type=f32)
-
-        @pl.when(s == 0)
-        def _():
-            total[...] = product
-
-        @pl.when((s > 0) & (s < n - 1))
-        def _():
-            total[...] += product
-
-        @pl.when((h == 0) & (s == n - 1))
-        def _():
-            wait(lora)
-
-        for i in range(split):
-
-            @pl.when((h == i) & (s == n - 1))
-            def _():
-                mine = slice(i * part, (i + 1) * part)
-                added = terms[0, :, mine].astype(f32) + terms[1, :, mine].astype(f32)
-                out[...] = (total[...] + product + added).astype(bf16)
-
-    return call(
-        kernel,
-        (split, n),
+        flat, W, rest_ = refs[: len(arrays)], refs[len(arrays)], refs[len(arrays) + 1 : len(arrays) + 1 + len(rest)]
+        out, held, w, total, *sides, sem, side_sem = refs[len(arrays) + 1 + len(rest) :]
+        flat = iter(flat)
+        mine = [[next(flat) for _ in block] for block in blocks]
+        ins, lefts = [], []
+        for s, block in enumerate(mine):
+            pick = [pltpu.make_async_copy(ref, held.at[s], side_sem.at[s]) for ref in block]
+            if len(block) == 1:
+                pick[0].start()
+            else:
+                pl.when(plan[at + 2 * s + 1] == 1)(pick[0].start)
+                pl.when(plan[at + 2 * s + 1] == 0)(pick[1].start)
+            lefts.append(pick[0])
+            for i in range(fine):
+                source = pl.multiple_of(plan[at + 2 * s] * width + i * chunk, chunk)
+                to = pl.ds(s * width + i * chunk, chunk)
+                ins += fetch([(W.at[pl.ds(source, chunk)], w.at[to])], sem, s * fine + i)
+        added = []
+        if rest:
+            pairs = [(rest_[0], sides[0]), (rest_[1], sides[1].at[0]), (rest_[2].at[pl.ds(0, rows)], sides[1].at[1])]
+            added = fetch(pairs, side_sem, count)
+        for s in range(count):
+            lefts[s].wait()
+            for i in range(coarse):
+                per = fine // coarse
+                wait(ins[s * fine + i * per : s * fine + (i + 1) * per])
+                span = pl.ds(i * tile, tile)
+                product = dot(held[s, :, span], w[pl.ds(s * width + i * tile, tile)], 1, 0)
+                if s + i == 0:
+                    total[...] = product
+                else:
+                    total[...] += product
+        wait(added)
+        if rest:
+            lora = sides[1][0].astype(f32) + sides[1][1].astype(f32)
+            sides[2][...] = (total[...] + sides[0][...] + lora).astype(bf16)
+            wait(fetch([(sides[2], out)], side_sem, count + 3))
+        else:
+            wait(fetch([(total, out)], side_sem, count + 3))
+
+    scratch = [vmem(count, rows, width), vmem(count * width, columns), pltpu.VMEM((rows, columns), f32)]
+    if rest:
+        scratch += [pltpu.VMEM((rows, columns), f32), vmem(2, rows, columns), vmem(rows, columns)]
+    return call(
+        kernel,
+        (1,),
         1,
-        [HBM] * len(blocks) + [pl.BlockSpec((width, part), lambda h, s, plan: (plan[at + s], h)), HBM, HBM],
-        pl.BlockSpec((rows, part), lambda h, s, plan: (0, h)),
-        array(rows, columns),
-        [vmem(n, rows, width), pltpu.VMEM((rows, part), f32), vmem(2, rows, columns), sems(n + 2)],
-        mib=32,
-    )(plan, *far(*blocks, W, term, other))
+        [HBM] * (len(arrays) + 1 + len(rest)),
+        HBM,
+        pltpu.HBM((rows, columns), bf16 if rest else f32),
+        scratch + [sems(count * fine), sems(count + 4)],
+        mib=BIG,
+    )(plan, *far(*arrays, W, *rest))
 
 
 def chosen_of(plan, slots, ids, rank, half):
@@ -260,7 +275,7 @@
     for a in range(slots.shape[0]):
         slot = jnp.where(ids == a, slots[a], slot)
     column = lax.broadcasted_iota(jnp.int32, (ids.shape[0], half * rank), 1) // rank
-    return slot == 2 * column + (plan[1] & 1)
+    return slot == 2 * column + plan[0]
 
 
 def pieces(gathered, downs, ups, rank):
@@ -340,6 +355,7 @@
         HBM,
         array(half, 2 * rank, width),
         [vmem(*parts.shape)] + [vmem(2 * rows, width)] * 2 + [vmem(half, 2 * rank, width), sems(6)],
+        cost=GRADS,
     )(plan, slots, ids, *far(parts, *Xs, *dYs))
 
 
@@ -399,22 +415,31 @@
     chips = [list(range(k, D, 2)) for k in (0, 1)]
 
     odd = me & 1
-    place = [jnp.where(odd == 0, z, n - 1 - z), jnp.where(odd == 0, n - 1 - z, z)]
     up = [(d * n + i, d * n + i + 1) for d in range(D) for i in range(n - 1)]
     pairs = [[(a, b) if (a // n) % 2 == k else (b, a) for a, b in up] for k in (0, 1)]
 
     def along(x, k):
         return lax.ppermute(x, ("dp", "tensor"), pairs[k])
 
-    def z_of(position, k):
-        return jnp.where(odd == k, position, n - 1 - position)
-
-    plan = [z, me]
-    for s in range(1, n):
+    early = [s for s in range(1, n) if 2 * s == n] + [0]
+    late = [s for s in range(1, n) if 2 * s != n]
+    table = []
+    for i in range(n):
         for k in (0, 1):
-            plan += [jnp.clip(z_of(n - s + place[k], k), 0, n - 1), place[k] < s]
-    plan += [z_of(lax.rem(place[0] - s + n, n), 0) for s in range(n)] + [place[0] >= s for s in range(n)]
-    plan = jnp.stack([v.astype(jnp.int32) for v in plan])
+            order = sorted(range(n), key=lambda d: (-abs(d - i), d))
+            row = [k] + order
+            for s in range(1, n):
+                for way in (0, 1):
+                    p = i if k == way else n - 1 - i
+                    target = min(max(n - s + p, 0), n - 1)
+                    row += [order.index(target if k == way else n - 1 - target), int(p < s)]
+            p = i if k == 0 else n - 1 - i
+            for s in early + late:
+                source = (p - s) % n
+                row += [source if k == 0 else n - 1 - source, int(p >= s)]
+            table.append(row)
+    steps_at, forward_at = 1 + n, 1 + n + 4 * (n - 1)
+    plan = lax.dynamic_index_in_dim(jnp.asarray(table, jnp.int32), 2 * z + odd, 0, keepdims=False)
 
     arrived = [[X], [X]]
     arrived[0].append(along(X, 0))
@@ -426,39 +451,48 @@
     arrived[1].append(along(after(X, *others), 1))
 
     ids = jnp.concatenate([adapter_rows, rows_other], axis=0)
-    back = backward(after(dY, own, ids), W, n)
-
-    def onward(s, k, *earlier):
-        cost = 1 if s < n - 1 else LATE
-        payload = add_on(plan, 2 + 4 * (s - 1) + 2 * k, after(arrived[k][s], *earlier), back, cost)
+    first = n // 2
+    backs = [backward(plan, 1, first, after(dY, own, ids), W, n, 10**3)]
+
+    def onward(s, k, last):
+        cost = 10**3 if s < n - 1 else LATE
+        payload = add_on(plan, steps_at + 4 * (s - 1) + 2 * k, after(arrived[k][s], last), backs, cost)
         arrived[k].append(along(payload, k))
         return payload
 
-    payload = onward(1, 0)
-    payload = onward(1, 1, payload)
-
-    gathered = after(gathered, payload)
+    last = onward(1, 0, backs[0])
+    last = onward(1, 1, last)
+    backs.append(backward(plan, 1 + first, n - first, after(dY, last), W, n, BACK))
+
+    gathered = after(gathered, backs[1])
     part = low_parts(plan, adapter_slot, ids, (X, X_other), (dY, dY_other), gathered, rank, n)
     parts = swap(part, "tensor", None)
 
-    payload = onward(2, 0, part)
-    payload = onward(2, 1, payload)
-
-    parts = after(parts, payload)
-    mine = adapter_grads(plan, adapter_slot, ids, parts, (X, X_other), (dY, dY_other), rank, half)
-    arriving = swap(mine, "dp", chips)
-    term, back_term, send = lora_terms(plan, adapter_slot, ids, after(parts, mine), gathered, rank)
-    other = exchange(send, "dp", 1)
-
-    for s in range(3, n):
-        payload = onward(s, 0, payload, send)
-        payload = onward(s, 1, payload, send)
-
-    blocks = [after(X, payload)] + arrived[0][1:n] + [arrived[1][n - s] for s in range(1, n)]
-    projected = forward(plan, 2 + 4 * (n - 1), n, W, blocks, term, other)
+    def block(s):
+        return (arrived[0][s], arrived[1][n - s]) if s else (X,)
+
+    last = part
+    for s in range(2, n):
+        last = onward(s, 0, last)
+        if s == n // 2:
+            begun = forward(plan, forward_at, n, W, [block(s) for s in early[:-1]] + [(after(X, last),)])
+            last = begun
+        if s == 3:
+            term, back_term, send = lora_terms(plan, adapter_slot, ids, after(parts, last), gathered, rank)
+            other = exchange(send, "dp", 1)
+            last = send
+        last = onward(s, 1, last)
+        if s == 2:
+            parts = after(parts, last)
+            mine = adapter_grads(plan, adapter_slot, ids, parts, (X, X_other), (dY, dY_other), rank, half)
+            arriving = swap(mine, "dp", chips)
+            last = mine
+
+    rest = (after(begun, last), term, other)
+    projected = forward(plan, forward_at + 2 * len(early), n, W, [block(s) for s in late], rest)
 
     shrink, expand = add_up(after(arriving, projected), rank)
-    activation = finish(plan, (arrived[0][n], arrived[1][n]), back, after(back_term, expand), other)
+    activation = finish(plan, (arrived[0][n], arrived[1][n]), backs[1], after(back_term, expand), other)
     return projected, activation, shrink.T[None], expand[None]
 
 

time: 159 us -> 137 us (0.86)
  waiting for transfers between devices: 30.2 us -> 2.08 us
  Pallas kernels: 80.7 us -> 86.7 us
  local copies, waits for them, and re-layouts: 5.42 us -> 2.88 us
  starting transfers between devices: 40.6 us -> 43.1 us
    all_to_all x3, waiting for transfers between devices: 23.3 us -> 0.01 us  [swap(): return lax.all_to_all(x, axis, 0, 0, axis_index_groups=groups, tiled=True)]
    unnamed x21 -> x17, local copies, waits for them, and re-layouts: 5.18 us -> 0.83 us
    ppermute x8, waiting for transfers between devices: 5.54 us -> 1.68 us  [along(): return lax.ppermute(x, ('dp', 'tensor'), pairs[k])]
    all_to_all x3, starting transfers between devices: 11.8 us -> 15.3 us  [swap(): return lax.all_to_all(x, axis, 0, 0, axis_index_groups=groups, tiled=True)]
    pallas_call x8 -> x10, Pallas kernels: 54.7 us -> 57.9 us  [the longest x2 22.5 us: forward(): call(kernel, (1,), 1, [HBM] * (len(arrays) + 1 + len(rest)), HBM, pltpu.H...]
  transfers between devices with their start and end apart: 15 -> 15, of which waited for: 3 -> 2; matrix products, arithmetic and copies ran while one was open for 0% -> 2% of each run, Pallas kernels for 48% -> 61%
where the time goes in v3:
time: 137 us; the launch traced here: 136 us
  Pallas kernels  86.7 us (63%)
  starting transfers between devices  43.1 us (31%)
  local copies, waits for them, and re-layouts  2.88 us (2%)
  waiting for transfers between devices  2.08 us (2%)
    ppermute x8, starting transfers between devices, along(): return lax.ppermute(x, ('dp', 'tensor'), pairs[k])  26.7 us
    pallas_call x2, Pallas kernels, forward(): call(kernel, (1,), 1, [HBM] * (len(arrays) + 1 + len(rest)), HBM, pltpu.H...  22.5 us
    pallas_call x2, Pallas kernels, backward(): call(kernel, (1,), 1, [HBM, HBM], HBM, array(blocks, rows, size), [vmem(r...  19 us
    pallas_call x6, Pallas kernels, add_on(): call(kernel, (1,), 1, [HBM] * (1 + len(backs)), HBM, array(rows, width),...  16.4 us
    all_to_all x3, starting transfers between devices, swap(): return lax.all_to_all(x, axis, 0, 0, axis_index_groups=groups, tiled=True)  15.3 us
    pallas_call x1, Pallas kernels, low_parts(): call(kernel, (1,), 2, [pl.BlockSpec((2 * rows, 1), lambda i, *_: (0, 0))]...  7.22 us
    pallas_call x1, Pallas kernels, adapter_grads(): call(kernel, (1,), 2, [pl.BlockSpec((2 * rows, 1), lambda i, *_: (0, 0))]...  6.24 us
    pallas_call x1, Pallas kernels, lora_terms(): call(kernel, (1,), 2, [pl.BlockSpec((2 * rows, 1), lambda i, *_: (0, 0)),...  6.12 us
  transfers between devices with their start and end apart: 15, of which 2 were waited for; matrix products, arithmetic and copies ran while one was open for 2% of the time, Pallas kernels for 61%

profile of v3, /device:TPU:0, one launch (start us, length us, event | category | flops | bytes accessed | tf_op | source)
XLA Modules:
  0.0 135.9 jit_solution(13870823427039176510)
XLA Ops:
  0.6 0.5 collective-permute-start.2
  1.1 0.1 collective-permute-start.1
  1.2 0.4 collective-permute-start.3
  1.7 5.6 %collective-permute-start = (bf16[256,2048]{1,0:T(8,128)(2,1)}, bf16[256,2048]{1,0:T(8,128)(2,1)}, u32[]{:S(2)}, u32[]{:S(2)}) collective-permute-start(bf16[256,2048]{1,0:T(8,128)(2,1)} %X.3), channel_id=1, source_target_pairs={{0,1},{1,2},{2,3},{5,4},{6,5},{7,6},{8,9},{9,10},{10,11},{13,12},{... | collective-permute-start | bytes 3145736 | tf_op jit(solution)/shard_map/ppermute | solution.py:422
  7.2 0.0 collective-permute-done.3
  7.2 0.0 collective-permute-done.2.dY_other
  7.2 0.0 collective-permute-done.1.X_other
  7.2 1.3 collective-permute-start.4
  8.5 2.5 %shard_map.111 = bf16[4,128,2048]{2,1,0:T(8,128)(2,1)} custom-call(bf16[64,2048]{1,0:T(8,128)(2,1)} %bitcast.10, bf16[64,2048]{1,0:T(8,128)(2,1)} %bitcast.11), custom_call_target="tpu_custom_call" | custom-call | flops 1000 | bytes 1 | tf_op jit(solution)/shard_map/pallas_call | solution.py:81
  11.0 0.0 copy-start.7
  11.0 4.5 %all-to-all-start = ((bf16[4,128,2048]{2,1,0:T(8,128)(2,1)}), bf16[4,128,2048]{2,1,0:T(8,128)(2,1)}, u32[]{:S(2)}, u32[]{:S(2)}) async-start(bf16[4,128,2048]{2,1,0:T(8,128)(2,1)} %shard_map.111), calls=%async_computation | async-start | bytes 4194304 | tf_op jit(solution)/shard_map/all_to_all | solution.py:27
  15.5 1.2 dynamic-slice_bitcast_fusion.plan
  16.7 0.0 copy-done.7
  16.7 0.9 copy.14.ids
  17.6 0.0 copy-start
  17.6 9.6 %shard_map.112.refs_0_ = bf16[2,256,2048]{2,1,0:T(8,128)(2,1)} custom-call(s32[25]{0:T(128)} %dynamic-slice_bitcast_fusion.plan, bf16[256,2048]{1,0:T(8,128)(2,1)} %dY.5, bf16[8192,2048]{1,0:T(8,128)(2,1)} %refs_4_.1), custom_call_target="tpu_custom_call" | custom-call | flops 1000 | bytes 1 | tf_op jit(solution)/shard_map/pallas_call | solution.py:112
  27.2 0.0 collective-permute-done.arrived.refs_0_
  27.2 0.0 copy-done
  27.2 2.9 %shard_map.113 = bf16[256,2048]{1,0:T(8,128)(2,1)} custom-call(s32[25]{0:T(128)S(1)} %copy-done, bf16[256,2048]{1,0:T(8,128)(2,1)} %collective-permute-done.arrived.refs_0_, bf16[2,256,2048]{2,1,0:T(8,128)(2,1)} %shard_map.112.refs_0_), custom_call_target="tpu_custom_call" | custom-call | flops 1000 | bytes 1 | tf_op jit(solution)/shard_map/pallas_call | solution.py:163
  30.1 5.2 %collective-permute-start.6 = (bf16[256,2048]{1,0:T(8,128)(2,1)}, bf16[256,2048]{1,0:T(8,128)(2,1)}, u32[]{:S(2)}, u32[]{:S(2)}) collective-permute-start(bf16[256,2048]{1,0:T(8,128)(2,1)} %shard_map.113), channel_id=1, source_target_pairs={{0,1},{1,2},{2,3},{5,4},{6,5},{7,6},{8,9},{9,10},{10,11},{13,12},{... | collective-permute-start | bytes 3145736 | tf_op jit(solution)/shard_map/ppermute | solution.py:422
  35.3 0.0 collective-permute-done.4.arrived.refs_3_
  35.3 2.6 %shard_map.114 = bf16[256,2048]{1,0:T(8,128)(2,1)} custom-call(s32[25]{0:T(128)S(1)} %copy-done, bf16[256,2048]{1,0:T(8,128)(2,1)} %collective-permute-done.4.arrived.refs_3_, bf16[2,256,2048]{2,1,0:T(8,128)(2,1)} %shard_map.112.refs_0_), custom_call_target="tpu_custom_call" | custom-call | flops 1000 | bytes 1 | tf_op jit(solution)/shard_map/pallas_call | solution.py:163
  37.9 1.3 collective-permute-start.5
  39.2 9.4 %shard_map.115.refs_1_.back = bf16[2,256,2048]{2,1,0:T(8,128)(2,1)} custom-call(s32[25]{0:T(128)} %dynamic-slice_bitcast_fusion.plan, bf16[256,2048]{1,0:T(8,128)(2,1)} %dY.5, bf16[8192,2048]{1,0:T(8,128)(2,1)} %refs_4_.1), custom_call_target="tpu_custom_call" | custom-call | flops 10000000000 | bytes 1 | tf_op jit(solution)/shard_map/pallas_call | solution.py:112
  48.6 0.0 copy-start.1
  48.6 0.0 all-to-all-done.gathered
  48.6 7.2 %shard_map.116 = bf16[4,512,128]{2,1,0:T(8,128)(2,1)} custom-call(s32[25]{0:T(128)} %dynamic-slice_bitcast_fusion.plan, s32[8]{0:T(128)} %slots.5, s32[512,1]{1,0:T(8,128)} %copy.14.ids, bf16[256,2048]{1,0:T(8,128)(2,1)} %X.3, bf16[256,2048]{1,0:T(8,128)(2,1)} %collective-permute-done.1.X_other, bf16[256,2048]{1,0:T(8,128)(2,1)} %dY.5, ...), custom_call_target="tpu_custom_call" | custom-call | flops 1000 | bytes 1 | tf_op jit(solution)/shard_map/pallas_call | solution.py:309
  55.8 6.4 %all-to-all-start.1 = ((bf16[4,512,128]{2,1,0:T(8,128)(2,1)}), bf16[4,512,128]{2,1,0:T(8,128)(2,1)S(1)}, u32[]{:S(2)}, u32[]{:S(2)}) async-start(bf16[4,512,128]{2,1,0:T(8,128)(2,1)} %shard_map.116), calls=%async_computation.1 | async-start | bytes 1048576 | tf_op jit(solution)/shard_map/all_to_all | solution.py:27
  62.2 0.0 collective-permute-done.6.arrived.refs_0_
  62.2 0.0 copy-done.1
  62.3 2.9 %shard_map.117 = bf16[256,2048]{1,0:T(8,128)(2,1)} custom-call(s32[25]{0:T(128)S(1)} %copy-done.1, bf16[256,2048]{1,0:T(8,128)(2,1)} %collective-permute-done.6.arrived.refs_0_, bf16[2,256,2048]{2,1,0:T(8,128)(2,1)} %shard_map.112.refs_0_, bf16[2,256,2048]{2,1,0:T(8,128)(2,1)} %shard_map.115.refs_1_.back), custom_call_target="tpu_custom_call" | custom-call | flops 1000 | bytes 1 | tf_op jit(solution)/shard_map/pallas_call | solution.py:163
  65.2 0.0 copy-start.2
  65.2 4.9 %collective-permute-start.8 = (bf16[256,2048]{1,0:T(8,128)(2,1)}, bf16[256,2048]{1,0:T(8,128)(2,1)}, u32[]{:S(2)}, u32[]{:S(2)}) collective-permute-start(bf16[256,2048]{1,0:T(8,128)(2,1)} %shard_map.117), channel_id=1, source_target_pairs={{0,1},{1,2},{2,3},{5,4},{6,5},{7,6},{8,9},{9,10},{10,11},{13,12},{... | collective-permute-start | bytes 3145736 | tf_op jit(solution)/shard_map/ppermute | solution.py:422
  70.1 0.0 collective-permute-done.5.refs_1_.arrived
  70.1 11.7 %shard_map.118.refs_5_ = f32[256,2048]{1,0:T(8,128)} custom-call(s32[25]{0:T(128)} %dynamic-slice_bitcast_fusion.plan, bf16[256,2048]{1,0:T(8,128)(2,1)} %collective-permute-done.6.arrived.refs_0_, bf16[256,2048]{1,0:T(8,128)(2,1)} %collective-permute-done.5.refs_1_.arrived, bf16[256,2048]{1,0:T(8,128)(2,1)} %X.3, bf16[8192,2048]{1,0:T(8,128)(2,1)} %refs_4_.1), custom_call_target="tpu_custom_call" | custom-call | flops 1000 | bytes 1 | tf_op jit(solution)/shard_map/pallas_call | solution.py:261
  81.9 0.0 copy-done.2
  81.9 2.6 %shard_map.119 = bf16[256,2048]{1,0:T(8,128)(2,1)} custom-call(s32[25]{0:T(128)S(1)} %copy-done.2, bf16[256,2048]{1,0:T(8,128)(2,1)} %collective-permute-done.5.refs_1_.arrived, bf16[2,256,2048]{2,1,0:T(8,128)(2,1)} %shard_map.112.refs_0_, bf16[2,256,2048]{2,1,0:T(8,128)(2,1)} %shard_map.115.refs_1_.back), custom_call_target="tpu_custom_call" | custom-call | flops 1000 | bytes 1 | tf_op jit(solution)/shard_map/pallas_call | solution.py:163
  84.4 1.3 collective-permute-start.7
  85.7 0.0 all-to-all-done.1.parts
  85.7 0.0 copy-start.6
  85.7 0.8 copy-done.6
  86.5 6.2 %shard_map.120 = bf16[4,128,2048]{2,1,0:T(8,128)(2,1)} custom-call(s32[25]{0:T(128)} %dynamic-slice_bitcast_fusion.plan, s32[8]{0:T(128)} %slots.5, s32[512,1]{1,0:T(8,128)} %copy.14.ids, bf16[4,512,128]{2,1,0:T(8,128)(2,1)} %copy-done.6, bf16[256,2048]{1,0:T(8,128)(2,1)} %X.3, bf16[256,2048]{1,0:T(8,128)(2,1)} %collective-permute-done.1.X_other, ...), custom_call_target="tpu_custom_call" | custom-call | flops 10000000000 | bytes 1 | tf_op jit(solution)/shard_map/pallas_call | solution.py:350
  92.8 0.0 copy-start.3
  92.8 4.5 %all-to-all-start.2 = ((bf16[4,128,2048]{2,1,0:T(8,128)(2,1)}), bf16[4,128,2048]{2,1,0:T(8,128)(2,1)}, u32[]{:S(2)}, u32[]{:S(2)}) async-start(bf16[4,128,2048]{2,1,0:T(8,128)(2,1)} %shard_map.120), calls=%async_computation.2 | async-start | bytes 4194304 | tf_op jit(solution)/shard_map/all_to_all | solution.py:27
  97.3 0.0 collective-permute-done.8.arrived.refs_2_
  97.3 0.0 copy-done.3
  97.3 2.9 %shard_map.121 = bf16[256,2048]{1,0:T(8,128)(2,1)} custom-call(s32[25]{0:T(128)S(1)} %copy-done.3, bf16[256,2048]{1,0:T(8,128)(2,1)} %collective-permute-done.8.arrived.refs_2_, bf16[2,256,2048]{2,1,0:T(8,128)(2,1)} %shard_map.112.refs_0_, bf16[2,256,2048]{2,1,0:T(8,128)(2,1)} %shard_map.115.refs_1_.back), custom_call_target="tpu_custom_call" | custom-call | flops 999999995904 | bytes 1 | tf_op jit(solution)/shard_map/pallas_call | solution.py:163
  100.2 0.0 copy-start.4
  100.2 5.6 %collective-permute-start.10 = (bf16[256,2048]{1,0:T(8,128)(2,1)}, bf16[256,2048]{1,0:T(8,128)(2,1)}, u32[]{:S(2)}, u32[]{:S(2)}) collective-permute-start(bf16[256,2048]{1,0:T(8,128)(2,1)} %shard_map.121), channel_id=1, source_target_pairs={{0,1},{1,2},{2,3},{5,4},{6,5},{7,6},{8,9},{9,10},{10,11},{13,12},{... | collective-permute-start | bytes 3145736 | tf_op jit(solution)/shard_map/ppermute | solution.py:422
  105.8 6.1 %shard_map.122 = (bf16[256,2048]{1,0:T(8,128)(2,1)}, bf16[256,2048]{1,0:T(8,128)(2,1)}, bf16[512,2048]{1,0:T(8,128)(2,1)}) custom-call(s32[25]{0:T(128)} %dynamic-slice_bitcast_fusion.plan, s32[8]{0:T(128)} %slots.5, s32[512,1]{1,0:T(8,128)} %copy.14.ids, bf16[4,512,128]{2,1,0:T(8,128)(2,1)} %copy-done.6, bf16[4,128,2048]{2,1,0:T(8,128)(2,1)} %all-to-all-done.gathered), custom_call_target="tpu_custom_call" | custom-call | flops 1000 | bytes 1 | tf_op jit(solution)/shard_map/pallas_call | solution.py:378
  111.9 0.1 collective-permute-start.9
  112.0 0.0 collective-permute-done.7.arrived.refs_1_
  112.0 0.0 copy-done.4
  112.0 2.6 %shard_map.123 = bf16[256,2048]{1,0:T(8,128)(2,1)} custom-call(s32[25]{0:T(128)S(1)} %copy-done.4, bf16[256,2048]{1,0:T(8,128)(2,1)} %collective-permute-done.7.arrived.refs_1_, bf16[2,256,2048]{2,1,0:T(8,128)(2,1)} %shard_map.112.refs_0_, bf16[2,256,2048]{2,1,0:T(8,128)(2,1)} %shard_map.115.refs_1_.back), custom_call_target="tpu_custom_call" | custom-call | flops 999999995904 | bytes 1 | tf_op jit(solution)/shard_map/pallas_call | solution.py:163
  114.6 1.5 %collective-permute-start.11 = (bf16[256,2048]{1,0:T(8,128)(2,1)}, bf16[256,2048]{1,0:T(8,128)(2,1)}, u32[]{:S(2)}, u32[]{:S(2)}) collective-permute-start(bf16[256,2048]{1,0:T(8,128)(2,1)} %shard_map.123), channel_id=1, source_target_pairs={{1,0},{2,1},{3,2},{4,5},{5,6},{6,7},{9,8},{10,9},{11,10},{12,13},{... | collective-permute-start | bytes 3145736 | tf_op jit(solution)/shard_map/ppermute | solution.py:422
  116.1 0.4 collective-permute-done.9.refs_7_.other
  116.5 10.7 %shard_map.124 = bf16[256,2048]{1,0:T(8,128)(2,1)} custom-call(s32[25]{0:T(128)} %dynamic-slice_bitcast_fusion.plan, bf16[256,2048]{1,0:T(8,128)(2,1)} %collective-permute-done.arrived.refs_0_, bf16[256,2048]{1,0:T(8,128)(2,1)} %collective-permute-done.7.arrived.refs_1_, bf16[256,2048]{1,0:T(8,128)(2,1)} %collective-permute-done.8.arrived.refs_2_, ...), custom_call_target="tpu_custom_call" | custom-call | flops 1000 | bytes 1 | tf_op jit(solution)/shard_map/pallas_call | solution.py:261
  127.2 0.0 copy-start.5
  127.3 0.0 all-to-all-done.2.blocks
  127.3 2.7 %shard_map.125 = (bf16[64,2048]{1,0:T(8,128)(2,1)}, bf16[64,2048]{1,0:T(8,128)(2,1)}) custom-call(bf16[4,128,2048]{2,1,0:T(8,128)(2,1)} %all-to-all-done.2.blocks), custom_call_target="tpu_custom_call" | custom-call | flops 1000 | bytes 1 | tf_op jit(solution)/shard_map/pallas_call | solution.py:397
  129.9 0.0 collective-permute-done.10.one
  129.9 1.7 %collective-permute-done.11.two = bf16[256,2048]{1,0:T(8,128)(2,1)} collective-permute-done((bf16[256,2048]{1,0:T(8,128)(2,1)}, bf16[256,2048]{1,0:T(8,128)(2,1)}, u32[]{:S(2)}, u32[]{:S(2)}) %collective-permute-start.11) | collective-permute-done | bytes 1048608 | tf_op jit(solution)/shard_map/ppermute | solution.py:422
  131.6 0.0 copy-done.5
  131.6 4.2 %shard_map.126 = bf16[256,2048]{1,0:T(8,128)(2,1)} custom-call(s32[25]{0:T(128)S(1)} %copy-done.5, bf16[256,2048]{1,0:T(8,128)(2,1)} %collective-permute-done.10.one, bf16[256,2048]{1,0:T(8,128)(2,1)} %collective-permute-done.11.two, bf16[2,256,2048]{2,1,0:T(8,128)(2,1)} %shard_map.115.refs_1_.back, bf16[256,2048]{1,0:T(8,128)(2,1)} %get-tuple-element.46.own, ...), custom_call_target="tpu_custom_call" | custom-call | flops 1000 | bytes 1 | tf_op jit(solution)/shard_map/pallas_call | solution.py:196
  (2 shorter events, 0.0 us)
Async XLA Ops:
  0.6 6.6 %collective-permute-start.2 = (bf16[256,2048]{1,0:T(8,128)(2,1)}, bf16[256,2048]{1,0:T(8,128)(2,1)}, u32[]{:S(2)}, u32[]{:S(2)}) collective-permute-start(bf16[256,2048]{1,0:T(8,128)(2,1)} %dY.5), channel_id=1, source_target_pairs={{0,4},{4,0},{8,12},{12,8},{16,20},{20,16},{24,28},{28,24},{1,5},{5... | collective-permute-start | bytes 3145736 | tf_op jit(solution)/shard_map/ppermute | solution.py:23
  1.1 6.1 %collective-permute-start.1 = (bf16[256,2048]{1,0:T(8,128)(2,1)}, bf16[256,2048]{1,0:T(8,128)(2,1)}, u32[]{:S(2)}, u32[]{:S(2)}) collective-permute-start(bf16[256,2048]{1,0:T(8,128)(2,1)} %X.3), channel_id=1, source_target_pairs={{0,4},{4,0},{8,12},{12,8},{16,20},{20,16},{24,28},{28,24},{1,5},{5... | collective-permute-start | bytes 3145736 | tf_op jit(solution)/shard_map/ppermute | solution.py:23
  1.2 6.0 %collective-permute-start.3 = (s32[256,1]{0,1:T(1,128)}, s32[256,1]{0,1:T(1,128)S(1)}, u32[]{:S(2)}, u32[]{:S(2)}) collective-permute-start(s32[256,1]{0,1:T(1,128)} %param.13), channel_id=1, source_target_pairs={{0,4},{4,0},{8,12},{12,8},{16,20},{20,16},{24,28},{28,24},{1,5},{5... | collective-permute-start | bytes 3080 | tf_op jit(solution)/shard_map/ppermute | solution.py:23
  1.7 25.5 %collective-permute-start = (bf16[256,2048]{1,0:T(8,128)(2,1)}, bf16[256,2048]{1,0:T(8,128)(2,1)}, u32[]{:S(2)}, u32[]{:S(2)}) collective-permute-start(bf16[256,2048]{1,0:T(8,128)(2,1)} %X.3), channel_id=1, source_target_pairs={{0,1},{1,2},{2,3},{5,4},{6,5},{7,6},{8,9},{9,10},{10,11},{13,12},{... | collective-permute-start | bytes 3145736 | tf_op jit(solution)/shard_map/ppermute | solution.py:422
  7.2 28.1 %collective-permute-start.4 = (bf16[256,2048]{1,0:T(8,128)(2,1)}, bf16[256,2048]{1,0:T(8,128)(2,1)}, u32[]{:S(2)}, u32[]{:S(2)}) collective-permute-start(bf16[256,2048]{1,0:T(8,128)(2,1)} %X.3), channel_id=1, source_target_pairs={{1,0},{2,1},{3,2},{4,5},{5,6},{6,7},{9,8},{10,9},{11,10},{12,13},{... | collective-permute-start | bytes 3145736 | tf_op jit(solution)/shard_map/ppermute | solution.py:422
  11.0 5.7 %copy-start.7 = (s32[256,1]{0,1:T(1,128)S(1)}, s32[256,1]{0,1:T(1,128)}, u32[]{:S(2)}) copy-start(s32[256,1]{0,1:T(1,128)} %param.13) | copy-start | bytes 3076
  11.0 37.6 %all-to-all-start = ((bf16[4,128,2048]{2,1,0:T(8,128)(2,1)}), bf16[4,128,2048]{2,1,0:T(8,128)(2,1)}, u32[]{:S(2)}, u32[]{:S(2)}) async-start(bf16[4,128,2048]{2,1,0:T(8,128)(2,1)} %shard_map.111), calls=%async_computation | async-start | bytes 4194304 | tf_op jit(solution)/shard_map/all_to_all | solution.py:27
  17.6 9.6 %copy-start = (s32[25]{0:T(128)S(1)}, s32[25]{0:T(128)}, u32[]{:S(2)}) copy-start(s32[25]{0:T(128)} %dynamic-slice_bitcast_fusion.plan) | copy-start | bytes 304
  30.1 32.1 %collective-permute-start.6 = (bf16[256,2048]{1,0:T(8,128)(2,1)}, bf16[256,2048]{1,0:T(8,128)(2,1)}, u32[]{:S(2)}, u32[]{:S(2)}) collective-permute-start(bf16[256,2048]{1,0:T(8,128)(2,1)} %shard_map.113), channel_id=1, source_target_pairs={{0,1},{1,2},{2,3},{5,4},{6,5},{7,6},{8,9},{9,10},{10,11},{13,12},{... | collective-permute-start | bytes 3145736 | tf_op jit(solution)/shard_map/ppermute | solution.py:422
  37.9 32.3 %collective-permute-start.5 = (bf16[256,2048]{1,0:T(8,128)(2,1)}, bf16[256,2048]{1,0:T(8,128)(2,1)}, u32[]{:S(2)}, u32[]{:S(2)}) collective-permute-start(bf16[256,2048]{1,0:T(8,128)(2,1)} %shard_map.114), channel_id=1, source_target_pairs={{1,0},{2,1},{3,2},{4,5},{5,6},{6,7},{9,8},{10,9},{11,10},{12,13},{... | collective-permute-start | bytes 3145736 | tf_op jit(solution)/shard_map/ppermute | solution.py:422
  48.6 13.6 %copy-start.1 = (s32[25]{0:T(128)S(1)}, s32[25]{0:T(128)}, u32[]{:S(2)}) copy-start(s32[25]{0:T(128)} %dynamic-slice_bitcast_fusion.plan) | copy-start | bytes 304
  55.8 29.9 %all-to-all-start.1 = ((bf16[4,512,128]{2,1,0:T(8,128)(2,1)}), bf16[4,512,128]{2,1,0:T(8,128)(2,1)S(1)}, u32[]{:S(2)}, u32[]{:S(2)}) async-start(bf16[4,512,128]{2,1,0:T(8,128)(2,1)} %shard_map.116), calls=%async_computation.1 | async-start | bytes 1048576 | tf_op jit(solution)/shard_map/all_to_all | solution.py:27
  65.2 16.7 %copy-start.2 = (s32[25]{0:T(128)S(1)}, s32[25]{0:T(128)}, u32[]{:S(2)}) copy-start(s32[25]{0:T(128)} %dynamic-slice_bitcast_fusion.plan) | copy-start | bytes 304
  65.2 32.1 %collective-permute-start.8 = (bf16[256,2048]{1,0:T(8,128)(2,1)}, bf16[256,2048]{1,0:T(8,128)(2,1)}, u32[]{:S(2)}, u32[]{:S(2)}) collective-permute-start(bf16[256,2048]{1,0:T(8,128)(2,1)} %shard_map.117), channel_id=1, source_target_pairs={{0,1},{1,2},{2,3},{5,4},{6,5},{7,6},{8,9},{9,10},{10,11},{13,12},{... | collective-permute-start | bytes 3145736 | tf_op jit(solution)/shard_map/ppermute | solution.py:422
  84.4 27.6 %collective-permute-start.7 = (bf16[256,2048]{1,0:T(8,128)(2,1)}, bf16[256,2048]{1,0:T(8,128)(2,1)}, u32[]{:S(2)}, u32[]{:S(2)}) collective-permute-start(bf16[256,2048]{1,0:T(8,128)(2,1)} %shard_map.119), channel_id=1, source_target_pairs={{1,0},{2,1},{3,2},{4,5},{5,6},{6,7},{9,8},{10,9},{11,10},{12,13},{... | collective-permute-start | bytes 3145736 | tf_op jit(solution)/shard_map/ppermute | solution.py:422
  85.7 0.8 copy-start.6
  92.8 4.5 %copy-start.3 = (s32[25]{0:T(128)S(1)}, s32[25]{0:T(128)}, u32[]{:S(2)}) copy-start(s32[25]{0:T(128)} %dynamic-slice_bitcast_fusion.plan) | copy-start | bytes 304
  92.8 34.5 %all-to-all-start.2 = ((bf16[4,128,2048]{2,1,0:T(8,128)(2,1)}), bf16[4,128,2048]{2,1,0:T(8,128)(2,1)}, u32[]{:S(2)}, u32[]{:S(2)}) async-start(bf16[4,128,2048]{2,1,0:T(8,128)(2,1)} %shard_map.120), calls=%async_computation.2 | async-start | bytes 4194304 | tf_op jit(solution)/shard_map/all_to_all | solution.py:27
  100.2 11.8 %copy-start.4 = (s32[25]{0:T(128)S(1)}, s32[25]{0:T(128)}, u32[]{:S(2)}) copy-start(s32[25]{0:T(128)} %dynamic-slice_bitcast_fusion.plan) | copy-start | bytes 304
  100.2 29.7 %collective-permute-start.10 = (bf16[256,2048]{1,0:T(8,128)(2,1)}, bf16[256,2048]{1,0:T(8,128)(2,1)}, u32[]{:S(2)}, u32[]{:S(2)}) collective-permute-start(bf16[256,2048]{1,0:T(8,128)(2,1)} %shard_map.121), channel_id=1, source_target_pairs={{0,1},{1,2},{2,3},{5,4},{6,5},{7,6},{8,9},{9,10},{10,11},{13,12},{... | collective-permute-start | bytes 3145736 | tf_op jit(solution)/shard_map/ppermute | solution.py:422
  111.9 4.6 %collective-permute-start.9 = (bf16[512,2048]{1,0:T(8,128)(2,1)}, bf16[512,2048]{1,0:T(8,128)(2,1)}, u32[]{:S(2)}, u32[]{:S(2)}) collective-permute-start(bf16[512,2048]{1,0:T(8,128)(2,1)} %get-tuple-element.39), channel_id=1, source_target_pairs={{0,4},{4,0},{8,12},{12,8},{16,20},{20,16},{24,28},{28,24},{1,5},{5... | collective-permute-start | bytes 6291464 | tf_op jit(solution)/shard_map/ppermute | solution.py:23
  114.6 17.0 %collective-permute-start.11 = (bf16[256,2048]{1,0:T(8,128)(2,1)}, bf16[256,2048]{1,0:T(8,128)(2,1)}, u32[]{:S(2)}, u32[]{:S(2)}) collective-permute-start(bf16[256,2048]{1,0:T(8,128)(2,1)} %shard_map.123), channel_id=1, source_target_pairs={{1,0},{2,1},{3,2},{4,5},{5,6},{6,7},{9,8},{10,9},{11,10},{12,13},{... | collective-permute-start | bytes 3145736 | tf_op jit(solution)/shard_map/ppermute | solution.py:422
  127.2 4.4 %copy-start.5 = (s32[25]{0:T(128)S(1)}, s32[25]{0:T(128)}, u32[]{:S(2)}) copy-start(s32[25]{0:T(128)} %dynamic-slice_bitcast_fusion.plan) | copy-start | bytes 304

commit v4 on v3

v4 whole, which is shorter than its diff:
```python
import jax
import jax.numpy as jnp
from jax import lax
from jax.experimental import pallas as pl
from jax.experimental.pallas import tpu as pltpu
from jax.sharding import PartitionSpec as P

adapter_scale = 2.0
f32, bf16 = jnp.float32, jnp.bfloat16
HBM = pl.BlockSpec(memory_space=pltpu.HBM)
LATE = 10**12
GRADS = 10**10
BIG = 63
SOON = 10**10
AHEAD = 3


def dot(a, b, ca, cb):
    return lax.dot_general(a, b, (((ca,), (cb,)), ((), ())), preferred_element_type=f32)


def exchange(x, axis, offset):
    size = lax.axis_size(axis)
    return lax.ppermute(x, axis, [(i, i ^ offset) for i in range(size)])


def swap(x, axis, groups):
    return lax.all_to_all(x, axis, 0, 0, axis_index_groups=groups, tiled=True)


def after(x, *earlier):
    return lax.optimization_barrier((x,) + earlier)[0]


def call(kernel, grid, prefetch, ins, outs, shapes, scratch, mib=BIG, cost=10**3):
    return pl.pallas_call(
        kernel,
        grid_spec=pltpu.PrefetchScalarGridSpec(
            num_scalar_prefetch=prefetch, grid=grid, in_specs=ins, out_specs=outs, scratch_shapes=list(scratch)
        ),
        out_shape=shapes,
        cost_estimate=pl.CostEstimate(flops=cost, bytes_accessed=1, transcendentals=0),
        compiler_params=pltpu.CompilerParams(vmem_limit_bytes=mib * 2**20),
    )


def array(*shape):
    return pltpu.HBM(shape, bf16)


def far(*xs):
    return [pltpu.with_memory_space_constraint(x, pltpu.HBM) for x in xs]


def vmem(*shape):
    return pltpu.VMEM(shape, bf16)


def look_up(spot, table, column):
    value = jnp.int32(table[0][column])
    for i, row in enumerate(table[1:], 1):
        value = jnp.where(spot[0] == i, row[column], value)
    return value


def sems(count):
    return pltpu.SemaphoreType.DMA((count,))


def fetch(copies, sem, first=0):
    copies = [pltpu.make_async_copy(a, b, sem.at[first + i]) for i, (a, b) in enumerate(copies)]
    for c in copies:
        c.start()
    return copies


def wait(copies):
    for c in copies:
        c.wait()


def own_adapter(A, B, half):
    rank, width = B.shape

    def kernel(A, B, out, both, sem):
        wait(fetch([(A, both.at[pl.ds(0, rank)]), (B, both.at[pl.ds(rank, rank)])], sem))
        wait(fetch([(both, out.at[j]) for j in range(half)], sem, 2))

    return call(
        kernel, (1,), 0, [HBM, HBM], HBM, array(half, 2 * rank, width), [vmem(2 * rank, width), sems(2 + half)], mib=4
    )(*far(A, B))


class Stream:
    def __init__(self, W, w, starts, size, sem):
        chunk = size // 4 if size % 512 == 0 else size
        self.copies, self.started, self.done = [], 0, 0
        for b, start in enumerate(starts):
            for i in range(size // chunk):
                source = W.at[pl.ds(pl.multiple_of(start * size + i * chunk, chunk), chunk)]
                k = len(self.copies)
                self.copies.append(pltpu.make_async_copy(source, w.at[pl.ds(b * size + i * chunk, chunk)], sem.at[k]))

    def start(self, count):
        for c in self.copies[self.started : self.started + count]:
            c.start()
        self.started += count

    def take(self, parts):
        for _ in range(len(self.copies) // parts):
            self.copies[self.done].wait()
            self.done += 1
            self.start(1)


def backward_blocks(y, w, done, out, stream, size, sem):
    blocks = done.shape[0]
    coarse = 2 if size % 512 == 0 else 1
    tile = size // coarse
    outs = []
    for b in range(blocks):
        for i in range(coarse):
            stream.take(blocks * coarse)
            span = pl.ds(i * tile, tile)
            done[b, :, span] = dot(y, w[pl.ds(b * size + i * tile, tile)], 1, 1).astype(bf16)
            outs += fetch([(done.at[b, :, span], out.at[b, :, span])], sem, b * coarse + i)
    return outs


def backward(spot, table, columns, dY, W, n):
    rows, width = dY.shape
    size = W.shape[0] // n
    blocks = len(columns)

    def kernel(spot, dY, W, out, y, w, done, sem, out_sem, y_sem):
        ready = fetch([(dY, y)], y_sem)
        ins = Stream(W, w, [look_up(spot, table, c) for c in columns], size, sem)
        ins.start(AHEAD)
        wait(ready)
        wait(backward_blocks(y[...], w, done, out, ins, size, out_sem))

    return call(
        kernel,
        (1,),
        1,
        [HBM, HBM],
        HBM,
        array(blocks, rows, size),
        [vmem(rows, width), vmem(blocks * size, width), vmem(blocks, rows, size), sems(4 * blocks), sems(2 * blocks), sems(1)],
    )(spot, *far(dY, W))


def add_on(spot, table, at, arrived, backs, cost):
    rows, width = arrived.shape
    steps = 4
    size = rows // steps
    count = backs[0].shape[0]

    def kernel(spot, arrived, *refs):
        backs, (out, a, b, sem) = refs[:-4], refs[-4:]
        parts = [pl.ds(i * size, size) for i in range(steps)]
        add, block = look_up(spot, table, at + 1) == 1, look_up(spot, table, at)
        ins = [pltpu.make_async_copy(arrived.at[p], a.at[p], sem.at[i]) for i, p in enumerate(parts)]
        adds = [
            [pltpu.make_async_copy(r.at[lax.rem(block, count), p], b.at[p], sem.at[steps + i]) for r in backs]
            for i, p in enumerate(parts)
        ]
        outs = [pltpu.make_async_copy(a.at[p], out.at[p], sem.at[2 * steps + i]) for i, p in enumerate(parts)]
        for i in range(steps):
            ins[i].start()
            for k in range(len(backs)):
                pl.when(add & (lax.div(block, count) == k))(adds[i][k].start)
        for i, p in enumerate(parts):
            ins[i].wait()

            @pl.when(add)
            def _():
                adds[i][0].wait()
                a[p] = (a[p].astype(f32) + b[p].astype(f32)).astype(bf16)

            outs[i].start()
        wait(outs)

    return call(
        kernel,
        (1,),
        1,
        [HBM] * (1 + len(backs)),
        HBM,
        array(rows, width),
        [vmem(rows, width), vmem(rows, width), sems(3 * steps)],
        mib=8,
        cost=cost,
    )(spot, *far(arrived, *backs))


def finish(arrived, rest, blocks, rank):
    rows, width = rest.shape
    half = blocks.shape[0]
    steps = 4
    size = rows // steps

    def kernel(one, two, rest, blocks, out, shrink, expand, held, done, parts, total, sem, more):
        refs = [one, two, rest]
        spans = [pl.ds(i * size, size) for i in range(steps)]
        ins = [
            fetch([(r.at[p], held.at[k, p]) for k, r in enumerate(refs)], sem, i * len(refs))
            for i, p in enumerate(spans)
        ]
        gradients = fetch([(blocks, parts)], more)
        outs = []
        for i, p in enumerate(spans):
            wait(ins[i])
            done[p] = (held[0, p].astype(f32) + held[1, p].astype(f32) + held[2, p].astype(f32)).astype(bf16)
            outs += fetch([(done.at[p], out.at[p])], sem, steps * len(refs) + i)
        wait(gradients)
        total[...] = sum(parts[j].astype(f32) for j in range(half)).astype(bf16)
        outs += fetch([(total.at[pl.ds(0, rank)], shrink), (total.at[pl.ds(rank, rank)], expand)], more, 1)
        wait(outs)

    return call(
        kernel,
        (1,),
        0,
        [HBM] * 4,
        [HBM] * 3,
        [array(rows, width), array(rank, width), array(rank, width)],
        [vmem(3, rows, width), vmem(rows, width), vmem(*blocks.shape), vmem(2 * rank, width), sems(4 * steps), sems(3)],
        mib=16,
    )(*far(*arrived, rest, blocks))


def forward(spot, table, at, n, W, blocks, terms, back):
    rows, width = blocks[0][0].shape
    columns = W.shape[1]
    coarse = 2 if width % 512 == 0 else 1
    tile = width // coarse
    count = len(blocks)
    arrays = [b for block in blocks for b in block]

    def kernel(spot, *refs):
        flat, (W, term, back_term, other, back) = refs[: len(arrays)], refs[len(arrays) : len(arrays) + 5]
        out, rest, held, w, total, sides, sem, side_sem = refs[len(arrays) + 5 :]
        flat = iter(flat)
        mine = [[next(flat) for _ in block] for block in blocks]
        lefts = []
        for s, block in enumerate(mine):
            pick = [pltpu.make_async_copy(ref, held.at[s], side_sem.at[s]) for ref in block]
            if len(block) == 1:
                pick[0].start()
            else:
                one = look_up(spot, table, at + 2 * s + 1) == 1
                pl.when(one)(pick[0].start)
                pl.when(jnp.logical_not(one))(pick[1].start)
            lefts.append(pick[0])
        ins = Stream(W, w, [look_up(spot, table, at + 2 * s) for s in range(count)], width, sem)
        ins.start(AHEAD)
        own, theirs = pl.ds(0, rows), pl.ds(rows, rows)
        pairs = [term, other.at[own], back_term, other.at[theirs], back.at[back.shape[0] - 1]]
        for s in range(count):
            lefts[s].wait()
            for i in range(coarse):
                k = s * coarse + i
                ins.take(count * coarse)
                if k == count * coarse // 2:
                    added = fetch([(r, sides.at[i]) for i, r in enumerate(pairs)], side_sem, count)
                product = dot(held[s, :, pl.ds(i * tile, tile)], w[pl.ds(s * width + i * tile, tile)], 1, 0)
                if k == 0:
                    total[...] = product
                else:
                    total[...] += product
        wait(added)
        sides[0] = (total[...] + (sides[0].astype(f32) + sides[1].astype(f32))).astype(bf16)
        outs = fetch([(sides.at[0], out)], side_sem, count + 5)
        sides[2] = (sides[2].astype(f32) + sides[3].astype(f32) + sides[4].astype(f32)).astype(bf16)
        wait(outs + fetch([(sides.at[2], rest)], side_sem, count + 6))

    return call(
        kernel,
        (1,),
        1,
        [HBM] * (len(arrays) + 5),
        [HBM] * 2,
        [array(rows, columns), array(rows, width)],
        [
            vmem(count, rows, width),
            vmem(count * width, columns),
            pltpu.VMEM((rows, columns), f32),
            vmem(5, rows, columns),
            sems(4 * count),
            sems(count + 7),
        ],
    )(spot, *far(*arrays, W, *terms, back))


def chosen_of(spot, slots, ids, rank, half):
    ids = jnp.concatenate([r[...] for r in ids], axis=1)
    slot = jnp.zeros(ids.shape, jnp.int32)
    for a in range(slots.shape[0]):
        slot = jnp.where(ids == a, slots[a], slot)
    column = lax.broadcasted_iota(jnp.int32, (half * rank, ids.shape[1]), 0) // rank
    return jnp.where(slot == 2 * column + lax.rem(spot[0], 2), 1.0, 0.0).T > 0.5


def pieces(gathered, downs, ups, rank):
    half = gathered.shape[0]
    return [(gathered.at[j, pl.ds(0, rank)], downs.at[pl.ds(j * rank, rank)]) for j in range(half)] + [
        (gathered.at[j, pl.ds(rank, rank)], ups.at[pl.ds(j * rank, rank)]) for j in range(half)
    ]


def rows_of(X, dY, x, y, rows):
    top, bottom = pl.ds(0, rows), pl.ds(rows, rows)
    return [(X[0], x.at[top]), (X[1], x.at[bottom]), (dY[0], y.at[top]), (dY[1], y.at[bottom])]


def ids_spec(rows):
    return pl.BlockSpec((1, rows), lambda i, *_: (0, 0))


def low_parts(spot, slots, ids, Xs, dYs, gathered, rank, n):
    rows, width = Xs[0].shape
    half = gathered.shape[0]

    def kernel(spot, slots, id0, id1, X, X_other, dY, dY_other, gathered, out, x, y, downs, ups, part, sem):
        rights = pieces(gathered, downs, ups, rank)
        lefts = rows_of((X, X_other), (dY, dY_other), x, y, rows)
        ready = fetch(lefts[:2] + rights[:half], sem)
        more = fetch(lefts[2:] + rights[half:], sem, 2 + half)
        chosen = chosen_of(spot, slots, (id0, id1), rank, half)

        def pick(a, b):
            both = jnp.where(chosen, dot(a[...], b[...], 1, 1), 0)
            return sum(both[:, j * rank : (j + 1) * rank] for j in range(half))

        wait(ready)
        low = pick(x, downs)
        wait(more)
        part[...] = jnp.concatenate([low, pick(y, ups)], axis=1).astype(bf16)
        wait(fetch([(part, out.at[k]) for k in range(n)], sem, 4 + 2 * half))

    return call(
        kernel,
        (1,),
        2,
        [ids_spec(rows)] * 2 + [HBM] * 5,
        HBM,
        array(n, 2 * rows, 2 * rank),
        [vmem(2 * rows, width)] * 2
        + [vmem(half * rank, width)] * 2
        + [vmem(2 * rows, 2 * rank), sems(4 + 2 * half + n)],
    )(spot, slots, *ids, *far(*Xs, *dYs, gathered))


def adapters(spot, slots, ids, parts, Xs, dYs, gathered, rank):
    rows, width = Xs[0].shape
    half = gathered.shape[0]

    def kernel(spot, slots, id0, id1, parts, X, X_other, dY, dY_other, gathered, out, term, back, other, *scratch):
        held, x, y, downs, ups, grads, terms, sem, out_sem = scratch
        ins = fetch(
            [(parts, held)] + rows_of((X, X_other), (dY, dY_other), x, y, rows) + pieces(gathered, downs, ups, rank), sem
        )
        chosen = chosen_of(spot, slots, (id0, id1), rank, half)
        ins[0].wait()
        total = sum(held[k].astype(f32) for k in range(held.shape[0]))
        low, grad = total[:, :rank].astype(bf16), (adapter_scale * total[:, rank:]).astype(bf16)
        zero = jnp.zeros((), bf16)
        low, grad = [jnp.where(chosen, jnp.concatenate([v] * half, axis=1), zero) for v in (low, grad)]
        wait(ins[1:3])
        shrink = dot(grad, x[...], 0, 0).astype(bf16)
        for j in range(half):
            grads[j, :rank] = shrink[j * rank : (j + 1) * rank]
        wait(ins[3:5])
        expand = (adapter_scale * dot(low, y[...], 0, 0)).astype(bf16)
        for j in range(half):
            grads[j, rank:] = expand[j * rank : (j + 1) * rank]
        outs = fetch([(grads, out)], out_sem)
        wait(ins[5:])
        top, bottom = pl.ds(0, rows), pl.ds(rows, rows)
        terms[0] = (adapter_scale * dot(low, ups[...], 1, 0)).astype(bf16)
        outs += fetch([(terms.at[0, top], term), (terms.at[0, bottom], other.at[top])], out_sem, 1)
        terms[1] = dot(grad, downs[...], 1, 0).astype(bf16)
        outs += fetch([(terms.at[1, top], back), (terms.at[1, bottom], other.at[bottom])], out_sem, 3)
        wait(outs)

    return call(
        kernel,
        (1,),
        2,
        [ids_spec(rows)] * 2 + [HBM] * 6,
        [HBM] * 4,
        [array(half, 2 * rank, width), array(rows, width), array(rows, width), array(2 * rows, width)],
        [vmem(*parts.shape)]
        + [vmem(2 * rows, width)] * 2
        + [vmem(half * rank, width)] * 2
        + [vmem(half, 2 * rank, width), vmem(2, 2 * rows, width), sems(5 + 2 * half), sems(5)],
        cost=GRADS,
    )(spot, slots, *ids, *far(parts, *Xs, *dYs, gathered))


def body(X, dY, W, A, B, adapter_rows, adapter_slot):
    rows, width = X.shape
    rank = A.shape[2]
    n, D = lax.axis_size("tensor"), lax.axis_size("dp")
    z, me = lax.axis_index("tensor"), lax.axis_index("dp")
    half = D // 2
    chips = [list(range(k, D, 2)) for k in (0, 1)]

    odd = me & 1
    up = [(d * n + i, d * n + i + 1) for d in range(D) for i in range(n - 1)]
    pairs = [[(a, b) if (a // n) % 2 == k else (b, a) for a, b in up] for k in (0, 1)]

    def along(x, k):
        return lax.ppermute(x, ("dp", "tensor"), pairs[k])

    table = []
    for i in range(n):
        for k in (0, 1):
            order = sorted(range(n), key=lambda d: (-abs(d - i), d))
            row = [k] + order
            for s in range(1, n):
                for way in (0, 1):
                    p = i if k == way else n - 1 - i
                    target = min(max(n - s + p, 0), n - 1)
                    row += [order.index(target if k == way else n - 1 - target), int(p < s)]
            p = i if k == 0 else n - 1 - i
            for s in range(n):
                source = (p - s) % n
                row += [source if k == 0 else n - 1 - source, int(p >= s)]
            table.append(row)
    steps_at, forward_at = 1 + n, 1 + n + 4 * (n - 1)
    spot = jnp.stack([2 * z + odd])

    arrived = [[X], [X]]
    arrived[0].append(along(X, 0))

    X_other, dY_other, rows_other = (exchange(v, "dp", 1) for v in (X, dY, adapter_rows))
    others = (X_other, dY_other, rows_other)
    own = own_adapter(A[0].T, after(B, *others)[0], half)
    gathered = swap(own, "dp", chips)
    arrived[1].append(along(after(X, own), 1))

    first, second = list(range(1, n)), [n]
    backs = [backward(spot, table, first, after(dY, own, *others), W, n)]

    def onward(s, k, last):
        cost = LATE if s == n - 1 else SOON if (s, k) == (1, 1) else 10**3
        payload = add_on(spot, table, steps_at + 4 * (s - 1) + 2 * k, after(arrived[k][s], last), backs, cost)
        arrived[k].append(along(payload, k))
        return payload

    last = onward(1, 0, backs[0])
    last = onward(1, 1, last)

    ids = adapter_rows.reshape(1, rows), rows_other.reshape(1, rows)
    Xs, dYs = (X, X_other), (dY, dY_other)
    gathered = after(gathered, last)
    part = low_parts(spot, adapter_slot, ids, Xs, dYs, gathered, rank, n)
    parts = swap(part, "tensor", None)

    last = part
    for s in range(2, n):
        last = onward(s, 0, last)
        if s == 2:
            own_back = backward(spot, table, second, after(dY, last), W, n)
            last = own_back
        last = onward(s, 1, last)
        if s == 2:
            parts = after(parts, last)
            mine, term, back_term, send = adapters(spot, adapter_slot, ids, parts, Xs, dYs, gathered, rank)
            arriving = swap(mine, "dp", chips)
            other = exchange(send, "dp", 1)
            last = send

    blocks = [(after(X, last),)] + [(arrived[0][s], arrived[1][n - s]) for s in range(1, n)]
    projected, rest = forward(spot, table, forward_at, n, W, blocks, (term, back_term, other), own_back)
    activation, shrink, expand = finish((arrived[0][n], arrived[1][n]), rest, arriving, rank)
    return projected, activation, shrink.T[None], expand[None]


def solution(mesh):
    return jax.shard_map(
        body,
        mesh=mesh,
        in_specs=(
            P("dp", "tensor"),
            P("dp", "tensor"),
            P(None, "tensor"),
            P("dp", "tensor", None),
            P("dp", None, "tensor"),
            P("dp", None),
            P(),
        ),
        out_specs=(
            P("dp", "tensor"),
            P("dp", "tensor"),
            P("dp", "tensor", None),
            P("dp", None, "tensor"),
        ),
        check_vma=False,
    )
```

time: 137 us -> 124 us (0.905)
  Pallas kernels: 86.7 us -> 71.3 us
  waiting for transfers between devices: 2.08 us -> 7.53 us
  local copies, waits for them, and re-layouts: 2.88 us -> 0.81 us
    pallas_call x7 -> x4, Pallas kernels: 48.8 us -> 36.1 us  [the longest x1 17.8 us: forward(): call(kernel, (1,), 1, [HBM] * (len(arrays) + 5), [HBM] * 2, [array(rows,...]
    all_to_all x3, waiting for transfers between devices: 0.01 us -> 4.44 us  [swap(): return lax.all_to_all(x, axis, 0, 0, axis_index_groups=groups, tiled=True)]
    pallas_call x6, Pallas kernels: 16.4 us -> 13.2 us  [add_on(): call(kernel, (1,), 1, [HBM] * (1 + len(backs)), HBM, array(rows, width),...]
    ppermute x8, waiting for transfers between devices: 1.68 us -> 3.08 us  [along(): return lax.ppermute(x, ('dp', 'tensor'), pairs[k])]
  transfers between devices with their start and end apart: 15 -> 15, of which waited for: 2 -> 4; matrix products, arithmetic and copies ran while one was open for 2% -> 0% of each run, Pallas kernels for 61% -> 55%
where the time goes in v4:
time: 124 us; the launch traced here: 122 us
  Pallas kernels  71.3 us (58%)
  starting transfers between devices  41.9 us (34%)
  waiting for transfers between devices  7.53 us (6%)
    ppermute x8, starting transfers between devices, along(): return lax.ppermute(x, ('dp', 'tensor'), pairs[k])  25.9 us
    pallas_call x2, Pallas kernels, backward(): call(kernel, (1,), 1, [HBM, HBM], HBM, array(blocks, rows, size), [vmem(r...  19.6 us
    pallas_call x1, Pallas kernels, forward(): call(kernel, (1,), 1, [HBM] * (len(arrays) + 5), [HBM] * 2, [array(rows,...  17.8 us
    all_to_all x3, starting transfers between devices, swap(): return lax.all_to_all(x, axis, 0, 0, axis_index_groups=groups, tiled=True)  14.9 us
    pallas_call x6, Pallas kernels, add_on(): call(kernel, (1,), 1, [HBM] * (1 + len(backs)), HBM, array(rows, width),...  13.2 us
    pallas_call x1, Pallas kernels, adapters(): call(kernel, (1,), 2, [ids_spec(rows)] * 2 + [HBM] * 6, [HBM] * 4, [array...  7.39 us
    pallas_call x1, Pallas kernels, low_parts(): call(kernel, (1,), 2, [ids_spec(rows)] * 2 + [HBM] * 5, HBM, array(n, 2 *...  6.86 us
    all_to_all x3, waiting for transfers between devices, swap(): return lax.all_to_all(x, axis, 0, 0, axis_index_groups=groups, tiled=True)  4.44 us
  transfers between devices with their start and end apart: 15, of which 4 were waited for; matrix products, arithmetic and copies ran while one was open for 0% of the time, Pallas kernels for 55%

profile of v4, /device:TPU:0, one launch (start us, length us, event | category | flops | bytes accessed | tf_op | source)
XLA Modules:
  0.0 122.5 jit_solution(1105586266836395569)
XLA Ops:
  0.6 0.5 collective-permute-start.1
  1.1 0.1 collective-permute-start
  1.2 0.4 collective-permute-start.2
  1.7 5.6 %collective-permute-start.4 = (bf16[256,2048]{1,0:T(8,128)(2,1)}, bf16[256,2048]{1,0:T(8,128)(2,1)}, u32[]{:S(2)}, u32[]{:S(2)}) collective-permute-start(bf16[256,2048]{1,0:T(8,128)(2,1)} %refs_0_), channel_id=1, source_target_pairs={{0,1},{1,2},{2,3},{5,4},{6,5},{7,6},{8,9},{9,10},{10,11},{13,12},{... | collective-permute-start | bytes 3145736 | tf_op jit(solution)/shard_map/ppermute | solution.py:415
  7.2 0.0 collective-permute-done.2
  7.2 0.0 copy-start.1
  7.2 0.0 collective-permute-done.1.dY_other
  7.2 0.0 collective-permute-done.X_other
  7.2 2.4 %shard_map.102 = bf16[4,128,2048]{2,1,0:T(8,128)(2,1)} custom-call(bf16[64,2048]{1,0:T(8,128)(2,1)} %bitcast.11, bf16[64,2048]{1,0:T(8,128)(2,1)} %bitcast.12), custom_call_target="tpu_custom_call" | custom-call | flops 1000 | bytes 1 | tf_op jit(solution)/shard_map/pallas_call | solution.py:89
  9.7 1.3 %collective-permute-start.3 = (bf16[256,2048]{1,0:T(8,128)(2,1)}, bf16[256,2048]{1,0:T(8,128)(2,1)}, u32[]{:S(2)}, u32[]{:S(2)}) collective-permute-start(bf16[256,2048]{1,0:T(8,128)(2,1)} %refs_0_), channel_id=1, source_target_pairs={{1,0},{2,1},{3,2},{4,5},{5,6},{6,7},{9,8},{10,9},{11,10},{12,13},{... | collective-permute-start | bytes 3145736 | tf_op jit(solution)/shard_map/ppermute | solution.py:415
  11.0 0.0 copy-done.1
  11.0 4.5 %all-to-all-start = ((bf16[4,128,2048]{2,1,0:T(8,128)(2,1)}), bf16[4,128,2048]{2,1,0:T(8,128)(2,1)}, u32[]{:S(2)}, u32[]{:S(2)}) async-start(bf16[4,128,2048]{2,1,0:T(8,128)(2,1)} %shard_map.102), calls=%async_computation | async-start | bytes 4194304 | tf_op jit(solution)/shard_map/all_to_all | solution.py:28
  15.5 13.1 %shard_map.103.refs_0_ = bf16[3,256,2048]{2,1,0:T(8,128)(2,1)} custom-call(s32[1]{0:T(128)} %bitcast.spot, bf16[256,2048]{1,0:T(8,128)(2,1)} %dY.5, bf16[8192,2048]{1,0:T(8,128)(2,1)} %refs_7_.1), custom_call_target="tpu_custom_call" | custom-call | flops 1000 | bytes 1 | tf_op jit(solution)/shard_map/pallas_call | solution.py:142
  28.6 0.0 collective-permute-done.4.arrived.refs_1_
  28.6 2.4 %shard_map.104 = bf16[256,2048]{1,0:T(8,128)(2,1)} custom-call(s32[1]{0:T(128)} %bitcast.spot, bf16[256,2048]{1,0:T(8,128)(2,1)} %collective-permute-done.4.arrived.refs_1_, bf16[3,256,2048]{2,1,0:T(8,128)(2,1)} %shard_map.103.refs_0_), custom_call_target="tpu_custom_call" | custom-call | flops 1000 | bytes 1 | tf_op jit(solution)/shard_map/pallas_call | solution.py:184
  31.0 5.2 %collective-permute-start.6 = (bf16[256,2048]{1,0:T(8,128)(2,1)}, bf16[256,2048]{1,0:T(8,128)(2,1)}, u32[]{:S(2)}, u32[]{:S(2)}) collective-permute-start(bf16[256,2048]{1,0:T(8,128)(2,1)} %shard_map.104), channel_id=1, source_target_pairs={{0,1},{1,2},{2,3},{5,4},{6,5},{7,6},{8,9},{9,10},{10,11},{13,12},{... | collective-permute-start | bytes 3145736 | tf_op jit(solution)/shard_map/ppermute | solution.py:415
  36.2 0.0 collective-permute-done.3.arrived.refs_6_
  36.2 2.0 %shard_map.105 = bf16[256,2048]{1,0:T(8,128)(2,1)} custom-call(s32[1]{0:T(128)} %bitcast.spot, bf16[256,2048]{1,0:T(8,128)(2,1)} %collective-permute-done.3.arrived.refs_6_, bf16[3,256,2048]{2,1,0:T(8,128)(2,1)} %shard_map.103.refs_0_), custom_call_target="tpu_custom_call" | custom-call | flops 10000000000 | bytes 1 | tf_op jit(solution)/shard_map/pallas_call | solution.py:184
  38.2 1.3 %collective-permute-start.5 = (bf16[256,2048]{1,0:T(8,128)(2,1)}, bf16[256,2048]{1,0:T(8,128)(2,1)}, u32[]{:S(2)}, u32[]{:S(2)}) collective-permute-start(bf16[256,2048]{1,0:T(8,128)(2,1)} %shard_map.105), channel_id=1, source_target_pairs={{1,0},{2,1},{3,2},{4,5},{5,6},{6,7},{9,8},{10,9},{11,10},{12,13},{... | collective-permute-start | bytes 3145736 | tf_op jit(solution)/shard_map/ppermute | solution.py:415
  39.5 1.2 all-to-all-done.gathered
  40.7 6.9 %shard_map.106 = bf16[4,512,128]{2,1,0:T(8,128)(2,1)} custom-call(s32[1]{0:T(128)} %bitcast.spot, s32[8]{0:T(128)} %slots.3, s32[1,256]{1,0:T(1,128)} %bitcast.13, s32[1,256]{1,0:T(1,128)} %bitcast.15, bf16[256,2048]{1,0:T(8,128)(2,1)} %refs_0_, bf16[256,2048]{1,0:T(8,128)(2,1)} %collective-permute-done.X_other, bf16[256,2048]{1,0:T(8,128)(2,1)} %dY.5, ...), custom_call_target="tpu_custom_call" | custom-call | flops 1000 | bytes 1 | tf_op jit(solution)/shard_map/pallas_call | solution.py:342
  47.5 5.5 %all-to-all-start.1 = ((bf16[4,512,128]{2,1,0:T(8,128)(2,1)}), bf16[4,512,128]{2,1,0:T(8,128)(2,1)S(1)}, u32[]{:S(2)}, u32[]{:S(2)}) async-start(bf16[4,512,128]{2,1,0:T(8,128)(2,1)} %shard_map.106), calls=%async_computation.1 | async-start | bytes 1048576 | tf_op jit(solution)/shard_map/all_to_all | solution.py:28
  53.0 1.4 %collective-permute-done.6.arrived.refs_3_ = bf16[256,2048]{1,0:T(8,128)(2,1)} collective-permute-done((bf16[256,2048]{1,0:T(8,128)(2,1)}, bf16[256,2048]{1,0:T(8,128)(2,1)}, u32[]{:S(2)}, u32[]{:S(2)}) %collective-permute-start.6) | collective-permute-done | bytes 1048608 | tf_op jit(solution)/shard_map/ppermute | solution.py:415
  54.4 2.4 %shard_map.107 = bf16[256,2048]{1,0:T(8,128)(2,1)} custom-call(s32[1]{0:T(128)} %bitcast.spot, bf16[256,2048]{1,0:T(8,128)(2,1)} %collective-permute-done.6.arrived.refs_3_, bf16[3,256,2048]{2,1,0:T(8,128)(2,1)} %shard_map.103.refs_0_), custom_call_target="tpu_custom_call" | custom-call | flops 1000 | bytes 1 | tf_op jit(solution)/shard_map/pallas_call | solution.py:184
  56.8 5.4 %collective-permute-start.8 = (bf16[256,2048]{1,0:T(8,128)(2,1)}, bf16[256,2048]{1,0:T(8,128)(2,1)}, u32[]{:S(2)}, u32[]{:S(2)}) collective-permute-start(bf16[256,2048]{1,0:T(8,128)(2,1)} %shard_map.107), channel_id=1, source_target_pairs={{0,1},{1,2},{2,3},{5,4},{6,5},{7,6},{8,9},{9,10},{10,11},{13,12},{... | collective-permute-start | bytes 3145736 | tf_op jit(solution)/shard_map/ppermute | solution.py:415
  62.2 6.4 %shard_map.108.refs_11_ = bf16[1,256,2048]{2,1,0:T(8,128)(2,1)} custom-call(s32[1]{0:T(128)} %bitcast.spot, bf16[256,2048]{1,0:T(8,128)(2,1)} %dY.5, bf16[8192,2048]{1,0:T(8,128)(2,1)} %refs_7_.1), custom_call_target="tpu_custom_call" | custom-call | flops 1000 | bytes 1 | tf_op jit(solution)/shard_map/pallas_call | solution.py:142
  68.6 0.0 collective-permute-done.5.arrived.refs_4_
  68.6 2.0 %shard_map.109 = bf16[256,2048]{1,0:T(8,128)(2,1)} custom-call(s32[1]{0:T(128)} %bitcast.spot, bf16[256,2048]{1,0:T(8,128)(2,1)} %collective-permute-done.5.arrived.refs_4_, bf16[3,256,2048]{2,1,0:T(8,128)(2,1)} %shard_map.103.refs_0_), custom_call_target="tpu_custom_call" | custom-call | flops 1000 | bytes 1 | tf_op jit(solution)/shard_map/pallas_call | solution.py:184
  70.6 1.3 %collective-permute-start.7 = (bf16[256,2048]{1,0:T(8,128)(2,1)}, bf16[256,2048]{1,0:T(8,128)(2,1)}, u32[]{:S(2)}, u32[]{:S(2)}) collective-permute-start(bf16[256,2048]{1,0:T(8,128)(2,1)} %shard_map.109), channel_id=1, source_target_pairs={{1,0},{2,1},{3,2},{4,5},{5,6},{6,7},{9,8},{10,9},{11,10},{12,13},{... | collective-permute-start | bytes 3145736 | tf_op jit(solution)/shard_map/ppermute | solution.py:415
  71.9 3.3 %all-to-all-done.1.parts = bf16[4,512,128]{2,1,0:T(8,128)(2,1)S(1)} async-done(((bf16[4,512,128]{2,1,0:T(8,128)(2,1)}), bf16[4,512,128]{2,1,0:T(8,128)(2,1)S(1)}, u32[]{:S(2)}, u32[]{:S(2)}) %all-to-all-start.1) | async-done | bytes 524320 | tf_op jit(solution)/shard_map/all_to_all | solution.py:28
  75.2 0.0 copy-start
  75.2 0.8 copy-done
  76.0 7.4 %shard_map.110 = (bf16[4,128,2048]{2,1,0:T(8,128)(2,1)}, bf16[256,2048]{1,0:T(8,128)(2,1)}, bf16[256,2048]{1,0:T(8,128)(2,1)}, bf16[512,2048]{1,0:T(8,128)(2,1)}) custom-call(s32[1]{0:T(128)} %bitcast.spot, s32[8]{0:T(128)} %slots.3, s32[1,256]{1,0:T(1,128)} %bitcast.14, s32[1,256]{1,0:T(1,128)} %bitcast.16, bf16[4,512,128]{2,1,0:T(8,128)(2,1)} %copy-done, ...), custom_call_target="tpu_custom_call" | custom-call | flops 10000000000 | bytes 1 | tf_op jit(solution)/shard_map/pallas_call | solution.py:387
  83.4 5.0 %all-to-all-start.2 = ((bf16[4,128,2048]{2,1,0:T(8,128)(2,1)}), bf16[4,128,2048]{2,1,0:T(8,128)(2,1)}, u32[]{:S(2)}, u32[]{:S(2)}) async-start(bf16[4,128,2048]{2,1,0:T(8,128)(2,1)} %get-tuple-element.44), calls=%async_computation.2 | async-start | bytes 4194304 | tf_op jit(solution)/shard_map/all_to_all | solution.py:28
  88.4 0.0 collective-permute-start.9
  88.4 0.0 collective-permute-done.8.arrived.refs_5_
  88.4 2.4 %shard_map.111 = bf16[256,2048]{1,0:T(8,128)(2,1)} custom-call(s32[1]{0:T(128)} %bitcast.spot, bf16[256,2048]{1,0:T(8,128)(2,1)} %collective-permute-done.8.arrived.refs_5_, bf16[3,256,2048]{2,1,0:T(8,128)(2,1)} %shard_map.103.refs_0_), custom_call_target="tpu_custom_call" | custom-call | flops 999999995904 | bytes 1 | tf_op jit(solution)/shard_map/pallas_call | solution.py:184
  90.8 4.7 %collective-permute-start.10 = (bf16[256,2048]{1,0:T(8,128)(2,1)}, bf16[256,2048]{1,0:T(8,128)(2,1)}, u32[]{:S(2)}, u32[]{:S(2)}) collective-permute-start(bf16[256,2048]{1,0:T(8,128)(2,1)} %shard_map.111), channel_id=1, source_target_pairs={{0,1},{1,2},{2,3},{5,4},{6,5},{7,6},{8,9},{9,10},{10,11},{13,12},{... | collective-permute-start | bytes 3145736 | tf_op jit(solution)/shard_map/ppermute | solution.py:415
  95.5 0.0 collective-permute-done.7.arrived.refs_2_
  95.5 2.0 %shard_map.112 = bf16[256,2048]{1,0:T(8,128)(2,1)} custom-call(s32[1]{0:T(128)} %bitcast.spot, bf16[256,2048]{1,0:T(8,128)(2,1)} %collective-permute-done.7.arrived.refs_2_, bf16[3,256,2048]{2,1,0:T(8,128)(2,1)} %shard_map.103.refs_0_), custom_call_target="tpu_custom_call" | custom-call | flops 999999995904 | bytes 1 | tf_op jit(solution)/shard_map/pallas_call | solution.py:184
  97.5 1.3 %collective-permute-start.11 = (bf16[256,2048]{1,0:T(8,128)(2,1)}, bf16[256,2048]{1,0:T(8,128)(2,1)}, u32[]{:S(2)}, u32[]{:S(2)}) collective-permute-start(bf16[256,2048]{1,0:T(8,128)(2,1)} %shard_map.112), channel_id=1, source_target_pairs={{1,0},{2,1},{3,2},{4,5},{5,6},{6,7},{9,8},{10,9},{11,10},{12,13},{... | collective-permute-start | bytes 3145736 | tf_op jit(solution)/shard_map/ppermute | solution.py:415
  98.8 0.0 collective-permute-done.9.refs_10_
  98.8 17.8 %shard_map.113 = (bf16[256,2048]{1,0:T(8,128)(2,1)}, bf16[256,2048]{1,0:T(8,128)(2,1)}) custom-call(s32[1]{0:T(128)} %bitcast.spot, bf16[256,2048]{1,0:T(8,128)(2,1)} %refs_0_, bf16[256,2048]{1,0:T(8,128)(2,1)} %collective-permute-done.4.arrived.refs_1_, bf16[256,2048]{1,0:T(8,128)(2,1)} %collective-permute-done.7.arrived.refs_2_, ...), custom_call_target="tpu_custom_call" | custom-call | flops 1000 | bytes 1 | tf_op jit(solution)/shard_map/pallas_call | solution.py:278
  116.6 0.0 collective-permute-done.10.one
  116.6 0.0 all-to-all-done.2.blocks
  116.6 1.7 %collective-permute-done.11.two = bf16[256,2048]{1,0:T(8,128)(2,1)} collective-permute-done((bf16[256,2048]{1,0:T(8,128)(2,1)}, bf16[256,2048]{1,0:T(8,128)(2,1)}, u32[]{:S(2)}, u32[]{:S(2)}) %collective-permute-start.11) | collective-permute-done | bytes 1048608 | tf_op jit(solution)/shard_map/ppermute | solution.py:415
  118.3 4.1 %shard_map.114 = (bf16[256,2048]{1,0:T(8,128)(2,1)}, bf16[64,2048]{1,0:T(8,128)(2,1)}, bf16[64,2048]{1,0:T(8,128)(2,1)}) custom-call(bf16[256,2048]{1,0:T(8,128)(2,1)} %collective-permute-done.10.one, bf16[256,2048]{1,0:T(8,128)(2,1)} %collective-permute-done.11.two, bf16[256,2048]{1,0:T(8,128)(2,1)} %get-tuple-element.43.rest, ...), custom_call_target="tpu_custom_call" | custom-call | flops 1000 | bytes 1 | tf_op jit(solution)/shard_map/pallas_call | solution.py:221
Async XLA Ops:
  0.6 6.6 %collective-permute-start.1 = (bf16[256,2048]{1,0:T(8,128)(2,1)}, bf16[256,2048]{1,0:T(8,128)(2,1)}, u32[]{:S(2)}, u32[]{:S(2)}) collective-permute-start(bf16[256,2048]{1,0:T(8,128)(2,1)} %dY.5), channel_id=1, source_target_pairs={{0,4},{4,0},{8,12},{12,8},{16,20},{20,16},{24,28},{28,24},{1,5},{5... | collective-permute-start | bytes 3145736 | tf_op jit(solution)/shard_map/ppermute | solution.py:24
  1.1 6.1 %collective-permute-start = (bf16[256,2048]{1,0:T(8,128)(2,1)}, bf16[256,2048]{1,0:T(8,128)(2,1)}, u32[]{:S(2)}, u32[]{:S(2)}) collective-permute-start(bf16[256,2048]{1,0:T(8,128)(2,1)} %refs_0_), channel_id=1, source_target_pairs={{0,4},{4,0},{8,12},{12,8},{16,20},{20,16},{24,28},{28,24},{1,5},{5... | collective-permute-start | bytes 3145736 | tf_op jit(solution)/shard_map/ppermute | solution.py:24
  1.2 6.0 %collective-permute-start.2 = (s32[256,1]{0,1:T(1,128)}, s32[256,1]{0,1:T(1,128)S(1)}, u32[]{:S(2)}, u32[]{:S(2)}) collective-permute-start(s32[256,1]{0,1:T(1,128)} %param.12), channel_id=1, source_target_pairs={{0,4},{4,0},{8,12},{12,8},{16,20},{20,16},{24,28},{28,24},{1,5},{5... | collective-permute-start | bytes 3080 | tf_op jit(solution)/shard_map/ppermute | solution.py:24
  1.7 27.0 %collective-permute-start.4 = (bf16[256,2048]{1,0:T(8,128)(2,1)}, bf16[256,2048]{1,0:T(8,128)(2,1)}, u32[]{:S(2)}, u32[]{:S(2)}) collective-permute-start(bf16[256,2048]{1,0:T(8,128)(2,1)} %refs_0_), channel_id=1, source_target_pairs={{0,1},{1,2},{2,3},{5,4},{6,5},{7,6},{8,9},{9,10},{10,11},{13,12},{... | collective-permute-start | bytes 3145736 | tf_op jit(solution)/shard_map/ppermute | solution.py:415
  7.2 3.8 %copy-start.1 = (s32[256,1]{0,1:T(1,128)}, s32[256,1]{0,1:T(1,128)S(1)}, u32[]{:S(2)}) copy-start(s32[256,1]{0,1:T(1,128)S(1)} %collective-permute-done.2) | copy-start | bytes 3076
  9.7 26.5 %collective-permute-start.3 = (bf16[256,2048]{1,0:T(8,128)(2,1)}, bf16[256,2048]{1,0:T(8,128)(2,1)}, u32[]{:S(2)}, u32[]{:S(2)}) collective-permute-start(bf16[256,2048]{1,0:T(8,128)(2,1)} %refs_0_), channel_id=1, source_target_pairs={{1,0},{2,1},{3,2},{4,5},{5,6},{6,7},{9,8},{10,9},{11,10},{12,13},{... | collective-permute-start | bytes 3145736 | tf_op jit(solution)/shard_map/ppermute | solution.py:415
  11.0 29.7 %all-to-all-start = ((bf16[4,128,2048]{2,1,0:T(8,128)(2,1)}), bf16[4,128,2048]{2,1,0:T(8,128)(2,1)}, u32[]{:S(2)}, u32[]{:S(2)}) async-start(bf16[4,128,2048]{2,1,0:T(8,128)(2,1)} %shard_map.102), calls=%async_computation | async-start | bytes 4194304 | tf_op jit(solution)/shard_map/all_to_all | solution.py:28
  31.0 23.4 %collective-permute-start.6 = (bf16[256,2048]{1,0:T(8,128)(2,1)}, bf16[256,2048]{1,0:T(8,128)(2,1)}, u32[]{:S(2)}, u32[]{:S(2)}) collective-permute-start(bf16[256,2048]{1,0:T(8,128)(2,1)} %shard_map.104), channel_id=1, source_target_pairs={{0,1},{1,2},{2,3},{5,4},{6,5},{7,6},{8,9},{9,10},{10,11},{13,12},{... | collective-permute-start | bytes 3145736 | tf_op jit(solution)/shard_map/ppermute | solution.py:415
  38.2 30.4 %collective-permute-start.5 = (bf16[256,2048]{1,0:T(8,128)(2,1)}, bf16[256,2048]{1,0:T(8,128)(2,1)}, u32[]{:S(2)}, u32[]{:S(2)}) collective-permute-start(bf16[256,2048]{1,0:T(8,128)(2,1)} %shard_map.105), channel_id=1, source_target_pairs={{1,0},{2,1},{3,2},{4,5},{5,6},{6,7},{9,8},{10,9},{11,10},{12,13},{... | collective-permute-start | bytes 3145736 | tf_op jit(solution)/shard_map/ppermute | solution.py:415
  47.5 27.7 %all-to-all-start.1 = ((bf16[4,512,128]{2,1,0:T(8,128)(2,1)}), bf16[4,512,128]{2,1,0:T(8,128)(2,1)S(1)}, u32[]{:S(2)}, u32[]{:S(2)}) async-start(bf16[4,512,128]{2,1,0:T(8,128)(2,1)} %shard_map.106), calls=%async_computation.1 | async-start | bytes 1048576 | tf_op jit(solution)/shard_map/all_to_all | solution.py:28
  56.8 31.6 %collective-permute-start.8 = (bf16[256,2048]{1,0:T(8,128)(2,1)}, bf16[256,2048]{1,0:T(8,128)(2,1)}, u32[]{:S(2)}, u32[]{:S(2)}) collective-permute-start(bf16[256,2048]{1,0:T(8,128)(2,1)} %shard_map.107), channel_id=1, source_target_pairs={{0,1},{1,2},{2,3},{5,4},{6,5},{7,6},{8,9},{9,10},{10,11},{13,12},{... | collective-permute-start | bytes 3145736 | tf_op jit(solution)/shard_map/ppermute | solution.py:415
  70.6 24.8 %collective-permute-start.7 = (bf16[256,2048]{1,0:T(8,128)(2,1)}, bf16[256,2048]{1,0:T(8,128)(2,1)}, u32[]{:S(2)}, u32[]{:S(2)}) collective-permute-start(bf16[256,2048]{1,0:T(8,128)(2,1)} %shard_map.109), channel_id=1, source_target_pairs={{1,0},{2,1},{3,2},{4,5},{5,6},{6,7},{9,8},{10,9},{11,10},{12,13},{... | collective-permute-start | bytes 3145736 | tf_op jit(solution)/shard_map/ppermute | solution.py:415
  75.2 0.8 copy-start
  83.4 33.2 %all-to-all-start.2 = ((bf16[4,128,2048]{2,1,0:T(8,128)(2,1)}), bf16[4,128,2048]{2,1,0:T(8,128)(2,1)}, u32[]{:S(2)}, u32[]{:S(2)}) async-start(bf16[4,128,2048]{2,1,0:T(8,128)(2,1)} %get-tuple-element.44), calls=%async_computation.2 | async-start | bytes 4194304 | tf_op jit(solution)/shard_map/all_to_all | solution.py:28
  88.4 10.4 %collective-permute-start.9 = (bf16[512,2048]{1,0:T(8,128)(2,1)}, bf16[512,2048]{1,0:T(8,128)(2,1)}, u32[]{:S(2)}, u32[]{:S(2)}) collective-permute-start(bf16[512,2048]{1,0:T(8,128)(2,1)} %get-tuple-element.36), channel_id=1, source_target_pairs={{0,4},{4,0},{8,12},{12,8},{16,20},{20,16},{24,28},{28,24},{1,5},{5... | collective-permute-start | bytes 6291464 | tf_op jit(solution)/shard_map/ppermute | solution.py:24
  90.8 25.8 %collective-permute-start.10 = (bf16[256,2048]{1,0:T(8,128)(2,1)}, bf16[256,2048]{1,0:T(8,128)(2,1)}, u32[]{:S(2)}, u32[]{:S(2)}) collective-permute-start(bf16[256,2048]{1,0:T(8,128)(2,1)} %shard_map.111), channel_id=1, source_target_pairs={{0,1},{1,2},{2,3},{5,4},{6,5},{7,6},{8,9},{9,10},{10,11},{13,12},{... | collective-permute-start | bytes 3145736 | tf_op jit(solution)/shard_map/ppermute | solution.py:415
  97.5 20.8 %collective-permute-start.11 = (bf16[256,2048]{1,0:T(8,128)(2,1)}, bf16[256,2048]{1,0:T(8,128)(2,1)}, u32[]{:S(2)}, u32[]{:S(2)}) collective-permute-start(bf16[256,2048]{1,0:T(8,128)(2,1)} %shard_map.112), channel_id=1, source_target_pairs={{1,0},{2,1},{3,2},{4,5},{5,6},{6,7},{9,8},{10,9},{11,10},{12,13},{... | collective-permute-start | bytes 3145736 | tf_op jit(solution)/shard_map/ppermute | solution.py:415

commit v5 on v4

--- a/solution.py
+++ b/solution.py
@@ -12,7 +12,6 @@
 GRADS = 10**10
 BIG = 63
 SOON = 10**10
-AHEAD = 3
 
 
 def dot(a, b, ca, cb):
@@ -135,7 +134,7 @@
     def kernel(spot, dY, W, out, y, w, done, sem, out_sem, y_sem):
         ready = fetch([(dY, y)], y_sem)
         ins = Stream(W, w, [look_up(spot, table, c) for c in columns], size, sem)
-        ins.start(AHEAD)
+        ins.start(4)
         wait(ready)
         wait(backward_blocks(y[...], w, done, out, ins, size, out_sem))
 
@@ -254,7 +253,7 @@
                 pl.when(jnp.logical_not(one))(pick[1].start)
             lefts.append(pick[0])
         ins = Stream(W, w, [look_up(spot, table, at + 2 * s) for s in range(count)], width, sem)
-        ins.start(AHEAD)
+        ins.start(6)
         own, theirs = pl.ds(0, rows), pl.ds(rows, rows)
         pairs = [term, other.at[own], back_term, other.at[theirs], back.at[back.shape[0] - 1]]
         for s in range(count):
@@ -357,26 +356,25 @@
     half = gathered.shape[0]
 
     def kernel(spot, slots, id0, id1, parts, X, X_other, dY, dY_other, gathered, out, term, back, other, *scratch):
-        held, x, y, downs, ups, grads, terms, sem, out_sem = scratch
+        x, y, downs, ups, grads, terms, sem, out_sem = scratch
         ins = fetch(
-            [(parts, held)] + rows_of((X, X_other), (dY, dY_other), x, y, rows) + pieces(gathered, downs, ups, rank), sem
+            rows_of((X, X_other), (dY, dY_other), x, y, rows) + pieces(gathered, downs, ups, rank), sem
         )
         chosen = chosen_of(spot, slots, (id0, id1), rank, half)
-        ins[0].wait()
-        total = sum(held[k].astype(f32) for k in range(held.shape[0]))
+        total = sum(parts[k].astype(f32) for k in range(parts.shape[0]))
         low, grad = total[:, :rank].astype(bf16), (adapter_scale * total[:, rank:]).astype(bf16)
         zero = jnp.zeros((), bf16)
         low, grad = [jnp.where(chosen, jnp.concatenate([v] * half, axis=1), zero) for v in (low, grad)]
-        wait(ins[1:3])
+        wait(ins[:2])
         shrink = dot(grad, x[...], 0, 0).astype(bf16)
         for j in range(half):
             grads[j, :rank] = shrink[j * rank : (j + 1) * rank]
-        wait(ins[3:5])
+        wait(ins[2:4])
         expand = (adapter_scale * dot(low, y[...], 0, 0)).astype(bf16)
         for j in range(half):
             grads[j, rank:] = expand[j * rank : (j + 1) * rank]
         outs = fetch([(grads, out)], out_sem)
-        wait(ins[5:])
+        wait(ins[4:])
         top, bottom = pl.ds(0, rows), pl.ds(rows, rows)
         terms[0] = (adapter_scale * dot(low, ups[...], 1, 0)).astype(bf16)
         outs += fetch([(terms.at[0, top], term), (terms.at[0, bottom], other.at[top])], out_sem, 1)
@@ -388,15 +386,15 @@
         kernel,
         (1,),
         2,
-        [ids_spec(rows)] * 2 + [HBM] * 6,
+        [ids_spec(rows)] * 2 + [pl.BlockSpec(memory_space=pltpu.VMEM)] + [HBM] * 5,
         [HBM] * 4,
         [array(half, 2 * rank, width), array(rows, width), array(rows, width), array(2 * rows, width)],
-        [vmem(*parts.shape)]
-        + [vmem(2 * rows, width)] * 2
+        [vmem(2 * rows, width)] * 2
         + [vmem(half * rank, width)] * 2
-        + [vmem(half, 2 * rank, width), vmem(2, 2 * rows, width), sems(5 + 2 * half), sems(5)],
+        + [vmem(half, 2 * rank, width), vmem(2, 2 * rows, width), sems(4 + 2 * half), sems(5)],
+        mib=60,
         cost=GRADS,
-    )(spot, slots, *ids, *far(parts, *Xs, *dYs, gathered))
+    )(spot, slots, *ids, pltpu.with_memory_space_constraint(parts, pltpu.VMEM), *far(*Xs, *dYs, gathered))
 
 
 def body(X, dY, W, A, B, adapter_rows, adapter_slot):
@@ -441,7 +439,7 @@
     gathered = swap(own, "dp", chips)
     arrived[1].append(along(after(X, own), 1))
 
-    first, second = list(range(1, n)), [n]
+    first, second, third = list(range(1, n - 1)), [n - 1], [n]
     backs = [backward(spot, table, first, after(dY, own, *others), W, n)]
 
     def onward(s, k, last):
@@ -455,7 +453,8 @@
 
     ids = adapter_rows.reshape(1, rows), rows_other.reshape(1, rows)
     Xs, dYs = (X, X_other), (dY, dY_other)
-    gathered = after(gathered, last)
+    backs.append(backward(spot, table, second, after(dY, last), W, n))
+    gathered = after(gathered, backs[1])
     part = low_parts(spot, adapter_slot, ids, Xs, dYs, gathered, rank, n)
     parts = swap(part, "tensor", None)
 
@@ -463,7 +462,7 @@
     for s in range(2, n):
         last = onward(s, 0, last)
         if s == 2:
-            own_back = backward(spot, table, second, after(dY, last), W, n)
+            own_back = backward(spot, table, third, after(dY, last), W, n)
             last = own_back
         last = onward(s, 1, last)
         if s == 2:

time: 124 us -> 121 us (0.976)
  waiting for transfers between devices: 7.53 us -> 4.23 us
    all_to_all x3, waiting for transfers between devices: 4.44 us -> 0.01 us  [swap(): return lax.all_to_all(x, axis, 0, 0, axis_index_groups=groups, tiled=True)]
    pallas_call x2 -> x3, Pallas kernels: 19.6 us -> 22.6 us  [backward(): call(kernel, (1,), 1, [HBM, HBM], HBM, array(blocks, rows, size), [vmem(r...]
    pallas_call x1, Pallas kernels: 17.8 us -> 15.4 us  [forward(): call(kernel, (1,), 1, [HBM] * (len(arrays) + 5), [HBM] * 2, [array(rows,...]
  transfers between devices with their start and end apart: 15 -> 15, of which waited for: 4 -> 1; matrix products, arithmetic and copies ran while one was open for 0% -> 0% of each run, Pallas kernels for 55% -> 56%
where the time goes in v5:
time: 121 us; the launch traced here: 120 us
  Pallas kernels  71.9 us (59%)
  starting transfers between devices  43.1 us (36%)
  waiting for transfers between devices  4.23 us (3%)
    ppermute x8, starting transfers between devices, along(): return lax.ppermute(x, ('dp', 'tensor'), pairs[k])  26.7 us
    pallas_call x3, Pallas kernels, backward(): call(kernel, (1,), 1, [HBM, HBM], HBM, array(blocks, rows, size), [vmem(r...  22.6 us
    pallas_call x1, Pallas kernels, forward(): call(kernel, (1,), 1, [HBM] * (len(arrays) + 5), [HBM] * 2, [array(rows,...  15.4 us
    all_to_all x3, starting transfers between devices, swap(): return lax.all_to_all(x, axis, 0, 0, axis_index_groups=groups, tiled=True)  15.3 us
    pallas_call x6, Pallas kernels, add_on(): call(kernel, (1,), 1, [HBM] * (1 + len(backs)), HBM, array(rows, width),...  13.1 us
    pallas_call x1, Pallas kernels, adapters(): call(kernel, (1,), 2, [ids_spec(rows)] * 2 + [pl.BlockSpec(memory_space=p...  7.45 us
    pallas_call x1, Pallas kernels, low_parts(): call(kernel, (1,), 2, [ids_spec(rows)] * 2 + [HBM] * 5, HBM, array(n, 2 *...  6.86 us
    ppermute x8, waiting for transfers between devices, along(): return lax.ppermute(x, ('dp', 'tensor'), pairs[k])  4.21 us
  transfers between devices with their start and end apart: 15, of which 1 were waited for; matrix products, arithmetic and copies ran while one was open for 0% of the time, Pallas kernels for 56%

profile of v5, /device:TPU:0, one launch (start us, length us, event | category | flops | bytes accessed | tf_op | source)
XLA Modules:
  0.0 120.3 jit_solution(4606703117361490886)
XLA Ops:
  0.6 0.5 collective-permute-start
  1.1 0.1 collective-permute-start.1
  1.2 0.4 collective-permute-start.2
  1.7 5.5 %collective-permute-start.4 = (bf16[256,2048]{1,0:T(8,128)(2,1)}, bf16[256,2048]{1,0:T(8,128)(2,1)}, u32[]{:S(2)}, u32[]{:S(2)}) collective-permute-start(bf16[256,2048]{1,0:T(8,128)(2,1)} %refs_0_), channel_id=1, source_target_pairs={{0,1},{1,2},{2,3},{5,4},{6,5},{7,6},{8,9},{9,10},{10,11},{13,12},{... | collective-permute-start | bytes 3145736 | tf_op jit(solution)/shard_map/ppermute | solution.py:413
  7.2 0.0 collective-permute-done.2
  7.2 0.0 copy-start
  7.2 0.0 collective-permute-done.X_other
  7.2 0.0 collective-permute-done.1.dY_other
  7.2 2.4 %shard_map.102 = bf16[4,128,2048]{2,1,0:T(8,128)(2,1)} custom-call(bf16[64,2048]{1,0:T(8,128)(2,1)} %bitcast.11, bf16[64,2048]{1,0:T(8,128)(2,1)} %bitcast.12), custom_call_target="tpu_custom_call" | custom-call | flops 1000 | bytes 1 | tf_op jit(solution)/shard_map/pallas_call | solution.py:88
  9.6 1.3 %collective-permute-start.3 = (bf16[256,2048]{1,0:T(8,128)(2,1)}, bf16[256,2048]{1,0:T(8,128)(2,1)}, u32[]{:S(2)}, u32[]{:S(2)}) collective-permute-start(bf16[256,2048]{1,0:T(8,128)(2,1)} %refs_0_), channel_id=1, source_target_pairs={{1,0},{2,1},{3,2},{4,5},{5,6},{6,7},{9,8},{10,9},{11,10},{12,13},{... | collective-permute-start | bytes 3145736 | tf_op jit(solution)/shard_map/ppermute | solution.py:413
  10.9 0.0 copy-done
  10.9 4.5 %all-to-all-start = ((bf16[4,128,2048]{2,1,0:T(8,128)(2,1)}), bf16[4,128,2048]{2,1,0:T(8,128)(2,1)}, u32[]{:S(2)}, u32[]{:S(2)}) async-start(bf16[4,128,2048]{2,1,0:T(8,128)(2,1)} %shard_map.102), calls=%async_computation | async-start | bytes 4194304 | tf_op jit(solution)/shard_map/all_to_all | solution.py:27
  15.4 9.5 %shard_map.103.refs_0_ = bf16[2,256,2048]{2,1,0:T(8,128)(2,1)} custom-call(s32[1]{0:T(128)} %bitcast.spot, bf16[256,2048]{1,0:T(8,128)(2,1)} %dY.6, bf16[8192,2048]{1,0:T(8,128)(2,1)} %refs_7_.1), custom_call_target="tpu_custom_call" | custom-call | flops 1000 | bytes 1 | tf_op jit(solution)/shard_map/pallas_call | solution.py:141
  24.9 0.0 collective-permute-done.4.arrived.refs_1_
  24.9 2.4 %shard_map.104 = bf16[256,2048]{1,0:T(8,128)(2,1)} custom-call(s32[1]{0:T(128)} %bitcast.spot, bf16[256,2048]{1,0:T(8,128)(2,1)} %collective-permute-done.4.arrived.refs_1_, bf16[2,256,2048]{2,1,0:T(8,128)(2,1)} %shard_map.103.refs_0_), custom_call_target="tpu_custom_call" | custom-call | flops 1000 | bytes 1 | tf_op jit(solution)/shard_map/pallas_call | solution.py:183
  27.2 5.3 %collective-permute-start.6 = (bf16[256,2048]{1,0:T(8,128)(2,1)}, bf16[256,2048]{1,0:T(8,128)(2,1)}, u32[]{:S(2)}, u32[]{:S(2)}) collective-permute-start(bf16[256,2048]{1,0:T(8,128)(2,1)} %shard_map.104), channel_id=1, source_target_pairs={{0,1},{1,2},{2,3},{5,4},{6,5},{7,6},{8,9},{9,10},{10,11},{13,12},{... | collective-permute-start | bytes 3145736 | tf_op jit(solution)/shard_map/ppermute | solution.py:413
  32.5 0.0 collective-permute-done.3.arrived.refs_6_
  32.6 2.0 %shard_map.105 = bf16[256,2048]{1,0:T(8,128)(2,1)} custom-call(s32[1]{0:T(128)} %bitcast.spot, bf16[256,2048]{1,0:T(8,128)(2,1)} %collective-permute-done.3.arrived.refs_6_, bf16[2,256,2048]{2,1,0:T(8,128)(2,1)} %shard_map.103.refs_0_), custom_call_target="tpu_custom_call" | custom-call | flops 10000000000 | bytes 1 | tf_op jit(solution)/shard_map/pallas_call | solution.py:183
  34.6 1.3 %collective-permute-start.5 = (bf16[256,2048]{1,0:T(8,128)(2,1)}, bf16[256,2048]{1,0:T(8,128)(2,1)}, u32[]{:S(2)}, u32[]{:S(2)}) collective-permute-start(bf16[256,2048]{1,0:T(8,128)(2,1)} %shard_map.105), channel_id=1, source_target_pairs={{1,0},{2,1},{3,2},{4,5},{5,6},{6,7},{9,8},{10,9},{11,10},{12,13},{... | collective-permute-start | bytes 3145736 | tf_op jit(solution)/shard_map/ppermute | solution.py:413
  35.9 6.6 %shard_map.106.refs_1_ = bf16[1,256,2048]{2,1,0:T(8,128)(2,1)} custom-call(s32[1]{0:T(128)} %bitcast.spot, bf16[256,2048]{1,0:T(8,128)(2,1)} %dY.6, bf16[8192,2048]{1,0:T(8,128)(2,1)} %refs_7_.1), custom_call_target="tpu_custom_call" | custom-call | flops 1000 | bytes 1 | tf_op jit(solution)/shard_map/pallas_call | solution.py:141
  42.5 0.0 all-to-all-done.gathered
  42.5 6.9 %shard_map.107 = bf16[4,512,128]{2,1,0:T(8,128)(2,1)} custom-call(s32[1]{0:T(128)} %bitcast.spot, s32[8]{0:T(128)} %slots.3, s32[1,256]{1,0:T(1,128)} %bitcast.13, s32[1,256]{1,0:T(1,128)} %bitcast.15, bf16[256,2048]{1,0:T(8,128)(2,1)} %refs_0_, bf16[256,2048]{1,0:T(8,128)(2,1)} %collective-permute-done.X_other, bf16[256,2048]{1,0:T(8,128)(2,1)} %dY.6, ...), custom_call_target="tpu_custom_call" | custom-call | flops 1000 | bytes 1 | tf_op jit(solution)/shard_map/pallas_call | solution.py:341
  49.3 6.4 %all-to-all-start.1 = ((bf16[4,512,128]{2,1,0:T(8,128)(2,1)}), bf16[4,512,128]{2,1,0:T(8,128)(2,1)S(1)}, u32[]{:S(2)}, u32[]{:S(2)}) async-start(bf16[4,512,128]{2,1,0:T(8,128)(2,1)} %shard_map.107), calls=%async_computation.1 | async-start | bytes 1048576 | tf_op jit(solution)/shard_map/all_to_all | solution.py:27
  55.8 0.0 collective-permute-done.6.arrived.refs_3_
  55.8 2.4 %shard_map.108 = bf16[256,2048]{1,0:T(8,128)(2,1)} custom-call(s32[1]{0:T(128)} %bitcast.spot, bf16[256,2048]{1,0:T(8,128)(2,1)} %collective-permute-done.6.arrived.refs_3_, bf16[2,256,2048]{2,1,0:T(8,128)(2,1)} %shard_map.103.refs_0_, bf16[1,256,2048]{2,1,0:T(8,128)(2,1)} %shard_map.106.refs_1_), custom_call_target="tpu_custom_call" | custom-call | flops 1000 | bytes 1 | tf_op jit(solution)/shard_map/pallas_call | solution.py:183
  58.1 4.9 %collective-permute-start.8 = (bf16[256,2048]{1,0:T(8,128)(2,1)}, bf16[256,2048]{1,0:T(8,128)(2,1)}, u32[]{:S(2)}, u32[]{:S(2)}) collective-permute-start(bf16[256,2048]{1,0:T(8,128)(2,1)} %shard_map.108), channel_id=1, source_target_pairs={{0,1},{1,2},{2,3},{5,4},{6,5},{7,6},{8,9},{9,10},{10,11},{13,12},{... | collective-permute-start | bytes 3145736 | tf_op jit(solution)/shard_map/ppermute | solution.py:413
  63.0 6.6 %shard_map.109.refs_11_ = bf16[1,256,2048]{2,1,0:T(8,128)(2,1)} custom-call(s32[1]{0:T(128)} %bitcast.spot, bf16[256,2048]{1,0:T(8,128)(2,1)} %dY.6, bf16[8192,2048]{1,0:T(8,128)(2,1)} %refs_7_.1), custom_call_target="tpu_custom_call" | custom-call | flops 1000 | bytes 1 | tf_op jit(solution)/shard_map/pallas_call | solution.py:141
  69.6 0.0 collective-permute-done.5.arrived.refs_4_
  69.6 2.0 %shard_map.110 = bf16[256,2048]{1,0:T(8,128)(2,1)} custom-call(s32[1]{0:T(128)} %bitcast.spot, bf16[256,2048]{1,0:T(8,128)(2,1)} %collective-permute-done.5.arrived.refs_4_, bf16[2,256,2048]{2,1,0:T(8,128)(2,1)} %shard_map.103.refs_0_, bf16[1,256,2048]{2,1,0:T(8,128)(2,1)} %shard_map.106.refs_1_), custom_call_target="tpu_custom_call" | custom-call | flops 1000 | bytes 1 | tf_op jit(solution)/shard_map/pallas_call | solution.py:183
  71.7 1.3 %collective-permute-start.7 = (bf16[256,2048]{1,0:T(8,128)(2,1)}, bf16[256,2048]{1,0:T(8,128)(2,1)}, u32[]{:S(2)}, u32[]{:S(2)}) collective-permute-start(bf16[256,2048]{1,0:T(8,128)(2,1)} %shard_map.110), channel_id=1, source_target_pairs={{1,0},{2,1},{3,2},{4,5},{5,6},{6,7},{9,8},{10,9},{11,10},{12,13},{... | collective-permute-start | bytes 3145736 | tf_op jit(solution)/shard_map/ppermute | solution.py:413
  73.0 0.0 all-to-all-done.1.parts
  73.0 7.4 %shard_map.111 = (bf16[4,128,2048]{2,1,0:T(8,128)(2,1)}, bf16[256,2048]{1,0:T(8,128)(2,1)}, bf16[256,2048]{1,0:T(8,128)(2,1)}, bf16[512,2048]{1,0:T(8,128)(2,1)}) custom-call(s32[1]{0:T(128)} %bitcast.spot, s32[8]{0:T(128)} %slots.3, s32[1,256]{1,0:T(1,128)} %bitcast.14, s32[1,256]{1,0:T(1,128)} %bitcast.16, bf16[4,512,128]{2,1,0:T(8,128)(2,1)S(1)} %all-to-all-done.1.parts, ...), custom_call_target="tpu_custom_call" | custom-call | flops 10000000000 | bytes 1 | tf_op jit(solution)/shard_map/pallas_call | solution.py:385
  80.4 4.5 %all-to-all-start.2 = ((bf16[4,128,2048]{2,1,0:T(8,128)(2,1)}), bf16[4,128,2048]{2,1,0:T(8,128)(2,1)}, u32[]{:S(2)}, u32[]{:S(2)}) async-start(bf16[4,128,2048]{2,1,0:T(8,128)(2,1)} %get-tuple-element.46), calls=%async_computation.2 | async-start | bytes 4194304 | tf_op jit(solution)/shard_map/all_to_all | solution.py:27
  84.9 0.1 collective-permute-start.9
  85.0 0.0 collective-permute-done.8.arrived.refs_5_
  85.0 2.4 %shard_map.112 = bf16[256,2048]{1,0:T(8,128)(2,1)} custom-call(s32[1]{0:T(128)} %bitcast.spot, bf16[256,2048]{1,0:T(8,128)(2,1)} %collective-permute-done.8.arrived.refs_5_, bf16[2,256,2048]{2,1,0:T(8,128)(2,1)} %shard_map.103.refs_0_, bf16[1,256,2048]{2,1,0:T(8,128)(2,1)} %shard_map.106.refs_1_), custom_call_target="tpu_custom_call" | custom-call | flops 999999995904 | bytes 1 | tf_op jit(solution)/shard_map/pallas_call | solution.py:183
  87.4 5.5 %collective-permute-start.10 = (bf16[256,2048]{1,0:T(8,128)(2,1)}, bf16[256,2048]{1,0:T(8,128)(2,1)}, u32[]{:S(2)}, u32[]{:S(2)}) collective-permute-start(bf16[256,2048]{1,0:T(8,128)(2,1)} %shard_map.112), channel_id=1, source_target_pairs={{0,1},{1,2},{2,3},{5,4},{6,5},{7,6},{8,9},{9,10},{10,11},{13,12},{... | collective-permute-start | bytes 3145736 | tf_op jit(solution)/shard_map/ppermute | solution.py:413
  92.9 0.0 collective-permute-done.7.arrived.refs_2_
  92.9 2.0 %shard_map.113 = bf16[256,2048]{1,0:T(8,128)(2,1)} custom-call(s32[1]{0:T(128)} %bitcast.spot, bf16[256,2048]{1,0:T(8,128)(2,1)} %collective-permute-done.7.arrived.refs_2_, bf16[2,256,2048]{2,1,0:T(8,128)(2,1)} %shard_map.103.refs_0_, bf16[1,256,2048]{2,1,0:T(8,128)(2,1)} %shard_map.106.refs_1_), custom_call_target="tpu_custom_call" | custom-call | flops 999999995904 | bytes 1 | tf_op jit(solution)/shard_map/pallas_call | solution.py:183
  94.9 1.5 %collective-permute-start.11 = (bf16[256,2048]{1,0:T(8,128)(2,1)}, bf16[256,2048]{1,0:T(8,128)(2,1)}, u32[]{:S(2)}, u32[]{:S(2)}) collective-permute-start(bf16[256,2048]{1,0:T(8,128)(2,1)} %shard_map.113), channel_id=1, source_target_pairs={{1,0},{2,1},{3,2},{4,5},{5,6},{6,7},{9,8},{10,9},{11,10},{12,13},{... | collective-permute-start | bytes 3145736 | tf_op jit(solution)/shard_map/ppermute | solution.py:413
  96.5 0.0 collective-permute-done.9.refs_10_
  96.5 15.4 %shard_map.114 = (bf16[256,2048]{1,0:T(8,128)(2,1)}, bf16[256,2048]{1,0:T(8,128)(2,1)}) custom-call(s32[1]{0:T(128)} %bitcast.spot, bf16[256,2048]{1,0:T(8,128)(2,1)} %refs_0_, bf16[256,2048]{1,0:T(8,128)(2,1)} %collective-permute-done.4.arrived.refs_1_, bf16[256,2048]{1,0:T(8,128)(2,1)} %collective-permute-done.7.arrived.refs_2_, ...), custom_call_target="tpu_custom_call" | custom-call | flops 1000 | bytes 1 | tf_op jit(solution)/shard_map/pallas_call | solution.py:277
  111.8 0.0 collective-permute-done.10.one
  111.9 0.0 all-to-all-done.2.blocks
  111.9 4.2 %collective-permute-done.11.two = bf16[256,2048]{1,0:T(8,128)(2,1)} collective-permute-done((bf16[256,2048]{1,0:T(8,128)(2,1)}, bf16[256,2048]{1,0:T(8,128)(2,1)}, u32[]{:S(2)}, u32[]{:S(2)}) %collective-permute-start.11) | collective-permute-done | bytes 1048608 | tf_op jit(solution)/shard_map/ppermute | solution.py:413
  116.0 4.1 %shard_map.115 = (bf16[256,2048]{1,0:T(8,128)(2,1)}, bf16[64,2048]{1,0:T(8,128)(2,1)}, bf16[64,2048]{1,0:T(8,128)(2,1)}) custom-call(bf16[256,2048]{1,0:T(8,128)(2,1)} %collective-permute-done.10.one, bf16[256,2048]{1,0:T(8,128)(2,1)} %collective-permute-done.11.two, bf16[256,2048]{1,0:T(8,128)(2,1)} %get-tuple-element.45.rest, ...), custom_call_target="tpu_custom_call" | custom-call | flops 1000 | bytes 1 | tf_op jit(solution)/shard_map/pallas_call | solution.py:220
Async XLA Ops:
  0.6 6.6 %collective-permute-start = (bf16[256,2048]{1,0:T(8,128)(2,1)}, bf16[256,2048]{1,0:T(8,128)(2,1)}, u32[]{:S(2)}, u32[]{:S(2)}) collective-permute-start(bf16[256,2048]{1,0:T(8,128)(2,1)} %refs_0_), channel_id=1, source_target_pairs={{0,4},{4,0},{8,12},{12,8},{16,20},{20,16},{24,28},{28,24},{1,5},{5... | collective-permute-start | bytes 3145736 | tf_op jit(solution)/shard_map/ppermute | solution.py:23
  1.1 6.0 %collective-permute-start.1 = (bf16[256,2048]{1,0:T(8,128)(2,1)}, bf16[256,2048]{1,0:T(8,128)(2,1)}, u32[]{:S(2)}, u32[]{:S(2)}) collective-permute-start(bf16[256,2048]{1,0:T(8,128)(2,1)} %dY.6), channel_id=1, source_target_pairs={{0,4},{4,0},{8,12},{12,8},{16,20},{20,16},{24,28},{28,24},{1,5},{5... | collective-permute-start | bytes 3145736 | tf_op jit(solution)/shard_map/ppermute | solution.py:23
  1.2 6.0 %collective-permute-start.2 = (s32[256,1]{0,1:T(1,128)}, s32[256,1]{0,1:T(1,128)S(1)}, u32[]{:S(2)}, u32[]{:S(2)}) collective-permute-start(s32[256,1]{0,1:T(1,128)} %param.12), channel_id=1, source_target_pairs={{0,4},{4,0},{8,12},{12,8},{16,20},{20,16},{24,28},{28,24},{1,5},{5... | collective-permute-start | bytes 3080 | tf_op jit(solution)/shard_map/ppermute | solution.py:23
  1.7 23.2 %collective-permute-start.4 = (bf16[256,2048]{1,0:T(8,128)(2,1)}, bf16[256,2048]{1,0:T(8,128)(2,1)}, u32[]{:S(2)}, u32[]{:S(2)}) collective-permute-start(bf16[256,2048]{1,0:T(8,128)(2,1)} %refs_0_), channel_id=1, source_target_pairs={{0,1},{1,2},{2,3},{5,4},{6,5},{7,6},{8,9},{9,10},{10,11},{13,12},{... | collective-permute-start | bytes 3145736 | tf_op jit(solution)/shard_map/ppermute | solution.py:413
  7.2 3.7 %copy-start = (s32[256,1]{0,1:T(1,128)}, s32[256,1]{0,1:T(1,128)S(1)}, u32[]{:S(2)}) copy-start(s32[256,1]{0,1:T(1,128)S(1)} %collective-permute-done.2) | copy-start | bytes 3076
  9.6 23.0 %collective-permute-start.3 = (bf16[256,2048]{1,0:T(8,128)(2,1)}, bf16[256,2048]{1,0:T(8,128)(2,1)}, u32[]{:S(2)}, u32[]{:S(2)}) collective-permute-start(bf16[256,2048]{1,0:T(8,128)(2,1)} %refs_0_), channel_id=1, source_target_pairs={{1,0},{2,1},{3,2},{4,5},{5,6},{6,7},{9,8},{10,9},{11,10},{12,13},{... | collective-permute-start | bytes 3145736 | tf_op jit(solution)/shard_map/ppermute | solution.py:413
  10.9 31.6 %all-to-all-start = ((bf16[4,128,2048]{2,1,0:T(8,128)(2,1)}), bf16[4,128,2048]{2,1,0:T(8,128)(2,1)}, u32[]{:S(2)}, u32[]{:S(2)}) async-start(bf16[4,128,2048]{2,1,0:T(8,128)(2,1)} %shard_map.102), calls=%async_computation | async-start | bytes 4194304 | tf_op jit(solution)/shard_map/all_to_all | solution.py:27
  27.2 28.5 %collective-permute-start.6 = (bf16[256,2048]{1,0:T(8,128)(2,1)}, bf16[256,2048]{1,0:T(8,128)(2,1)}, u32[]{:S(2)}, u32[]{:S(2)}) collective-permute-start(bf16[256,2048]{1,0:T(8,128)(2,1)} %shard_map.104), channel_id=1, source_target_pairs={{0,1},{1,2},{2,3},{5,4},{6,5},{7,6},{8,9},{9,10},{10,11},{13,12},{... | collective-permute-start | bytes 3145736 | tf_op jit(solution)/shard_map/ppermute | solution.py:413
  34.6 35.1 %collective-permute-start.5 = (bf16[256,2048]{1,0:T(8,128)(2,1)}, bf16[256,2048]{1,0:T(8,128)(2,1)}, u32[]{:S(2)}, u32[]{:S(2)}) collective-permute-start(bf16[256,2048]{1,0:T(8,128)(2,1)} %shard_map.105), channel_id=1, source_target_pairs={{1,0},{2,1},{3,2},{4,5},{5,6},{6,7},{9,8},{10,9},{11,10},{12,13},{... | collective-permute-start | bytes 3145736 | tf_op jit(solution)/shard_map/ppermute | solution.py:413
  49.3 23.6 %all-to-all-start.1 = ((bf16[4,512,128]{2,1,0:T(8,128)(2,1)}), bf16[4,512,128]{2,1,0:T(8,128)(2,1)S(1)}, u32[]{:S(2)}, u32[]{:S(2)}) async-start(bf16[4,512,128]{2,1,0:T(8,128)(2,1)} %shard_map.107), calls=%async_computation.1 | async-start | bytes 1048576 | tf_op jit(solution)/shard_map/all_to_all | solution.py:27
  58.1 26.8 %collective-permute-start.8 = (bf16[256,2048]{1,0:T(8,128)(2,1)}, bf16[256,2048]{1,0:T(8,128)(2,1)}, u32[]{:S(2)}, u32[]{:S(2)}) collective-permute-start(bf16[256,2048]{1,0:T(8,128)(2,1)} %shard_map.108), channel_id=1, source_target_pairs={{0,1},{1,2},{2,3},{5,4},{6,5},{7,6},{8,9},{9,10},{10,11},{13,12},{... | collective-permute-start | bytes 3145736 | tf_op jit(solution)/shard_map/ppermute | solution.py:413
  71.7 21.2 %collective-permute-start.7 = (bf16[256,2048]{1,0:T(8,128)(2,1)}, bf16[256,2048]{1,0:T(8,128)(2,1)}, u32[]{:S(2)}, u32[]{:S(2)}) collective-permute-start(bf16[256,2048]{1,0:T(8,128)(2,1)} %shard_map.110), channel_id=1, source_target_pairs={{1,0},{2,1},{3,2},{4,5},{5,6},{6,7},{9,8},{10,9},{11,10},{12,13},{... | collective-permute-start | bytes 3145736 | tf_op jit(solution)/shard_map/ppermute | solution.py:413
  80.4 31.4 %all-to-all-start.2 = ((bf16[4,128,2048]{2,1,0:T(8,128)(2,1)}), bf16[4,128,2048]{2,1,0:T(8,128)(2,1)}, u32[]{:S(2)}, u32[]{:S(2)}) async-start(bf16[4,128,2048]{2,1,0:T(8,128)(2,1)} %get-tuple-element.46), calls=%async_computation.2 | async-start | bytes 4194304 | tf_op jit(solution)/shard_map/all_to_all | solution.py:27
  84.9 11.6 %collective-permute-start.9 = (bf16[512,2048]{1,0:T(8,128)(2,1)}, bf16[512,2048]{1,0:T(8,128)(2,1)}, u32[]{:S(2)}, u32[]{:S(2)}) collective-permute-start(bf16[512,2048]{1,0:T(8,128)(2,1)} %get-tuple-element.38), channel_id=1, source_target_pairs={{0,4},{4,0},{8,12},{12,8},{16,20},{20,16},{24,28},{28,24},{1,5},{5... | collective-permute-start | bytes 6291464 | tf_op jit(solution)/shard_map/ppermute | solution.py:23
  87.4 24.5 %collective-permute-start.10 = (bf16[256,2048]{1,0:T(8,128)(2,1)}, bf16[256,2048]{1,0:T(8,128)(2,1)}, u32[]{:S(2)}, u32[]{:S(2)}) collective-permute-start(bf16[256,2048]{1,0:T(8,128)(2,1)} %shard_map.112), channel_id=1, source_target_pairs={{0,1},{1,2},{2,3},{5,4},{6,5},{7,6},{8,9},{9,10},{10,11},{13,12},{... | collective-permute-start | bytes 3145736 | tf_op jit(solution)/shard_map/ppermute | solution.py:413
  94.9 21.1 %collective-permute-start.11 = (bf16[256,2048]{1,0:T(8,128)(2,1)}, bf16[256,2048]{1,0:T(8,128)(2,1)}, u32[]{:S(2)}, u32[]{:S(2)}) collective-permute-start(bf16[256,2048]{1,0:T(8,128)(2,1)} %shard_map.113), channel_id=1, source_target_pairs={{1,0},{2,1},{3,2},{4,5},{5,6},{6,7},{9,8},{10,9},{11,10},{12,13},{... | collective-permute-start | bytes 3145736 | tf_op jit(solution)/shard_map/ppermute | solution.py:413

commit v6 on v5

--- a/solution.py
+++ b/solution.py
@@ -112,9 +112,8 @@
             self.start(1)
 
 
-def backward_blocks(y, w, done, out, stream, size, sem):
+def backward_blocks(y, w, done, out, stream, size, coarse, sem):
     blocks = done.shape[0]
-    coarse = 2 if size % 512 == 0 else 1
     tile = size // coarse
     outs = []
     for b in range(blocks):
@@ -130,13 +129,14 @@
     rows, width = dY.shape
     size = W.shape[0] // n
     blocks = len(columns)
+    coarse = 1 if size % 512 else 2 if blocks > 1 else 4
 
     def kernel(spot, dY, W, out, y, w, done, sem, out_sem, y_sem):
         ready = fetch([(dY, y)], y_sem)
         ins = Stream(W, w, [look_up(spot, table, c) for c in columns], size, sem)
-        ins.start(4)
+        ins.start(4 if blocks > 1 else 2)
         wait(ready)
-        wait(backward_blocks(y[...], w, done, out, ins, size, out_sem))
+        wait(backward_blocks(y[...], w, done, out, ins, size, coarse, out_sem))
 
     return call(
         kernel,
@@ -145,7 +145,7 @@
         [HBM, HBM],
         HBM,
         array(blocks, rows, size),
-        [vmem(rows, width), vmem(blocks * size, width), vmem(blocks, rows, size), sems(4 * blocks), sems(2 * blocks), sems(1)],
+        [vmem(rows, width), vmem(blocks * size, width), vmem(blocks, rows, size), sems(4 * blocks), sems(4 * blocks), sems(1)],
     )(spot, *far(dY, W))
 
 
@@ -193,40 +193,55 @@
     )(spot, *far(arrived, *backs))
 
 
-def finish(arrived, rest, blocks, rank):
+def finish(arrived, rest):
     rows, width = rest.shape
-    half = blocks.shape[0]
     steps = 4
     size = rows // steps
 
-    def kernel(one, two, rest, blocks, out, shrink, expand, held, done, parts, total, sem, more):
+    def kernel(one, two, rest, out, held, done, sem):
         refs = [one, two, rest]
         spans = [pl.ds(i * size, size) for i in range(steps)]
         ins = [
             fetch([(r.at[p], held.at[k, p]) for k, r in enumerate(refs)], sem, i * len(refs))
             for i, p in enumerate(spans)
         ]
-        gradients = fetch([(blocks, parts)], more)
         outs = []
         for i, p in enumerate(spans):
             wait(ins[i])
             done[p] = (held[0, p].astype(f32) + held[1, p].astype(f32) + held[2, p].astype(f32)).astype(bf16)
             outs += fetch([(done.at[p], out.at[p])], sem, steps * len(refs) + i)
-        wait(gradients)
+        wait(outs)
+
+    return call(
+        kernel,
+        (1,),
+        0,
+        [HBM] * 3,
+        HBM,
+        array(rows, width),
+        [vmem(3, rows, width), vmem(rows, width), sems(4 * steps)],
+        mib=16,
+    )(*far(*arrived, rest))
+
+
+def add_up(blocks, rank):
+    half, _, width = blocks.shape
+
+    def kernel(blocks, shrink, expand, parts, total, sem):
+        wait(fetch([(blocks, parts)], sem))
         total[...] = sum(parts[j].astype(f32) for j in range(half)).astype(bf16)
-        outs += fetch([(total.at[pl.ds(0, rank)], shrink), (total.at[pl.ds(rank, rank)], expand)], more, 1)
-        wait(outs)
+        wait(fetch([(total.at[pl.ds(0, rank)], shrink), (total.at[pl.ds(rank, rank)], expand)], sem, 1))
 
     return call(
         kernel,
         (1,),
         0,
-        [HBM] * 4,
-        [HBM] * 3,
-        [array(rows, width), array(rank, width), array(rank, width)],
-        [vmem(3, rows, width), vmem(rows, width), vmem(*blocks.shape), vmem(2 * rank, width), sems(4 * steps), sems(3)],
+        [HBM],
+        [HBM] * 2,
+        [array(rank, width)] * 2,
+        [vmem(*blocks.shape), vmem(2 * rank, width), sems(3)],
         mib=16,
-    )(*far(*arrived, rest, blocks))
+    )(*far(blocks))
 
 
 def forward(spot, table, at, n, W, blocks, terms, back):
@@ -474,7 +489,8 @@
 
     blocks = [(after(X, last),)] + [(arrived[0][s], arrived[1][n - s]) for s in range(1, n)]
     projected, rest = forward(spot, table, forward_at, n, W, blocks, (term, back_term, other), own_back)
-    activation, shrink, expand = finish((arrived[0][n], arrived[1][n]), rest, arriving, rank)
+    shrink, expand = add_up(after(arriving, projected), rank)
+    activation = finish((arrived[0][n], arrived[1][n]), after(rest, shrink))
     return projected, activation, shrink.T[None], expand[None]
 
 

time: 121 us -> 119 us (0.983)
  waiting for transfers between devices: 4.23 us -> 1.55 us
    ppermute x8, waiting for transfers between devices: 4.21 us -> 1.54 us  [along(): return lax.ppermute(x, ('dp', 'tensor'), pairs[k])]
    pallas_call x1 -> x2, Pallas kernels: 4.05 us -> 5.41 us  [the longest x1 2.75 us: finish(): call(kernel, (1,), 0, [HBM] * 3, HBM, array(rows, width), [vmem(3, rows,...]
  transfers between devices with their start and end apart: 15 -> 15, of which waited for: 1 -> 1; matrix products, arithmetic and copies ran while one was open for 0% -> 0% of each run, Pallas kernels for 56% -> 59%
where the time goes in v6:
time: 119 us; the launch traced here: 118 us
  Pallas kernels  72.2 us (61%)
  starting transfers between devices  43.1 us (36%)
  waiting for transfers between devices  1.55 us (1%)
    ppermute x8, starting transfers between devices, along(): return lax.ppermute(x, ('dp', 'tensor'), pairs[k])  26.7 us
    pallas_call x3, Pallas kernels, backward(): call(kernel, (1,), 1, [HBM, HBM], HBM, array(blocks, rows, size), [vmem(r...  21.6 us
    pallas_call x1, Pallas kernels, forward(): call(kernel, (1,), 1, [HBM] * (len(arrays) + 5), [HBM] * 2, [array(rows,...  15.4 us
    all_to_all x3, starting transfers between devices, swap(): return lax.all_to_all(x, axis, 0, 0, axis_index_groups=groups, tiled=True)  15.3 us
    pallas_call x6, Pallas kernels, add_on(): call(kernel, (1,), 1, [HBM] * (1 + len(backs)), HBM, array(rows, width),...  13.1 us
    pallas_call x1, Pallas kernels, adapters(): call(kernel, (1,), 2, [ids_spec(rows)] * 2 + [pl.BlockSpec(memory_space=p...  7.45 us
    pallas_call x1, Pallas kernels, low_parts(): call(kernel, (1,), 2, [ids_spec(rows)] * 2 + [HBM] * 5, HBM, array(n, 2 *...  6.87 us
    pallas_call x1, Pallas kernels, finish(): call(kernel, (1,), 0, [HBM] * 3, HBM, array(rows, width), [vmem(3, rows,...  2.75 us
  transfers between devices with their start and end apart: 15, of which 1 were waited for; matrix products, arithmetic and copies ran while one was open for 0% of the time, Pallas kernels for 59%

profile of v6, /device:TPU:0, one launch (start us, length us, event | category | flops | bytes accessed | tf_op | source)
XLA Modules:
  0.0 117.9 jit_solution(17915180102913457453)
XLA Ops:
  0.6 0.5 collective-permute-start
  1.1 0.1 collective-permute-start.1
  1.2 0.4 collective-permute-start.2
  1.7 5.5 %collective-permute-start.4 = (bf16[256,2048]{1,0:T(8,128)(2,1)}, bf16[256,2048]{1,0:T(8,128)(2,1)}, u32[]{:S(2)}, u32[]{:S(2)}) collective-permute-start(bf16[256,2048]{1,0:T(8,128)(2,1)} %refs_0_), channel_id=1, source_target_pairs={{0,1},{1,2},{2,3},{5,4},{6,5},{7,6},{8,9},{9,10},{10,11},{13,12},{... | collective-permute-start | bytes 3145736 | tf_op jit(solution)/shard_map/ppermute | solution.py:428
  7.2 0.0 collective-permute-done.2
  7.2 0.0 copy-start
  7.2 0.0 collective-permute-done.X_other
  7.2 0.0 collective-permute-done.1.dY_other
  7.2 2.4 %shard_map.102 = bf16[4,128,2048]{2,1,0:T(8,128)(2,1)} custom-call(bf16[64,2048]{1,0:T(8,128)(2,1)} %bitcast.11, bf16[64,2048]{1,0:T(8,128)(2,1)} %bitcast.12), custom_call_target="tpu_custom_call" | custom-call | flops 1000 | bytes 1 | tf_op jit(solution)/shard_map/pallas_call | solution.py:88
  9.6 1.3 %collective-permute-start.3 = (bf16[256,2048]{1,0:T(8,128)(2,1)}, bf16[256,2048]{1,0:T(8,128)(2,1)}, u32[]{:S(2)}, u32[]{:S(2)}) collective-permute-start(bf16[256,2048]{1,0:T(8,128)(2,1)} %refs_0_), channel_id=1, source_target_pairs={{1,0},{2,1},{3,2},{4,5},{5,6},{6,7},{9,8},{10,9},{11,10},{12,13},{... | collective-permute-start | bytes 3145736 | tf_op jit(solution)/shard_map/ppermute | solution.py:428
  10.9 0.0 copy-done
  10.9 4.5 %all-to-all-start = ((bf16[4,128,2048]{2,1,0:T(8,128)(2,1)}), bf16[4,128,2048]{2,1,0:T(8,128)(2,1)}, u32[]{:S(2)}, u32[]{:S(2)}) async-start(bf16[4,128,2048]{2,1,0:T(8,128)(2,1)} %shard_map.102), calls=%async_computation | async-start | bytes 4194304 | tf_op jit(solution)/shard_map/all_to_all | solution.py:27
  15.4 9.5 %shard_map.103.refs_0_ = bf16[2,256,2048]{2,1,0:T(8,128)(2,1)} custom-call(s32[1]{0:T(128)} %bitcast.spot, bf16[256,2048]{1,0:T(8,128)(2,1)} %dY.6, bf16[8192,2048]{1,0:T(8,128)(2,1)} %refs_7_.1), custom_call_target="tpu_custom_call" | custom-call | flops 1000 | bytes 1 | tf_op jit(solution)/shard_map/pallas_call | solution.py:141
  24.9 0.0 collective-permute-done.4.arrived.refs_1_
  24.9 2.4 %shard_map.104 = bf16[256,2048]{1,0:T(8,128)(2,1)} custom-call(s32[1]{0:T(128)} %bitcast.spot, bf16[256,2048]{1,0:T(8,128)(2,1)} %collective-permute-done.4.arrived.refs_1_, bf16[2,256,2048]{2,1,0:T(8,128)(2,1)} %shard_map.103.refs_0_), custom_call_target="tpu_custom_call" | custom-call | flops 1000 | bytes 1 | tf_op jit(solution)/shard_map/pallas_call | solution.py:183
  27.3 5.3 %collective-permute-start.6 = (bf16[256,2048]{1,0:T(8,128)(2,1)}, bf16[256,2048]{1,0:T(8,128)(2,1)}, u32[]{:S(2)}, u32[]{:S(2)}) collective-permute-start(bf16[256,2048]{1,0:T(8,128)(2,1)} %shard_map.104), channel_id=1, source_target_pairs={{0,1},{1,2},{2,3},{5,4},{6,5},{7,6},{8,9},{9,10},{10,11},{13,12},{... | collective-permute-start | bytes 3145736 | tf_op jit(solution)/shard_map/ppermute | solution.py:428
  32.6 0.0 collective-permute-done.3.arrived.refs_6_
  32.6 2.0 %shard_map.105 = bf16[256,2048]{1,0:T(8,128)(2,1)} custom-call(s32[1]{0:T(128)} %bitcast.spot, bf16[256,2048]{1,0:T(8,128)(2,1)} %collective-permute-done.3.arrived.refs_6_, bf16[2,256,2048]{2,1,0:T(8,128)(2,1)} %shard_map.103.refs_0_), custom_call_target="tpu_custom_call" | custom-call | flops 10000000000 | bytes 1 | tf_op jit(solution)/shard_map/pallas_call | solution.py:183
  34.6 1.3 %collective-permute-start.5 = (bf16[256,2048]{1,0:T(8,128)(2,1)}, bf16[256,2048]{1,0:T(8,128)(2,1)}, u32[]{:S(2)}, u32[]{:S(2)}) collective-permute-start(bf16[256,2048]{1,0:T(8,128)(2,1)} %shard_map.105), channel_id=1, source_target_pairs={{1,0},{2,1},{3,2},{4,5},{5,6},{6,7},{9,8},{10,9},{11,10},{12,13},{... | collective-permute-start | bytes 3145736 | tf_op jit(solution)/shard_map/ppermute | solution.py:428
  35.9 6.0 %shard_map.106.refs_1_ = bf16[1,256,2048]{2,1,0:T(8,128)(2,1)} custom-call(s32[1]{0:T(128)} %bitcast.spot, bf16[256,2048]{1,0:T(8,128)(2,1)} %dY.6, bf16[8192,2048]{1,0:T(8,128)(2,1)} %refs_7_.1), custom_call_target="tpu_custom_call" | custom-call | flops 1000 | bytes 1 | tf_op jit(solution)/shard_map/pallas_call | solution.py:141
  41.9 0.0 all-to-all-done.gathered
  42.0 6.9 %shard_map.107 = bf16[4,512,128]{2,1,0:T(8,128)(2,1)} custom-call(s32[1]{0:T(128)} %bitcast.spot, s32[8]{0:T(128)} %slots.3, s32[1,256]{1,0:T(1,128)} %bitcast.13, s32[1,256]{1,0:T(1,128)} %bitcast.15, bf16[256,2048]{1,0:T(8,128)(2,1)} %refs_0_, bf16[256,2048]{1,0:T(8,128)(2,1)} %collective-permute-done.X_other, bf16[256,2048]{1,0:T(8,128)(2,1)} %dY.6, ...), custom_call_target="tpu_custom_call" | custom-call | flops 1000 | bytes 1 | tf_op jit(solution)/shard_map/pallas_call | solution.py:356
  48.8 6.4 %all-to-all-start.1 = ((bf16[4,512,128]{2,1,0:T(8,128)(2,1)}), bf16[4,512,128]{2,1,0:T(8,128)(2,1)S(1)}, u32[]{:S(2)}, u32[]{:S(2)}) async-start(bf16[4,512,128]{2,1,0:T(8,128)(2,1)} %shard_map.107), calls=%async_computation.1 | async-start | bytes 1048576 | tf_op jit(solution)/shard_map/all_to_all | solution.py:27
  55.2 0.0 collective-permute-done.6.arrived.refs_3_
  55.2 2.4 %shard_map.108 = bf16[256,2048]{1,0:T(8,128)(2,1)} custom-call(s32[1]{0:T(128)} %bitcast.spot, bf16[256,2048]{1,0:T(8,128)(2,1)} %collective-permute-done.6.arrived.refs_3_, bf16[2,256,2048]{2,1,0:T(8,128)(2,1)} %shard_map.103.refs_0_, bf16[1,256,2048]{2,1,0:T(8,128)(2,1)} %shard_map.106.refs_1_), custom_call_target="tpu_custom_call" | custom-call | flops 1000 | bytes 1 | tf_op jit(solution)/shard_map/pallas_call | solution.py:183
  57.6 4.9 %collective-permute-start.8 = (bf16[256,2048]{1,0:T(8,128)(2,1)}, bf16[256,2048]{1,0:T(8,128)(2,1)}, u32[]{:S(2)}, u32[]{:S(2)}) collective-permute-start(bf16[256,2048]{1,0:T(8,128)(2,1)} %shard_map.108), channel_id=1, source_target_pairs={{0,1},{1,2},{2,3},{5,4},{6,5},{7,6},{8,9},{9,10},{10,11},{13,12},{... | collective-permute-start | bytes 3145736 | tf_op jit(solution)/shard_map/ppermute | solution.py:428
  62.5 6.0 %shard_map.109.refs_11_ = bf16[1,256,2048]{2,1,0:T(8,128)(2,1)} custom-call(s32[1]{0:T(128)} %bitcast.spot, bf16[256,2048]{1,0:T(8,128)(2,1)} %dY.6, bf16[8192,2048]{1,0:T(8,128)(2,1)} %refs_7_.1), custom_call_target="tpu_custom_call" | custom-call | flops 1000 | bytes 1 | tf_op jit(solution)/shard_map/pallas_call | solution.py:141
  68.6 0.0 collective-permute-done.5.arrived.refs_4_
  68.6 2.0 %shard_map.110 = bf16[256,2048]{1,0:T(8,128)(2,1)} custom-call(s32[1]{0:T(128)} %bitcast.spot, bf16[256,2048]{1,0:T(8,128)(2,1)} %collective-permute-done.5.arrived.refs_4_, bf16[2,256,2048]{2,1,0:T(8,128)(2,1)} %shard_map.103.refs_0_, bf16[1,256,2048]{2,1,0:T(8,128)(2,1)} %shard_map.106.refs_1_), custom_call_target="tpu_custom_call" | custom-call | flops 1000 | bytes 1 | tf_op jit(solution)/shard_map/pallas_call | solution.py:183
  70.6 1.3 %collective-permute-start.7 = (bf16[256,2048]{1,0:T(8,128)(2,1)}, bf16[256,2048]{1,0:T(8,128)(2,1)}, u32[]{:S(2)}, u32[]{:S(2)}) collective-permute-start(bf16[256,2048]{1,0:T(8,128)(2,1)} %shard_map.110), channel_id=1, source_target_pairs={{1,0},{2,1},{3,2},{4,5},{5,6},{6,7},{9,8},{10,9},{11,10},{12,13},{... | collective-permute-start | bytes 3145736 | tf_op jit(solution)/shard_map/ppermute | solution.py:428
  71.9 0.0 all-to-all-done.1.parts
  71.9 7.4 %shard_map.111 = (bf16[4,128,2048]{2,1,0:T(8,128)(2,1)}, bf16[256,2048]{1,0:T(8,128)(2,1)}, bf16[256,2048]{1,0:T(8,128)(2,1)}, bf16[512,2048]{1,0:T(8,128)(2,1)}) custom-call(s32[1]{0:T(128)} %bitcast.spot, s32[8]{0:T(128)} %slots.3, s32[1,256]{1,0:T(1,128)} %bitcast.14, s32[1,256]{1,0:T(1,128)} %bitcast.16, bf16[4,512,128]{2,1,0:T(8,128)(2,1)S(1)} %all-to-all-done.1.parts, ...), custom_call_target="tpu_custom_call" | custom-call | flops 10000000000 | bytes 1 | tf_op jit(solution)/shard_map/pallas_call | solution.py:400
  79.4 4.5 %all-to-all-start.2 = ((bf16[4,128,2048]{2,1,0:T(8,128)(2,1)}), bf16[4,128,2048]{2,1,0:T(8,128)(2,1)}, u32[]{:S(2)}, u32[]{:S(2)}) async-start(bf16[4,128,2048]{2,1,0:T(8,128)(2,1)} %get-tuple-element.47), calls=%async_computation.2 | async-start | bytes 4194304 | tf_op jit(solution)/shard_map/all_to_all | solution.py:27
  83.8 0.1 collective-permute-start.9
  83.9 0.0 collective-permute-done.8.arrived.refs_5_
  83.9 2.4 %shard_map.112 = bf16[256,2048]{1,0:T(8,128)(2,1)} custom-call(s32[1]{0:T(128)} %bitcast.spot, bf16[256,2048]{1,0:T(8,128)(2,1)} %collective-permute-done.8.arrived.refs_5_, bf16[2,256,2048]{2,1,0:T(8,128)(2,1)} %shard_map.103.refs_0_, bf16[1,256,2048]{2,1,0:T(8,128)(2,1)} %shard_map.106.refs_1_), custom_call_target="tpu_custom_call" | custom-call | flops 999999995904 | bytes 1 | tf_op jit(solution)/shard_map/pallas_call | solution.py:183
  86.3 5.5 %collective-permute-start.10 = (bf16[256,2048]{1,0:T(8,128)(2,1)}, bf16[256,2048]{1,0:T(8,128)(2,1)}, u32[]{:S(2)}, u32[]{:S(2)}) collective-permute-start(bf16[256,2048]{1,0:T(8,128)(2,1)} %shard_map.112), channel_id=1, source_target_pairs={{0,1},{1,2},{2,3},{5,4},{6,5},{7,6},{8,9},{9,10},{10,11},{13,12},{... | collective-permute-start | bytes 3145736 | tf_op jit(solution)/shard_map/ppermute | solution.py:428
  91.9 0.0 collective-permute-done.7.arrived.refs_2_
  91.9 2.0 %shard_map.113 = bf16[256,2048]{1,0:T(8,128)(2,1)} custom-call(s32[1]{0:T(128)} %bitcast.spot, bf16[256,2048]{1,0:T(8,128)(2,1)} %collective-permute-done.7.arrived.refs_2_, bf16[2,256,2048]{2,1,0:T(8,128)(2,1)} %shard_map.103.refs_0_, bf16[1,256,2048]{2,1,0:T(8,128)(2,1)} %shard_map.106.refs_1_), custom_call_target="tpu_custom_call" | custom-call | flops 999999995904 | bytes 1 | tf_op jit(solution)/shard_map/pallas_call | solution.py:183
  93.9 1.5 %collective-permute-start.11 = (bf16[256,2048]{1,0:T(8,128)(2,1)}, bf16[256,2048]{1,0:T(8,128)(2,1)}, u32[]{:S(2)}, u32[]{:S(2)}) collective-permute-start(bf16[256,2048]{1,0:T(8,128)(2,1)} %shard_map.113), channel_id=1, source_target_pairs={{1,0},{2,1},{3,2},{4,5},{5,6},{6,7},{9,8},{10,9},{11,10},{12,13},{... | collective-permute-start | bytes 3145736 | tf_op jit(solution)/shard_map/ppermute | solution.py:428
  95.4 0.0 collective-permute-done.9.refs_10_
  95.4 15.4 %shard_map.114 = (bf16[256,2048]{1,0:T(8,128)(2,1)}, bf16[256,2048]{1,0:T(8,128)(2,1)}) custom-call(s32[1]{0:T(128)} %bitcast.spot, bf16[256,2048]{1,0:T(8,128)(2,1)} %refs_0_, bf16[256,2048]{1,0:T(8,128)(2,1)} %collective-permute-done.4.arrived.refs_1_, bf16[256,2048]{1,0:T(8,128)(2,1)} %collective-permute-done.7.arrived.refs_2_, ...), custom_call_target="tpu_custom_call" | custom-call | flops 1000 | bytes 1 | tf_op jit(solution)/shard_map/pallas_call | solution.py:292
  110.8 0.0 all-to-all-done.2.blocks
  110.8 2.7 %shard_map.115 = (bf16[64,2048]{1,0:T(8,128)(2,1)}, bf16[64,2048]{1,0:T(8,128)(2,1)}) custom-call(bf16[4,128,2048]{2,1,0:T(8,128)(2,1)} %all-to-all-done.2.blocks), custom_call_target="tpu_custom_call" | custom-call | flops 1000 | bytes 1 | tf_op jit(solution)/shard_map/pallas_call | solution.py:235
  113.5 0.0 collective-permute-done.10.one
  113.5 1.5 %collective-permute-done.11.two = bf16[256,2048]{1,0:T(8,128)(2,1)} collective-permute-done((bf16[256,2048]{1,0:T(8,128)(2,1)}, bf16[256,2048]{1,0:T(8,128)(2,1)}, u32[]{:S(2)}, u32[]{:S(2)}) %collective-permute-start.11) | collective-permute-done | bytes 1048608 | tf_op jit(solution)/shard_map/ppermute | solution.py:428
  115.0 2.8 %shard_map.116 = bf16[256,2048]{1,0:T(8,128)(2,1)} custom-call(bf16[256,2048]{1,0:T(8,128)(2,1)} %collective-permute-done.10.one, bf16[256,2048]{1,0:T(8,128)(2,1)} %collective-permute-done.11.two, bf16[256,2048]{1,0:T(8,128)(2,1)} %get-tuple-element.50.rest), custom_call_target="tpu_custom_call" | custom-call | flops 1000 | bytes 1 | tf_op jit(solution)/shard_map/pallas_call | solution.py:215
Async XLA Ops:
  0.6 6.6 %collective-permute-start = (bf16[256,2048]{1,0:T(8,128)(2,1)}, bf16[256,2048]{1,0:T(8,128)(2,1)}, u32[]{:S(2)}, u32[]{:S(2)}) collective-permute-start(bf16[256,2048]{1,0:T(8,128)(2,1)} %refs_0_), channel_id=1, source_target_pairs={{0,4},{4,0},{8,12},{12,8},{16,20},{20,16},{24,28},{28,24},{1,5},{5... | collective-permute-start | bytes 3145736 | tf_op jit(solution)/shard_map/ppermute | solution.py:23
  1.1 6.0 %collective-permute-start.1 = (bf16[256,2048]{1,0:T(8,128)(2,1)}, bf16[256,2048]{1,0:T(8,128)(2,1)}, u32[]{:S(2)}, u32[]{:S(2)}) collective-permute-start(bf16[256,2048]{1,0:T(8,128)(2,1)} %dY.6), channel_id=1, source_target_pairs={{0,4},{4,0},{8,12},{12,8},{16,20},{20,16},{24,28},{28,24},{1,5},{5... | collective-permute-start | bytes 3145736 | tf_op jit(solution)/shard_map/ppermute | solution.py:23
  1.2 6.0 %collective-permute-start.2 = (s32[256,1]{0,1:T(1,128)}, s32[256,1]{0,1:T(1,128)S(1)}, u32[]{:S(2)}, u32[]{:S(2)}) collective-permute-start(s32[256,1]{0,1:T(1,128)} %param.12), channel_id=1, source_target_pairs={{0,4},{4,0},{8,12},{12,8},{16,20},{20,16},{24,28},{28,24},{1,5},{5... | collective-permute-start | bytes 3080 | tf_op jit(solution)/shard_map/ppermute | solution.py:23
  1.7 23.2 %collective-permute-start.4 = (bf16[256,2048]{1,0:T(8,128)(2,1)}, bf16[256,2048]{1,0:T(8,128)(2,1)}, u32[]{:S(2)}, u32[]{:S(2)}) collective-permute-start(bf16[256,2048]{1,0:T(8,128)(2,1)} %refs_0_), channel_id=1, source_target_pairs={{0,1},{1,2},{2,3},{5,4},{6,5},{7,6},{8,9},{9,10},{10,11},{13,12},{... | collective-permute-start | bytes 3145736 | tf_op jit(solution)/shard_map/ppermute | solution.py:428
  7.2 3.7 %copy-start = (s32[256,1]{0,1:T(1,128)}, s32[256,1]{0,1:T(1,128)S(1)}, u32[]{:S(2)}) copy-start(s32[256,1]{0,1:T(1,128)S(1)} %collective-permute-done.2) | copy-start | bytes 3076
  9.6 23.0 %collective-permute-start.3 = (bf16[256,2048]{1,0:T(8,128)(2,1)}, bf16[256,2048]{1,0:T(8,128)(2,1)}, u32[]{:S(2)}, u32[]{:S(2)}) collective-permute-start(bf16[256,2048]{1,0:T(8,128)(2,1)} %refs_0_), channel_id=1, source_target_pairs={{1,0},{2,1},{3,2},{4,5},{5,6},{6,7},{9,8},{10,9},{11,10},{12,13},{... | collective-permute-start | bytes 3145736 | tf_op jit(solution)/shard_map/ppermute | solution.py:428
  10.9 31.0 %all-to-all-start = ((bf16[4,128,2048]{2,1,0:T(8,128)(2,1)}), bf16[4,128,2048]{2,1,0:T(8,128)(2,1)}, u32[]{:S(2)}, u32[]{:S(2)}) async-start(bf16[4,128,2048]{2,1,0:T(8,128)(2,1)} %shard_map.102), calls=%async_computation | async-start | bytes 4194304 | tf_op jit(solution)/shard_map/all_to_all | solution.py:27
  27.3 28.0 %collective-permute-start.6 = (bf16[256,2048]{1,0:T(8,128)(2,1)}, bf16[256,2048]{1,0:T(8,128)(2,1)}, u32[]{:S(2)}, u32[]{:S(2)}) collective-permute-start(bf16[256,2048]{1,0:T(8,128)(2,1)} %shard_map.104), channel_id=1, source_target_pairs={{0,1},{1,2},{2,3},{5,4},{6,5},{7,6},{8,9},{9,10},{10,11},{13,12},{... | collective-permute-start | bytes 3145736 | tf_op jit(solution)/shard_map/ppermute | solution.py:428
  34.6 34.0 %collective-permute-start.5 = (bf16[256,2048]{1,0:T(8,128)(2,1)}, bf16[256,2048]{1,0:T(8,128)(2,1)}, u32[]{:S(2)}, u32[]{:S(2)}) collective-permute-start(bf16[256,2048]{1,0:T(8,128)(2,1)} %shard_map.105), channel_id=1, source_target_pairs={{1,0},{2,1},{3,2},{4,5},{5,6},{6,7},{9,8},{10,9},{11,10},{12,13},{... | collective-permute-start | bytes 3145736 | tf_op jit(solution)/shard_map/ppermute | solution.py:428
  48.8 23.1 %all-to-all-start.1 = ((bf16[4,512,128]{2,1,0:T(8,128)(2,1)}), bf16[4,512,128]{2,1,0:T(8,128)(2,1)S(1)}, u32[]{:S(2)}, u32[]{:S(2)}) async-start(bf16[4,512,128]{2,1,0:T(8,128)(2,1)} %shard_map.107), calls=%async_computation.1 | async-start | bytes 1048576 | tf_op jit(solution)/shard_map/all_to_all | solution.py:27
  57.6 26.3 %collective-permute-start.8 = (bf16[256,2048]{1,0:T(8,128)(2,1)}, bf16[256,2048]{1,0:T(8,128)(2,1)}, u32[]{:S(2)}, u32[]{:S(2)}) collective-permute-start(bf16[256,2048]{1,0:T(8,128)(2,1)} %shard_map.108), channel_id=1, source_target_pairs={{0,1},{1,2},{2,3},{5,4},{6,5},{7,6},{8,9},{9,10},{10,11},{13,12},{... | collective-permute-start | bytes 3145736 | tf_op jit(solution)/shard_map/ppermute | solution.py:428
  70.6 21.2 %collective-permute-start.7 = (bf16[256,2048]{1,0:T(8,128)(2,1)}, bf16[256,2048]{1,0:T(8,128)(2,1)}, u32[]{:S(2)}, u32[]{:S(2)}) collective-permute-start(bf16[256,2048]{1,0:T(8,128)(2,1)} %shard_map.110), channel_id=1, source_target_pairs={{1,0},{2,1},{3,2},{4,5},{5,6},{6,7},{9,8},{10,9},{11,10},{12,13},{... | collective-permute-start | bytes 3145736 | tf_op jit(solution)/shard_map/ppermute | solution.py:428
  79.4 31.4 %all-to-all-start.2 = ((bf16[4,128,2048]{2,1,0:T(8,128)(2,1)}), bf16[4,128,2048]{2,1,0:T(8,128)(2,1)}, u32[]{:S(2)}, u32[]{:S(2)}) async-start(bf16[4,128,2048]{2,1,0:T(8,128)(2,1)} %get-tuple-element.47), calls=%async_computation.2 | async-start | bytes 4194304 | tf_op jit(solution)/shard_map/all_to_all | solution.py:27
  83.8 11.6 %collective-permute-start.9 = (bf16[512,2048]{1,0:T(8,128)(2,1)}, bf16[512,2048]{1,0:T(8,128)(2,1)}, u32[]{:S(2)}, u32[]{:S(2)}) collective-permute-start(bf16[512,2048]{1,0:T(8,128)(2,1)} %get-tuple-element.39), channel_id=1, source_target_pairs={{0,4},{4,0},{8,12},{12,8},{16,20},{20,16},{24,28},{28,24},{1,5},{5... | collective-permute-start | bytes 6291464 | tf_op jit(solution)/shard_map/ppermute | solution.py:23
  86.3 27.1 %collective-permute-start.10 = (bf16[256,2048]{1,0:T(8,128)(2,1)}, bf16[256,2048]{1,0:T(8,128)(2,1)}, u32[]{:S(2)}, u32[]{:S(2)}) collective-permute-start(bf16[256,2048]{1,0:T(8,128)(2,1)} %shard_map.112), channel_id=1, source_target_pairs={{0,1},{1,2},{2,3},{5,4},{6,5},{7,6},{8,9},{9,10},{10,11},{13,12},{... | collective-permute-start | bytes 3145736 | tf_op jit(solution)/shard_map/ppermute | solution.py:428
  93.9 21.1 %collective-permute-start.11 = (bf16[256,2048]{1,0:T(8,128)(2,1)}, bf16[256,2048]{1,0:T(8,128)(2,1)}, u32[]{:S(2)}, u32[]{:S(2)}) collective-permute-start(bf16[256,2048]{1,0:T(8,128)(2,1)} %shard_map.113), channel_id=1, source_target_pairs={{1,0},{2,1},{3,2},{4,5},{5,6},{6,7},{9,8},{10,9},{11,10},{12,13},{... | collective-permute-start | bytes 3145736 | tf_op jit(solution)/shard_map/ppermute | solution.py:428

commit v7 on v6

--- a/solution.py
+++ b/solution.py
@@ -351,7 +351,7 @@
         low = pick(x, downs)
         wait(more)
         part[...] = jnp.concatenate([low, pick(y, ups)], axis=1).astype(bf16)
-        wait(fetch([(part, out.at[k]) for k in range(n)], sem, 4 + 2 * half))
+        wait(fetch([(part, out)], sem, 4 + 2 * half))
 
     return call(
         kernel,
@@ -359,24 +359,25 @@
         2,
         [ids_spec(rows)] * 2 + [HBM] * 5,
         HBM,
-        array(n, 2 * rows, 2 * rank),
+        array(2 * rows, 2 * rank),
         [vmem(2 * rows, width)] * 2
         + [vmem(half * rank, width)] * 2
         + [vmem(2 * rows, 2 * rank), sems(4 + 2 * half + n)],
     )(spot, slots, *ids, *far(*Xs, *dYs, gathered))
 
 
-def adapters(spot, slots, ids, parts, Xs, dYs, gathered, rank):
+def adapters(spot, slots, ids, few, Xs, dYs, gathered, rank):
     rows, width = Xs[0].shape
     half = gathered.shape[0]
 
-    def kernel(spot, slots, id0, id1, parts, X, X_other, dY, dY_other, gathered, out, term, back, other, *scratch):
+    def kernel(spot, slots, id0, id1, *refs):
+        parts, (X, X_other, dY, dY_other, gathered, out, term, back, other, *scratch) = refs[: len(few)], refs[len(few) :]
         x, y, downs, ups, grads, terms, sem, out_sem = scratch
         ins = fetch(
             rows_of((X, X_other), (dY, dY_other), x, y, rows) + pieces(gathered, downs, ups, rank), sem
         )
         chosen = chosen_of(spot, slots, (id0, id1), rank, half)
-        total = sum(parts[k].astype(f32) for k in range(parts.shape[0]))
+        total = sum(p[...].astype(f32) for p in parts)
         low, grad = total[:, :rank].astype(bf16), (adapter_scale * total[:, rank:]).astype(bf16)
         zero = jnp.zeros((), bf16)
         low, grad = [jnp.where(chosen, jnp.concatenate([v] * half, axis=1), zero) for v in (low, grad)]
@@ -401,7 +402,7 @@
         kernel,
         (1,),
         2,
-        [ids_spec(rows)] * 2 + [pl.BlockSpec(memory_space=pltpu.VMEM)] + [HBM] * 5,
+        [ids_spec(rows)] * 2 + [pl.BlockSpec(memory_space=pltpu.VMEM)] * len(few) + [HBM] * 5,
         [HBM] * 4,
         [array(half, 2 * rank, width), array(rows, width), array(rows, width), array(2 * rows, width)],
         [vmem(2 * rows, width)] * 2
@@ -409,7 +410,7 @@
         + [vmem(half, 2 * rank, width), vmem(2, 2 * rows, width), sems(4 + 2 * half), sems(5)],
         mib=60,
         cost=GRADS,
-    )(spot, slots, *ids, pltpu.with_memory_space_constraint(parts, pltpu.VMEM), *far(*Xs, *dYs, gathered))
+    )(spot, slots, *ids, *[pltpu.with_memory_space_constraint(p, pltpu.VMEM) for p in few], *far(*Xs, *dYs, gathered))
 
 
 def body(X, dY, W, A, B, adapter_rows, adapter_slot):
@@ -471,7 +472,7 @@
     backs.append(backward(spot, table, second, after(dY, last), W, n))
     gathered = after(gathered, backs[1])
     part = low_parts(spot, adapter_slot, ids, Xs, dYs, gathered, rank, n)
-    parts = swap(part, "tensor", None)
+    parts = [part] + [exchange(part, "tensor", k) for k in range(1, n)]
 
     last = part
     for s in range(2, n):
@@ -481,7 +482,7 @@
             last = own_back
         last = onward(s, 1, last)
         if s == 2:
-            parts = after(parts, last)
+            parts = [after(p, last) for p in parts]
             mine, term, back_term, send = adapters(spot, adapter_slot, ids, parts, Xs, dYs, gathered, rank)
             arriving = swap(mine, "dp", chips)
             other = exchange(send, "dp", 1)

time: 119 us -> 118 us (level)
  starting transfers between devices: 43.1 us -> 41.9 us
    all_to_all x3 -> x2, starting transfers between devices: 15.3 us -> 8.93 us  [swap(): return lax.all_to_all(x, axis, 0, 0, axis_index_groups=groups, tiled=True)]
    ppermute x4 -> x7, starting transfers between devices: 1.1 us -> 6.93 us  [exchange(): return lax.ppermute(x, axis, [(i, i ^ offset) for i in range(size)])]
  transfers between devices with their start and end apart: 15 -> 17, of which waited for: 1 -> 2; matrix products, arithmetic and copies ran while one was open for 0% -> 0% of each run, Pallas kernels for 59% -> 59%
where the time goes in v7:
time: 118 us; the launch traced here: 117 us
  Pallas kernels  72.1 us (61%)
  starting transfers between devices  41.9 us (36%)
  waiting for transfers between devices  1.59 us (1%)
    ppermute x8, starting transfers between devices, along(): return lax.ppermute(x, ('dp', 'tensor'), pairs[k])  26 us
    pallas_call x3, Pallas kernels, backward(): call(kernel, (1,), 1, [HBM, HBM], HBM, array(blocks, rows, size), [vmem(r...  21.6 us
    pallas_call x1, Pallas kernels, forward(): call(kernel, (1,), 1, [HBM] * (len(arrays) + 5), [HBM] * 2, [array(rows,...  15.3 us
    pallas_call x6, Pallas kernels, add_on(): call(kernel, (1,), 1, [HBM] * (1 + len(backs)), HBM, array(rows, width),...  13.2 us
    all_to_all x2, starting transfers between devices, swap(): return lax.all_to_all(x, axis, 0, 0, axis_index_groups=groups, tiled=True)  8.93 us
    pallas_call x1, Pallas kernels, adapters(): call(kernel, (1,), 2, [ids_spec(rows)] * 2 + [pl.BlockSpec(memory_space=p...  7.43 us
    ppermute x7, starting transfers between devices, exchange(): return lax.ppermute(x, axis, [(i, i ^ offset) for i in range(size)])  6.93 us
    pallas_call x1, Pallas kernels, low_parts(): call(kernel, (1,), 2, [ids_spec(rows)] * 2 + [HBM] * 5, HBM, array(2 * ro...  6.73 us
  transfers between devices with their start and end apart: 17, of which 2 were waited for; matrix products, arithmetic and copies ran while one was open for 0% of the time, Pallas kernels for 59%

profile of v7, /device:TPU:0, one launch (start us, length us, event | category | flops | bytes accessed | tf_op | source)
XLA Modules:
  0.0 116.7 jit_solution(3794950307035583063)
XLA Ops:
  0.6 0.5 collective-permute-start
  1.1 0.1 collective-permute-start.1
  1.2 0.4 collective-permute-start.2
  1.7 5.5 %collective-permute-start.4 = (bf16[256,2048]{1,0:T(8,128)(2,1)}, bf16[256,2048]{1,0:T(8,128)(2,1)}, u32[]{:S(2)}, u32[]{:S(2)}) collective-permute-start(bf16[256,2048]{1,0:T(8,128)(2,1)} %refs_0_), channel_id=1, source_target_pairs={{0,1},{1,2},{2,3},{5,4},{6,5},{7,6},{8,9},{9,10},{10,11},{13,12},{... | collective-permute-start | bytes 3145736 | tf_op jit(solution)/shard_map/ppermute | solution.py:429
  7.2 0.0 collective-permute-done.2
  7.2 0.0 copy-start.1
  7.2 0.0 collective-permute-done.X_other.refs_5_
  7.2 0.0 collective-permute-done.1.dY_other.refs_7_
  7.2 2.4 %shard_map.102 = bf16[4,128,2048]{2,1,0:T(8,128)(2,1)} custom-call(bf16[64,2048]{1,0:T(8,128)(2,1)} %bitcast.11, bf16[64,2048]{1,0:T(8,128)(2,1)} %bitcast.12), custom_call_target="tpu_custom_call" | custom-call | flops 1000 | bytes 1 | tf_op jit(solution)/shard_map/pallas_call | solution.py:88
  9.6 1.3 %collective-permute-start.3 = (bf16[256,2048]{1,0:T(8,128)(2,1)}, bf16[256,2048]{1,0:T(8,128)(2,1)}, u32[]{:S(2)}, u32[]{:S(2)}) collective-permute-start(bf16[256,2048]{1,0:T(8,128)(2,1)} %refs_0_), channel_id=1, source_target_pairs={{1,0},{2,1},{3,2},{4,5},{5,6},{6,7},{9,8},{10,9},{11,10},{12,13},{... | collective-permute-start | bytes 3145736 | tf_op jit(solution)/shard_map/ppermute | solution.py:429
  10.9 0.0 copy-done.1
  10.9 4.5 %all-to-all-start = ((bf16[4,128,2048]{2,1,0:T(8,128)(2,1)}), bf16[4,128,2048]{2,1,0:T(8,128)(2,1)}, u32[]{:S(2)}, u32[]{:S(2)}) async-start(bf16[4,128,2048]{2,1,0:T(8,128)(2,1)} %shard_map.102), calls=%async_computation | async-start | bytes 4194304 | tf_op jit(solution)/shard_map/all_to_all | solution.py:27
  15.4 9.5 %shard_map.103.refs_0_ = bf16[2,256,2048]{2,1,0:T(8,128)(2,1)} custom-call(s32[1]{0:T(128)} %bitcast.spot, bf16[256,2048]{1,0:T(8,128)(2,1)} %refs_6_.1, bf16[8192,2048]{1,0:T(8,128)(2,1)} %refs_7_.1), custom_call_target="tpu_custom_call" | custom-call | flops 1000 | bytes 1 | tf_op jit(solution)/shard_map/pallas_call | solution.py:141
  25.0 0.0 collective-permute-done.4.arrived.refs_1_
  25.0 2.4 %shard_map.104 = bf16[256,2048]{1,0:T(8,128)(2,1)} custom-call(s32[1]{0:T(128)} %bitcast.spot, bf16[256,2048]{1,0:T(8,128)(2,1)} %collective-permute-done.4.arrived.refs_1_, bf16[2,256,2048]{2,1,0:T(8,128)(2,1)} %shard_map.103.refs_0_), custom_call_target="tpu_custom_call" | custom-call | flops 1000 | bytes 1 | tf_op jit(solution)/shard_map/pallas_call | solution.py:183
  27.3 5.3 %collective-permute-start.6 = (bf16[256,2048]{1,0:T(8,128)(2,1)}, bf16[256,2048]{1,0:T(8,128)(2,1)}, u32[]{:S(2)}, u32[]{:S(2)}) collective-permute-start(bf16[256,2048]{1,0:T(8,128)(2,1)} %shard_map.104), channel_id=1, source_target_pairs={{0,1},{1,2},{2,3},{5,4},{6,5},{7,6},{8,9},{9,10},{10,11},{13,12},{... | collective-permute-start | bytes 3145736 | tf_op jit(solution)/shard_map/ppermute | solution.py:429
  32.7 0.0 collective-permute-done.3.arrived.refs_6_
  32.7 2.0 %shard_map.105 = bf16[256,2048]{1,0:T(8,128)(2,1)} custom-call(s32[1]{0:T(128)} %bitcast.spot, bf16[256,2048]{1,0:T(8,128)(2,1)} %collective-permute-done.3.arrived.refs_6_, bf16[2,256,2048]{2,1,0:T(8,128)(2,1)} %shard_map.103.refs_0_), custom_call_target="tpu_custom_call" | custom-call | flops 10000000000 | bytes 1 | tf_op jit(solution)/shard_map/pallas_call | solution.py:183
  34.7 1.3 %collective-permute-start.5 = (bf16[256,2048]{1,0:T(8,128)(2,1)}, bf16[256,2048]{1,0:T(8,128)(2,1)}, u32[]{:S(2)}, u32[]{:S(2)}) collective-permute-start(bf16[256,2048]{1,0:T(8,128)(2,1)} %shard_map.105), channel_id=1, source_target_pairs={{1,0},{2,1},{3,2},{4,5},{5,6},{6,7},{9,8},{10,9},{11,10},{12,13},{... | collective-permute-start | bytes 3145736 | tf_op jit(solution)/shard_map/ppermute | solution.py:429
  36.0 6.0 %shard_map.106.refs_1_ = bf16[1,256,2048]{2,1,0:T(8,128)(2,1)} custom-call(s32[1]{0:T(128)} %bitcast.spot, bf16[256,2048]{1,0:T(8,128)(2,1)} %refs_6_.1, bf16[8192,2048]{1,0:T(8,128)(2,1)} %refs_7_.1), custom_call_target="tpu_custom_call" | custom-call | flops 1000 | bytes 1 | tf_op jit(solution)/shard_map/pallas_call | solution.py:141
  42.0 0.0 all-to-all-done.gathered.refs_8_
  42.0 6.7 %shard_map.107.refs_0_ = bf16[512,128]{1,0:T(8,128)(2,1)} custom-call(s32[1]{0:T(128)} %bitcast.spot, s32[8]{0:T(128)} %slots.3, s32[1,256]{1,0:T(1,128)} %bitcast.13, s32[1,256]{1,0:T(1,128)} %bitcast.15, bf16[256,2048]{1,0:T(8,128)(2,1)} %refs_0_, bf16[256,2048]{1,0:T(8,128)(2,1)} %collective-permute-done.X_other.refs_5_, bf16[256,2048]{1,0:T(8,128)(2,1)} %refs_6_.1, ...), custom_call_target="tpu_custom_call" | custom-call | flops 1000 | bytes 1 | tf_op jit(solution)/shard_map/pallas_call | solution.py:356
  48.8 5.2 %collective-permute-start.11 = (bf16[512,128]{1,0:T(8,128)(2,1)}, bf16[512,128]{1,0:T(8,128)(2,1)S(1)}, u32[]{:S(2)}, u32[]{:S(2)}) collective-permute-start(bf16[512,128]{1,0:T(8,128)(2,1)} %shard_map.107.refs_0_), channel_id=1, source_target_pairs={{0,3},{1,2},{2,1},{3,0},{4,7},{5,6},{6,5},{7,4},{8,11},{9,10},{10,... | collective-permute-start | bytes 393224 | tf_op jit(solution)/shard_map/ppermute | solution.py:23
  53.9 0.0 collective-permute-start.10
  53.9 0.6 collective-permute-start.9
  54.6 0.0 collective-permute-done.6.arrived.refs_3_
  54.6 2.4 %shard_map.108 = bf16[256,2048]{1,0:T(8,128)(2,1)} custom-call(s32[1]{0:T(128)} %bitcast.spot, bf16[256,2048]{1,0:T(8,128)(2,1)} %collective-permute-done.6.arrived.refs_3_, bf16[2,256,2048]{2,1,0:T(8,128)(2,1)} %shard_map.103.refs_0_, bf16[1,256,2048]{2,1,0:T(8,128)(2,1)} %shard_map.106.refs_1_), custom_call_target="tpu_custom_call" | custom-call | flops 1000 | bytes 1 | tf_op jit(solution)/shard_map/pallas_call | solution.py:183
  57.0 4.3 %collective-permute-start.8 = (bf16[256,2048]{1,0:T(8,128)(2,1)}, bf16[256,2048]{1,0:T(8,128)(2,1)}, u32[]{:S(2)}, u32[]{:S(2)}) collective-permute-start(bf16[256,2048]{1,0:T(8,128)(2,1)} %shard_map.108), channel_id=1, source_target_pairs={{0,1},{1,2},{2,3},{5,4},{6,5},{7,6},{8,9},{9,10},{10,11},{13,12},{... | collective-permute-start | bytes 3145736 | tf_op jit(solution)/shard_map/ppermute | solution.py:429
  61.2 6.0 %shard_map.109.refs_11_ = bf16[1,256,2048]{2,1,0:T(8,128)(2,1)} custom-call(s32[1]{0:T(128)} %bitcast.spot, bf16[256,2048]{1,0:T(8,128)(2,1)} %refs_6_.1, bf16[8192,2048]{1,0:T(8,128)(2,1)} %refs_7_.1), custom_call_target="tpu_custom_call" | custom-call | flops 1000 | bytes 1 | tf_op jit(solution)/shard_map/pallas_call | solution.py:141
  67.3 0.0 copy-start
  67.3 0.0 collective-permute-done.5.arrived.refs_4_
  67.3 2.1 %shard_map.110 = bf16[256,2048]{1,0:T(8,128)(2,1)} custom-call(s32[1]{0:T(128)} %bitcast.spot, bf16[256,2048]{1,0:T(8,128)(2,1)} %collective-permute-done.5.arrived.refs_4_, bf16[2,256,2048]{2,1,0:T(8,128)(2,1)} %shard_map.103.refs_0_, bf16[1,256,2048]{2,1,0:T(8,128)(2,1)} %shard_map.106.refs_1_), custom_call_target="tpu_custom_call" | custom-call | flops 1000 | bytes 1 | tf_op jit(solution)/shard_map/pallas_call | solution.py:183
  69.4 1.3 %collective-permute-start.7 = (bf16[256,2048]{1,0:T(8,128)(2,1)}, bf16[256,2048]{1,0:T(8,128)(2,1)}, u32[]{:S(2)}, u32[]{:S(2)}) collective-permute-start(bf16[256,2048]{1,0:T(8,128)(2,1)} %shard_map.110), channel_id=1, source_target_pairs={{1,0},{2,1},{3,2},{4,5},{5,6},{6,7},{9,8},{10,9},{11,10},{12,13},{... | collective-permute-start | bytes 3145736 | tf_op jit(solution)/shard_map/ppermute | solution.py:429
  70.7 0.0 collective-permute-done.11.refs_3_
  70.7 0.6 collective-permute-done.10.refs_2_
  71.3 0.0 collective-permute-done.9.refs_1_
  71.3 0.0 copy-done
  71.3 7.4 %shard_map.111 = (bf16[4,128,2048]{2,1,0:T(8,128)(2,1)}, bf16[256,2048]{1,0:T(8,128)(2,1)}, bf16[256,2048]{1,0:T(8,128)(2,1)}, bf16[512,2048]{1,0:T(8,128)(2,1)}) custom-call(s32[1]{0:T(128)} %bitcast.spot, s32[8]{0:T(128)} %slots.3, s32[1,256]{1,0:T(1,128)} %bitcast.14, s32[1,256]{1,0:T(1,128)} %bitcast.16, bf16[512,128]{1,0:T(8,128)(2,1)S(1)} %copy-done, ...), custom_call_target="tpu_custom_call" | custom-call | flops 10000000000 | bytes 1 | tf_op jit(solution)/shard_map/pallas_call | solution.py:401
  78.8 4.5 %all-to-all-start.1 = ((bf16[4,128,2048]{2,1,0:T(8,128)(2,1)}), bf16[4,128,2048]{2,1,0:T(8,128)(2,1)}, u32[]{:S(2)}, u32[]{:S(2)}) async-start(bf16[4,128,2048]{2,1,0:T(8,128)(2,1)} %get-tuple-element.53), calls=%async_computation.1 | async-start | bytes 4194304 | tf_op jit(solution)/shard_map/all_to_all | solution.py:27
  83.2 0.1 collective-permute-start.12
  83.3 0.0 collective-permute-done.8.arrived.refs_5_
  83.3 2.4 %shard_map.112 = bf16[256,2048]{1,0:T(8,128)(2,1)} custom-call(s32[1]{0:T(128)} %bitcast.spot, bf16[256,2048]{1,0:T(8,128)(2,1)} %collective-permute-done.8.arrived.refs_5_, bf16[2,256,2048]{2,1,0:T(8,128)(2,1)} %shard_map.103.refs_0_, bf16[1,256,2048]{2,1,0:T(8,128)(2,1)} %shard_map.106.refs_1_), custom_call_target="tpu_custom_call" | custom-call | flops 999999995904 | bytes 1 | tf_op jit(solution)/shard_map/pallas_call | solution.py:183
  85.7 5.5 %collective-permute-start.13 = (bf16[256,2048]{1,0:T(8,128)(2,1)}, bf16[256,2048]{1,0:T(8,128)(2,1)}, u32[]{:S(2)}, u32[]{:S(2)}) collective-permute-start(bf16[256,2048]{1,0:T(8,128)(2,1)} %shard_map.112), channel_id=1, source_target_pairs={{0,1},{1,2},{2,3},{5,4},{6,5},{7,6},{8,9},{9,10},{10,11},{13,12},{... | collective-permute-start | bytes 3145736 | tf_op jit(solution)/shard_map/ppermute | solution.py:429
  91.3 0.0 collective-permute-done.7.arrived.refs_2_
  91.3 2.0 %shard_map.113 = bf16[256,2048]{1,0:T(8,128)(2,1)} custom-call(s32[1]{0:T(128)} %bitcast.spot, bf16[256,2048]{1,0:T(8,128)(2,1)} %collective-permute-done.7.arrived.refs_2_, bf16[2,256,2048]{2,1,0:T(8,128)(2,1)} %shard_map.103.refs_0_, bf16[1,256,2048]{2,1,0:T(8,128)(2,1)} %shard_map.106.refs_1_), custom_call_target="tpu_custom_call" | custom-call | flops 999999995904 | bytes 1 | tf_op jit(solution)/shard_map/pallas_call | solution.py:183
  93.3 1.5 %collective-permute-start.14 = (bf16[256,2048]{1,0:T(8,128)(2,1)}, bf16[256,2048]{1,0:T(8,128)(2,1)}, u32[]{:S(2)}, u32[]{:S(2)}) collective-permute-start(bf16[256,2048]{1,0:T(8,128)(2,1)} %shard_map.113), channel_id=1, source_target_pairs={{1,0},{2,1},{3,2},{4,5},{5,6},{6,7},{9,8},{10,9},{11,10},{12,13},{... | collective-permute-start | bytes 3145736 | tf_op jit(solution)/shard_map/ppermute | solution.py:429
  94.8 0.0 collective-permute-done.12.refs_10_
  94.8 15.3 %shard_map.114 = (bf16[256,2048]{1,0:T(8,128)(2,1)}, bf16[256,2048]{1,0:T(8,128)(2,1)}) custom-call(s32[1]{0:T(128)} %bitcast.spot, bf16[256,2048]{1,0:T(8,128)(2,1)} %refs_0_, bf16[256,2048]{1,0:T(8,128)(2,1)} %collective-permute-done.4.arrived.refs_1_, bf16[256,2048]{1,0:T(8,128)(2,1)} %collective-permute-done.7.arrived.refs_2_, ...), custom_call_target="tpu_custom_call" | custom-call | flops 1000 | bytes 1 | tf_op jit(solution)/shard_map/pallas_call | solution.py:292
  110.2 0.0 all-to-all-done.1.blocks
  110.2 2.7 %shard_map.115 = (bf16[64,2048]{1,0:T(8,128)(2,1)}, bf16[64,2048]{1,0:T(8,128)(2,1)}) custom-call(bf16[4,128,2048]{2,1,0:T(8,128)(2,1)} %all-to-all-done.1.blocks), custom_call_target="tpu_custom_call" | custom-call | flops 1000 | bytes 1 | tf_op jit(solution)/shard_map/pallas_call | solution.py:235
  112.8 0.0 collective-permute-done.13.one
  112.9 0.9 collective-permute-done.14.two
  113.8 2.8 %shard_map.116 = bf16[256,2048]{1,0:T(8,128)(2,1)} custom-call(bf16[256,2048]{1,0:T(8,128)(2,1)} %collective-permute-done.13.one, bf16[256,2048]{1,0:T(8,128)(2,1)} %collective-permute-done.14.two, bf16[256,2048]{1,0:T(8,128)(2,1)} %get-tuple-element.56.rest), custom_call_target="tpu_custom_call" | custom-call | flops 1000 | bytes 1 | tf_op jit(solution)/shard_map/pallas_call | solution.py:215
Async XLA Ops:
  0.6 6.6 %collective-permute-start = (bf16[256,2048]{1,0:T(8,128)(2,1)}, bf16[256,2048]{1,0:T(8,128)(2,1)}, u32[]{:S(2)}, u32[]{:S(2)}) collective-permute-start(bf16[256,2048]{1,0:T(8,128)(2,1)} %refs_0_), channel_id=1, source_target_pairs={{0,4},{4,0},{8,12},{12,8},{16,20},{20,16},{24,28},{28,24},{1,5},{5... | collective-permute-start | bytes 3145736 | tf_op jit(solution)/shard_map/ppermute | solution.py:23
  1.1 6.1 %collective-permute-start.1 = (bf16[256,2048]{1,0:T(8,128)(2,1)}, bf16[256,2048]{1,0:T(8,128)(2,1)}, u32[]{:S(2)}, u32[]{:S(2)}) collective-permute-start(bf16[256,2048]{1,0:T(8,128)(2,1)} %refs_6_.1), channel_id=1, source_target_pairs={{0,4},{4,0},{8,12},{12,8},{16,20},{20,16},{24,28},{28,24},{1,5},{5... | collective-permute-start | bytes 3145736 | tf_op jit(solution)/shard_map/ppermute | solution.py:23
  1.2 6.0 %collective-permute-start.2 = (s32[256,1]{0,1:T(1,128)}, s32[256,1]{0,1:T(1,128)S(1)}, u32[]{:S(2)}, u32[]{:S(2)}) collective-permute-start(s32[256,1]{0,1:T(1,128)} %param.12), channel_id=1, source_target_pairs={{0,4},{4,0},{8,12},{12,8},{16,20},{20,16},{24,28},{28,24},{1,5},{5... | collective-permute-start | bytes 3080 | tf_op jit(solution)/shard_map/ppermute | solution.py:23
  1.7 23.3 %collective-permute-start.4 = (bf16[256,2048]{1,0:T(8,128)(2,1)}, bf16[256,2048]{1,0:T(8,128)(2,1)}, u32[]{:S(2)}, u32[]{:S(2)}) collective-permute-start(bf16[256,2048]{1,0:T(8,128)(2,1)} %refs_0_), channel_id=1, source_target_pairs={{0,1},{1,2},{2,3},{5,4},{6,5},{7,6},{8,9},{9,10},{10,11},{13,12},{... | collective-permute-start | bytes 3145736 | tf_op jit(solution)/shard_map/ppermute | solution.py:429
  7.2 3.7 %copy-start.1 = (s32[256,1]{0,1:T(1,128)}, s32[256,1]{0,1:T(1,128)S(1)}, u32[]{:S(2)}) copy-start(s32[256,1]{0,1:T(1,128)S(1)} %collective-permute-done.2) | copy-start | bytes 3076
  9.6 23.0 %collective-permute-start.3 = (bf16[256,2048]{1,0:T(8,128)(2,1)}, bf16[256,2048]{1,0:T(8,128)(2,1)}, u32[]{:S(2)}, u32[]{:S(2)}) collective-permute-start(bf16[256,2048]{1,0:T(8,128)(2,1)} %refs_0_), channel_id=1, source_target_pairs={{1,0},{2,1},{3,2},{4,5},{5,6},{6,7},{9,8},{10,9},{11,10},{12,13},{... | collective-permute-start | bytes 3145736 | tf_op jit(solution)/shard_map/ppermute | solution.py:429
  10.9 31.1 %all-to-all-start = ((bf16[4,128,2048]{2,1,0:T(8,128)(2,1)}), bf16[4,128,2048]{2,1,0:T(8,128)(2,1)}, u32[]{:S(2)}, u32[]{:S(2)}) async-start(bf16[4,128,2048]{2,1,0:T(8,128)(2,1)} %shard_map.102), calls=%async_computation | async-start | bytes 4194304 | tf_op jit(solution)/shard_map/all_to_all | solution.py:27
  27.3 27.2 %collective-permute-start.6 = (bf16[256,2048]{1,0:T(8,128)(2,1)}, bf16[256,2048]{1,0:T(8,128)(2,1)}, u32[]{:S(2)}, u32[]{:S(2)}) collective-permute-start(bf16[256,2048]{1,0:T(8,128)(2,1)} %shard_map.104), channel_id=1, source_target_pairs={{0,1},{1,2},{2,3},{5,4},{6,5},{7,6},{8,9},{9,10},{10,11},{13,12},{... | collective-permute-start | bytes 3145736 | tf_op jit(solution)/shard_map/ppermute | solution.py:429
  34.7 32.6 %collective-permute-start.5 = (bf16[256,2048]{1,0:T(8,128)(2,1)}, bf16[256,2048]{1,0:T(8,128)(2,1)}, u32[]{:S(2)}, u32[]{:S(2)}) collective-permute-start(bf16[256,2048]{1,0:T(8,128)(2,1)} %shard_map.105), channel_id=1, source_target_pairs={{1,0},{2,1},{3,2},{4,5},{5,6},{6,7},{9,8},{10,9},{11,10},{12,13},{... | collective-permute-start | bytes 3145736 | tf_op jit(solution)/shard_map/ppermute | solution.py:429
  48.8 21.9 %collective-permute-start.11 = (bf16[512,128]{1,0:T(8,128)(2,1)}, bf16[512,128]{1,0:T(8,128)(2,1)S(1)}, u32[]{:S(2)}, u32[]{:S(2)}) collective-permute-start(bf16[512,128]{1,0:T(8,128)(2,1)} %shard_map.107.refs_0_), channel_id=1, source_target_pairs={{0,3},{1,2},{2,1},{3,0},{4,7},{5,6},{6,5},{7,4},{8,11},{9,10},{10,... | collective-permute-start | bytes 393224 | tf_op jit(solution)/shard_map/ppermute | solution.py:23
  53.9 17.4 %collective-permute-start.10 = (bf16[512,128]{1,0:T(8,128)(2,1)}, bf16[512,128]{1,0:T(8,128)(2,1)S(1)}, u32[]{:S(2)}, u32[]{:S(2)}) collective-permute-start(bf16[512,128]{1,0:T(8,128)(2,1)} %shard_map.107.refs_0_), channel_id=1, source_target_pairs={{0,2},{1,3},{2,0},{3,1},{4,6},{5,7},{6,4},{7,5},{8,10},{9,11},{10,... | collective-permute-start | bytes 393224 | tf_op jit(solution)/shard_map/ppermute | solution.py:23
  53.9 17.4 %collective-permute-start.9 = (bf16[512,128]{1,0:T(8,128)(2,1)}, bf16[512,128]{1,0:T(8,128)(2,1)S(1)}, u32[]{:S(2)}, u32[]{:S(2)}) collective-permute-start(bf16[512,128]{1,0:T(8,128)(2,1)} %shard_map.107.refs_0_), channel_id=1, source_target_pairs={{0,1},{1,0},{2,3},{3,2},{4,5},{5,4},{6,7},{7,6},{8,9},{9,8},{10,11... | collective-permute-start | bytes 393224 | tf_op jit(solution)/shard_map/ppermute | solution.py:23
  57.0 26.4 %collective-permute-start.8 = (bf16[256,2048]{1,0:T(8,128)(2,1)}, bf16[256,2048]{1,0:T(8,128)(2,1)}, u32[]{:S(2)}, u32[]{:S(2)}) collective-permute-start(bf16[256,2048]{1,0:T(8,128)(2,1)} %shard_map.108), channel_id=1, source_target_pairs={{0,1},{1,2},{2,3},{5,4},{6,5},{7,6},{8,9},{9,10},{10,11},{13,12},{... | collective-permute-start | bytes 3145736 | tf_op jit(solution)/shard_map/ppermute | solution.py:429
  67.3 4.0 %copy-start = (bf16[512,128]{1,0:T(8,128)(2,1)S(1)}, bf16[512,128]{1,0:T(8,128)(2,1)}, u32[]{:S(2)}) copy-start(bf16[512,128]{1,0:T(8,128)(2,1)} %shard_map.107.refs_0_) | copy-start | bytes 393220
  69.4 21.9 %collective-permute-start.7 = (bf16[256,2048]{1,0:T(8,128)(2,1)}, bf16[256,2048]{1,0:T(8,128)(2,1)}, u32[]{:S(2)}, u32[]{:S(2)}) collective-permute-start(bf16[256,2048]{1,0:T(8,128)(2,1)} %shard_map.110), channel_id=1, source_target_pairs={{1,0},{2,1},{3,2},{4,5},{5,6},{6,7},{9,8},{10,9},{11,10},{12,13},{... | collective-permute-start | bytes 3145736 | tf_op jit(solution)/shard_map/ppermute | solution.py:429
  78.8 31.4 %all-to-all-start.1 = ((bf16[4,128,2048]{2,1,0:T(8,128)(2,1)}), bf16[4,128,2048]{2,1,0:T(8,128)(2,1)}, u32[]{:S(2)}, u32[]{:S(2)}) async-start(bf16[4,128,2048]{2,1,0:T(8,128)(2,1)} %get-tuple-element.53), calls=%async_computation.1 | async-start | bytes 4194304 | tf_op jit(solution)/shard_map/all_to_all | solution.py:27
  83.2 11.6 %collective-permute-start.12 = (bf16[512,2048]{1,0:T(8,128)(2,1)}, bf16[512,2048]{1,0:T(8,128)(2,1)}, u32[]{:S(2)}, u32[]{:S(2)}) collective-permute-start(bf16[512,2048]{1,0:T(8,128)(2,1)} %get-tuple-element.45), channel_id=1, source_target_pairs={{0,4},{4,0},{8,12},{12,8},{16,20},{20,16},{24,28},{28,24},{1,5},{5... | collective-permute-start | bytes 6291464 | tf_op jit(solution)/shard_map/ppermute | solution.py:23
  85.7 27.1 %collective-permute-start.13 = (bf16[256,2048]{1,0:T(8,128)(2,1)}, bf16[256,2048]{1,0:T(8,128)(2,1)}, u32[]{:S(2)}, u32[]{:S(2)}) collective-permute-start(bf16[256,2048]{1,0:T(8,128)(2,1)} %shard_map.112), channel_id=1, source_target_pairs={{0,1},{1,2},{2,3},{5,4},{6,5},{7,6},{8,9},{9,10},{10,11},{13,12},{... | collective-permute-start | bytes 3145736 | tf_op jit(solution)/shard_map/ppermute | solution.py:429
  93.3 20.5 %collective-permute-start.14 = (bf16[256,2048]{1,0:T(8,128)(2,1)}, bf16[256,2048]{1,0:T(8,128)(2,1)}, u32[]{:S(2)}, u32[]{:S(2)}) collective-permute-start(bf16[256,2048]{1,0:T(8,128)(2,1)} %shard_map.113), channel_id=1, source_target_pairs={{1,0},{2,1},{3,2},{4,5},{5,6},{6,7},{9,8},{10,9},{11,10},{12,13},{... | collective-permute-start | bytes 3145736 | tf_op jit(solution)/shard_map/ppermute | solution.py:429

commit v8 on v5

--- a/solution.py
+++ b/solution.py
@@ -112,9 +112,8 @@
             self.start(1)
 
 
-def backward_blocks(y, w, done, out, stream, size, sem):
+def backward_blocks(y, w, done, out, stream, size, coarse, sem):
     blocks = done.shape[0]
-    coarse = 2 if size % 512 == 0 else 1
     tile = size // coarse
     outs = []
     for b in range(blocks):
@@ -130,13 +129,14 @@
     rows, width = dY.shape
     size = W.shape[0] // n
     blocks = len(columns)
+    coarse = 1 if size % 512 else 2 if blocks > 1 else 4
 
     def kernel(spot, dY, W, out, y, w, done, sem, out_sem, y_sem):
         ready = fetch([(dY, y)], y_sem)
         ins = Stream(W, w, [look_up(spot, table, c) for c in columns], size, sem)
-        ins.start(4)
+        ins.start(4 if blocks > 1 else 2)
         wait(ready)
-        wait(backward_blocks(y[...], w, done, out, ins, size, out_sem))
+        wait(backward_blocks(y[...], w, done, out, ins, size, coarse, out_sem))
 
     return call(
         kernel,
@@ -145,7 +145,7 @@
         [HBM, HBM],
         HBM,
         array(blocks, rows, size),
-        [vmem(rows, width), vmem(blocks * size, width), vmem(blocks, rows, size), sems(4 * blocks), sems(2 * blocks), sems(1)],
+        [vmem(rows, width), vmem(blocks * size, width), vmem(blocks, rows, size), sems(4 * blocks), sems(4 * blocks), sems(1)],
     )(spot, *far(dY, W))
 
 
@@ -336,7 +336,7 @@
         low = pick(x, downs)
         wait(more)
         part[...] = jnp.concatenate([low, pick(y, ups)], axis=1).astype(bf16)
-        wait(fetch([(part, out.at[k]) for k in range(n)], sem, 4 + 2 * half))
+        wait(fetch([(part, out)], sem, 4 + 2 * half))
 
     return call(
         kernel,
@@ -344,24 +344,25 @@
         2,
         [ids_spec(rows)] * 2 + [HBM] * 5,
         HBM,
-        array(n, 2 * rows, 2 * rank),
+        array(2 * rows, 2 * rank),
         [vmem(2 * rows, width)] * 2
         + [vmem(half * rank, width)] * 2
         + [vmem(2 * rows, 2 * rank), sems(4 + 2 * half + n)],
     )(spot, slots, *ids, *far(*Xs, *dYs, gathered))
 
 
-def adapters(spot, slots, ids, parts, Xs, dYs, gathered, rank):
+def adapters(spot, slots, ids, few, Xs, dYs, gathered, rank):
     rows, width = Xs[0].shape
     half = gathered.shape[0]
 
-    def kernel(spot, slots, id0, id1, parts, X, X_other, dY, dY_other, gathered, out, term, back, other, *scratch):
+    def kernel(spot, slots, id0, id1, *refs):
+        parts, (X, X_other, dY, dY_other, gathered, out, term, back, other, *scratch) = refs[: len(few)], refs[len(few) :]
         x, y, downs, ups, grads, terms, sem, out_sem = scratch
         ins = fetch(
             rows_of((X, X_other), (dY, dY_other), x, y, rows) + pieces(gathered, downs, ups, rank), sem
         )
         chosen = chosen_of(spot, slots, (id0, id1), rank, half)
-        total = sum(parts[k].astype(f32) for k in range(parts.shape[0]))
+        total = sum(p[...].astype(f32) for p in parts)
         low, grad = total[:, :rank].astype(bf16), (adapter_scale * total[:, rank:]).astype(bf16)
         zero = jnp.zeros((), bf16)
         low, grad = [jnp.where(chosen, jnp.concatenate([v] * half, axis=1), zero) for v in (low, grad)]
@@ -386,7 +387,7 @@
         kernel,
         (1,),
         2,
-        [ids_spec(rows)] * 2 + [pl.BlockSpec(memory_space=pltpu.VMEM)] + [HBM] * 5,
+        [ids_spec(rows)] * 2 + [pl.BlockSpec(memory_space=pltpu.VMEM)] * len(few) + [HBM] * 5,
         [HBM] * 4,
         [array(half, 2 * rank, width), array(rows, width), array(rows, width), array(2 * rows, width)],
         [vmem(2 * rows, width)] * 2
@@ -394,7 +395,7 @@
         + [vmem(half, 2 * rank, width), vmem(2, 2 * rows, width), sems(4 + 2 * half), sems(5)],
         mib=60,
         cost=GRADS,
-    )(spot, slots, *ids, pltpu.with_memory_space_constraint(parts, pltpu.VMEM), *far(*Xs, *dYs, gathered))
+    )(spot, slots, *ids, *[pltpu.with_memory_space_constraint(p, pltpu.VMEM) for p in few], *far(*Xs, *dYs, gathered))
 
 
 def body(X, dY, W, A, B, adapter_rows, adapter_slot):
@@ -456,7 +457,7 @@
     backs.append(backward(spot, table, second, after(dY, last), W, n))
     gathered = after(gathered, backs[1])
     part = low_parts(spot, adapter_slot, ids, Xs, dYs, gathered, rank, n)
-    parts = swap(part, "tensor", None)
+    parts = [part] + [exchange(part, "tensor", k) for k in range(1, n)]
 
     last = part
     for s in range(2, n):
@@ -466,7 +467,7 @@
             last = own_back
         last = onward(s, 1, last)
         if s == 2:
-            parts = after(parts, last)
+            parts = [after(p, last) for p in parts]
             mine, term, back_term, send = adapters(spot, adapter_slot, ids, parts, Xs, dYs, gathered, rank)
             arriving = swap(mine, "dp", chips)
             other = exchange(send, "dp", 1)

time: 121 us -> 120 us (level); the launches traced: 120 us -> 118 us
    all_to_all x3 -> x2, starting transfers between devices: 15.3 us -> 8.89 us  [swap(): return lax.all_to_all(x, axis, 0, 0, axis_index_groups=groups, tiled=True)]
    ppermute x4 -> x7, starting transfers between devices: 1.1 us -> 6.93 us  [exchange(): return lax.ppermute(x, axis, [(i, i ^ offset) for i in range(size)])]
  transfers between devices with their start and end apart: 15 -> 17, of which waited for: 1 -> 3; matrix products, arithmetic and copies ran while one was open for 0% -> 0% of each run, Pallas kernels for 56% -> 57%
where the time goes in v8:
time: 120 us; the launch traced here: 118 us
  Pallas kernels  70.7 us (59%)
  starting transfers between devices  41.9 us (35%)
  waiting for transfers between devices  4.21 us (4%)
    ppermute x8, starting transfers between devices, along(): return lax.ppermute(x, ('dp', 'tensor'), pairs[k])  26.1 us
    pallas_call x3, Pallas kernels, backward(): call(kernel, (1,), 1, [HBM, HBM], HBM, array(blocks, rows, size), [vmem(r...  21.6 us
    pallas_call x1, Pallas kernels, forward(): call(kernel, (1,), 1, [HBM] * (len(arrays) + 5), [HBM] * 2, [array(rows,...  15.4 us
    pallas_call x6, Pallas kernels, add_on(): call(kernel, (1,), 1, [HBM] * (1 + len(backs)), HBM, array(rows, width),...  13.2 us
    all_to_all x2, starting transfers between devices, swap(): return lax.all_to_all(x, axis, 0, 0, axis_index_groups=groups, tiled=True)  8.89 us
    pallas_call x1, Pallas kernels, adapters(): call(kernel, (1,), 2, [ids_spec(rows)] * 2 + [pl.BlockSpec(memory_space=p...  7.43 us
    ppermute x7, starting transfers between devices, exchange(): return lax.ppermute(x, axis, [(i, i ^ offset) for i in range(size)])  6.93 us
    pallas_call x1, Pallas kernels, low_parts(): call(kernel, (1,), 2, [ids_spec(rows)] * 2 + [HBM] * 5, HBM, array(2 * ro...  6.73 us
  transfers between devices with their start and end apart: 17, of which 3 were waited for; matrix products, arithmetic and copies ran while one was open for 0% of the time, Pallas kernels for 57%

profile of v8, /device:TPU:0, one launch (start us, length us, event | category | flops | bytes accessed | tf_op | source)
XLA Modules:
  0.0 117.9 jit_solution(10217839644772579978)
XLA Ops:
  0.6 0.5 collective-permute-start
  1.1 0.1 collective-permute-start.1
  1.2 0.4 collective-permute-start.2
  1.7 5.5 %collective-permute-start.4 = (bf16[256,2048]{1,0:T(8,128)(2,1)}, bf16[256,2048]{1,0:T(8,128)(2,1)}, u32[]{:S(2)}, u32[]{:S(2)}) collective-permute-start(bf16[256,2048]{1,0:T(8,128)(2,1)} %refs_0_), channel_id=1, source_target_pairs={{0,1},{1,2},{2,3},{5,4},{6,5},{7,6},{8,9},{9,10},{10,11},{13,12},{... | collective-permute-start | bytes 3145736 | tf_op jit(solution)/shard_map/ppermute | solution.py:414
  7.2 0.0 collective-permute-done.2
  7.2 0.0 copy-start.1
  7.2 0.0 collective-permute-done.X_other.refs_5_
  7.2 0.0 collective-permute-done.1.dY_other.refs_7_
  7.2 2.4 %shard_map.102 = bf16[4,128,2048]{2,1,0:T(8,128)(2,1)} custom-call(bf16[64,2048]{1,0:T(8,128)(2,1)} %bitcast.11, bf16[64,2048]{1,0:T(8,128)(2,1)} %bitcast.12), custom_call_target="tpu_custom_call" | custom-call | flops 1000 | bytes 1 | tf_op jit(solution)/shard_map/pallas_call | solution.py:88
  9.6 1.3 %collective-permute-start.3 = (bf16[256,2048]{1,0:T(8,128)(2,1)}, bf16[256,2048]{1,0:T(8,128)(2,1)}, u32[]{:S(2)}, u32[]{:S(2)}) collective-permute-start(bf16[256,2048]{1,0:T(8,128)(2,1)} %refs_0_), channel_id=1, source_target_pairs={{1,0},{2,1},{3,2},{4,5},{5,6},{6,7},{9,8},{10,9},{11,10},{12,13},{... | collective-permute-start | bytes 3145736 | tf_op jit(solution)/shard_map/ppermute | solution.py:414
  10.9 0.0 copy-done.1
  10.9 4.4 %all-to-all-start = ((bf16[4,128,2048]{2,1,0:T(8,128)(2,1)}), bf16[4,128,2048]{2,1,0:T(8,128)(2,1)}, u32[]{:S(2)}, u32[]{:S(2)}) async-start(bf16[4,128,2048]{2,1,0:T(8,128)(2,1)} %shard_map.102), calls=%async_computation | async-start | bytes 4194304 | tf_op jit(solution)/shard_map/all_to_all | solution.py:27
  15.4 9.5 %shard_map.103.refs_0_ = bf16[2,256,2048]{2,1,0:T(8,128)(2,1)} custom-call(s32[1]{0:T(128)} %bitcast.spot, bf16[256,2048]{1,0:T(8,128)(2,1)} %refs_6_.1, bf16[8192,2048]{1,0:T(8,128)(2,1)} %refs_7_.1), custom_call_target="tpu_custom_call" | custom-call | flops 1000 | bytes 1 | tf_op jit(solution)/shard_map/pallas_call | solution.py:141
  24.9 0.0 collective-permute-done.4.arrived.refs_1_
  24.9 2.4 %shard_map.104 = bf16[256,2048]{1,0:T(8,128)(2,1)} custom-call(s32[1]{0:T(128)} %bitcast.spot, bf16[256,2048]{1,0:T(8,128)(2,1)} %collective-permute-done.4.arrived.refs_1_, bf16[2,256,2048]{2,1,0:T(8,128)(2,1)} %shard_map.103.refs_0_), custom_call_target="tpu_custom_call" | custom-call | flops 1000 | bytes 1 | tf_op jit(solution)/shard_map/pallas_call | solution.py:183
  27.3 5.3 %collective-permute-start.6 = (bf16[256,2048]{1,0:T(8,128)(2,1)}, bf16[256,2048]{1,0:T(8,128)(2,1)}, u32[]{:S(2)}, u32[]{:S(2)}) collective-permute-start(bf16[256,2048]{1,0:T(8,128)(2,1)} %shard_map.104), channel_id=1, source_target_pairs={{0,1},{1,2},{2,3},{5,4},{6,5},{7,6},{8,9},{9,10},{10,11},{13,12},{... | collective-permute-start | bytes 3145736 | tf_op jit(solution)/shard_map/ppermute | solution.py:414
  32.6 0.0 collective-permute-done.3.arrived.refs_6_
  32.6 2.0 %shard_map.105 = bf16[256,2048]{1,0:T(8,128)(2,1)} custom-call(s32[1]{0:T(128)} %bitcast.spot, bf16[256,2048]{1,0:T(8,128)(2,1)} %collective-permute-done.3.arrived.refs_6_, bf16[2,256,2048]{2,1,0:T(8,128)(2,1)} %shard_map.103.refs_0_), custom_call_target="tpu_custom_call" | custom-call | flops 10000000000 | bytes 1 | tf_op jit(solution)/shard_map/pallas_call | solution.py:183
  34.6 1.3 %collective-permute-start.5 = (bf16[256,2048]{1,0:T(8,128)(2,1)}, bf16[256,2048]{1,0:T(8,128)(2,1)}, u32[]{:S(2)}, u32[]{:S(2)}) collective-permute-start(bf16[256,2048]{1,0:T(8,128)(2,1)} %shard_map.105), channel_id=1, source_target_pairs={{1,0},{2,1},{3,2},{4,5},{5,6},{6,7},{9,8},{10,9},{11,10},{12,13},{... | collective-permute-start | bytes 3145736 | tf_op jit(solution)/shard_map/ppermute | solution.py:414
  35.9 6.0 %shard_map.106.refs_1_ = bf16[1,256,2048]{2,1,0:T(8,128)(2,1)} custom-call(s32[1]{0:T(128)} %bitcast.spot, bf16[256,2048]{1,0:T(8,128)(2,1)} %refs_6_.1, bf16[8192,2048]{1,0:T(8,128)(2,1)} %refs_7_.1), custom_call_target="tpu_custom_call" | custom-call | flops 1000 | bytes 1 | tf_op jit(solution)/shard_map/pallas_call | solution.py:141
  41.9 0.0 all-to-all-done.gathered.refs_8_
  42.0 6.7 %shard_map.107.refs_0_ = bf16[512,128]{1,0:T(8,128)(2,1)} custom-call(s32[1]{0:T(128)} %bitcast.spot, s32[8]{0:T(128)} %slots.3, s32[1,256]{1,0:T(1,128)} %bitcast.13, s32[1,256]{1,0:T(1,128)} %bitcast.15, bf16[256,2048]{1,0:T(8,128)(2,1)} %refs_0_, bf16[256,2048]{1,0:T(8,128)(2,1)} %collective-permute-done.X_other.refs_5_, bf16[256,2048]{1,0:T(8,128)(2,1)} %refs_6_.1, ...), custom_call_target="tpu_custom_call" | custom-call | flops 1000 | bytes 1 | tf_op jit(solution)/shard_map/pallas_call | solution.py:341
  48.7 5.2 %collective-permute-start.11 = (bf16[512,128]{1,0:T(8,128)(2,1)}, bf16[512,128]{1,0:T(8,128)(2,1)S(1)}, u32[]{:S(2)}, u32[]{:S(2)}) collective-permute-start(bf16[512,128]{1,0:T(8,128)(2,1)} %shard_map.107.refs_0_), channel_id=1, source_target_pairs={{0,3},{1,2},{2,1},{3,0},{4,7},{5,6},{6,5},{7,4},{8,11},{9,10},{10,... | collective-permute-start | bytes 393224 | tf_op jit(solution)/shard_map/ppermute | solution.py:23
  53.9 0.0 collective-permute-start.10
  53.9 0.6 collective-permute-start.9
  54.5 0.0 collective-permute-done.6.arrived.refs_3_
  54.5 2.4 %shard_map.108 = bf16[256,2048]{1,0:T(8,128)(2,1)} custom-call(s32[1]{0:T(128)} %bitcast.spot, bf16[256,2048]{1,0:T(8,128)(2,1)} %collective-permute-done.6.arrived.refs_3_, bf16[2,256,2048]{2,1,0:T(8,128)(2,1)} %shard_map.103.refs_0_, bf16[1,256,2048]{2,1,0:T(8,128)(2,1)} %shard_map.106.refs_1_), custom_call_target="tpu_custom_call" | custom-call | flops 1000 | bytes 1 | tf_op jit(solution)/shard_map/pallas_call | solution.py:183
  56.9 4.3 %collective-permute-start.8 = (bf16[256,2048]{1,0:T(8,128)(2,1)}, bf16[256,2048]{1,0:T(8,128)(2,1)}, u32[]{:S(2)}, u32[]{:S(2)}) collective-permute-start(bf16[256,2048]{1,0:T(8,128)(2,1)} %shard_map.108), channel_id=1, source_target_pairs={{0,1},{1,2},{2,3},{5,4},{6,5},{7,6},{8,9},{9,10},{10,11},{13,12},{... | collective-permute-start | bytes 3145736 | tf_op jit(solution)/shard_map/ppermute | solution.py:414
  61.2 6.0 %shard_map.109.refs_11_ = bf16[1,256,2048]{2,1,0:T(8,128)(2,1)} custom-call(s32[1]{0:T(128)} %bitcast.spot, bf16[256,2048]{1,0:T(8,128)(2,1)} %refs_6_.1, bf16[8192,2048]{1,0:T(8,128)(2,1)} %refs_7_.1), custom_call_target="tpu_custom_call" | custom-call | flops 1000 | bytes 1 | tf_op jit(solution)/shard_map/pallas_call | solution.py:141
  67.2 0.0 copy-start
  67.2 0.0 collective-permute-done.5.arrived.refs_4_
  67.2 2.1 %shard_map.110 = bf16[256,2048]{1,0:T(8,128)(2,1)} custom-call(s32[1]{0:T(128)} %bitcast.spot, bf16[256,2048]{1,0:T(8,128)(2,1)} %collective-permute-done.5.arrived.refs_4_, bf16[2,256,2048]{2,1,0:T(8,128)(2,1)} %shard_map.103.refs_0_, bf16[1,256,2048]{2,1,0:T(8,128)(2,1)} %shard_map.106.refs_1_), custom_call_target="tpu_custom_call" | custom-call | flops 1000 | bytes 1 | tf_op jit(solution)/shard_map/pallas_call | solution.py:183
  69.3 1.3 %collective-permute-start.7 = (bf16[256,2048]{1,0:T(8,128)(2,1)}, bf16[256,2048]{1,0:T(8,128)(2,1)}, u32[]{:S(2)}, u32[]{:S(2)}) collective-permute-start(bf16[256,2048]{1,0:T(8,128)(2,1)} %shard_map.110), channel_id=1, source_target_pairs={{1,0},{2,1},{3,2},{4,5},{5,6},{6,7},{9,8},{10,9},{11,10},{12,13},{... | collective-permute-start | bytes 3145736 | tf_op jit(solution)/shard_map/ppermute | solution.py:414
  70.6 0.0 collective-permute-done.11.refs_3_
  70.6 0.6 collective-permute-done.10.refs_2_
  71.2 0.0 collective-permute-done.9.refs_1_
  71.2 0.0 copy-done
  71.3 7.4 %shard_map.111 = (bf16[4,128,2048]{2,1,0:T(8,128)(2,1)}, bf16[256,2048]{1,0:T(8,128)(2,1)}, bf16[256,2048]{1,0:T(8,128)(2,1)}, bf16[512,2048]{1,0:T(8,128)(2,1)}) custom-call(s32[1]{0:T(128)} %bitcast.spot, s32[8]{0:T(128)} %slots.3, s32[1,256]{1,0:T(1,128)} %bitcast.14, s32[1,256]{1,0:T(1,128)} %bitcast.16, bf16[512,128]{1,0:T(8,128)(2,1)S(1)} %copy-done, ...), custom_call_target="tpu_custom_call" | custom-call | flops 10000000000 | bytes 1 | tf_op jit(solution)/shard_map/pallas_call | solution.py:386
  78.7 4.4 %all-to-all-start.1 = ((bf16[4,128,2048]{2,1,0:T(8,128)(2,1)}), bf16[4,128,2048]{2,1,0:T(8,128)(2,1)}, u32[]{:S(2)}, u32[]{:S(2)}) async-start(bf16[4,128,2048]{2,1,0:T(8,128)(2,1)} %get-tuple-element.52), calls=%async_computation.1 | async-start | bytes 4194304 | tf_op jit(solution)/shard_map/all_to_all | solution.py:27
  83.1 0.1 collective-permute-start.12
  83.2 0.0 collective-permute-done.8.arrived.refs_5_
  83.2 2.4 %shard_map.112 = bf16[256,2048]{1,0:T(8,128)(2,1)} custom-call(s32[1]{0:T(128)} %bitcast.spot, bf16[256,2048]{1,0:T(8,128)(2,1)} %collective-permute-done.8.arrived.refs_5_, bf16[2,256,2048]{2,1,0:T(8,128)(2,1)} %shard_map.103.refs_0_, bf16[1,256,2048]{2,1,0:T(8,128)(2,1)} %shard_map.106.refs_1_), custom_call_target="tpu_custom_call" | custom-call | flops 999999995904 | bytes 1 | tf_op jit(solution)/shard_map/pallas_call | solution.py:183
  85.6 5.6 %collective-permute-start.13 = (bf16[256,2048]{1,0:T(8,128)(2,1)}, bf16[256,2048]{1,0:T(8,128)(2,1)}, u32[]{:S(2)}, u32[]{:S(2)}) collective-permute-start(bf16[256,2048]{1,0:T(8,128)(2,1)} %shard_map.112), channel_id=1, source_target_pairs={{0,1},{1,2},{2,3},{5,4},{6,5},{7,6},{8,9},{9,10},{10,11},{13,12},{... | collective-permute-start | bytes 3145736 | tf_op jit(solution)/shard_map/ppermute | solution.py:414
  91.2 0.0 collective-permute-done.7.arrived.refs_2_
  91.2 2.0 %shard_map.113 = bf16[256,2048]{1,0:T(8,128)(2,1)} custom-call(s32[1]{0:T(128)} %bitcast.spot, bf16[256,2048]{1,0:T(8,128)(2,1)} %collective-permute-done.7.arrived.refs_2_, bf16[2,256,2048]{2,1,0:T(8,128)(2,1)} %shard_map.103.refs_0_, bf16[1,256,2048]{2,1,0:T(8,128)(2,1)} %shard_map.106.refs_1_), custom_call_target="tpu_custom_call" | custom-call | flops 999999995904 | bytes 1 | tf_op jit(solution)/shard_map/pallas_call | solution.py:183
  93.2 1.5 %collective-permute-start.14 = (bf16[256,2048]{1,0:T(8,128)(2,1)}, bf16[256,2048]{1,0:T(8,128)(2,1)}, u32[]{:S(2)}, u32[]{:S(2)}) collective-permute-start(bf16[256,2048]{1,0:T(8,128)(2,1)} %shard_map.113), channel_id=1, source_target_pairs={{1,0},{2,1},{3,2},{4,5},{5,6},{6,7},{9,8},{10,9},{11,10},{12,13},{... | collective-permute-start | bytes 3145736 | tf_op jit(solution)/shard_map/ppermute | solution.py:414
  94.8 0.0 collective-permute-done.12.refs_10_
  94.8 15.4 %shard_map.114 = (bf16[256,2048]{1,0:T(8,128)(2,1)}, bf16[256,2048]{1,0:T(8,128)(2,1)}) custom-call(s32[1]{0:T(128)} %bitcast.spot, bf16[256,2048]{1,0:T(8,128)(2,1)} %refs_0_, bf16[256,2048]{1,0:T(8,128)(2,1)} %collective-permute-done.4.arrived.refs_1_, bf16[256,2048]{1,0:T(8,128)(2,1)} %collective-permute-done.7.arrived.refs_2_, ...), custom_call_target="tpu_custom_call" | custom-call | flops 1000 | bytes 1 | tf_op jit(solution)/shard_map/pallas_call | solution.py:277
  110.1 0.0 all-to-all-done.1.blocks
  110.1 0.5 collective-permute-done.13.one
  110.7 3.0 %collective-permute-done.14.two = bf16[256,2048]{1,0:T(8,128)(2,1)} collective-permute-done((bf16[256,2048]{1,0:T(8,128)(2,1)}, bf16[256,2048]{1,0:T(8,128)(2,1)}, u32[]{:S(2)}, u32[]{:S(2)}) %collective-permute-start.14) | collective-permute-done | bytes 1048608 | tf_op jit(solution)/shard_map/ppermute | solution.py:414
  113.7 4.1 %shard_map.115 = (bf16[256,2048]{1,0:T(8,128)(2,1)}, bf16[64,2048]{1,0:T(8,128)(2,1)}, bf16[64,2048]{1,0:T(8,128)(2,1)}) custom-call(bf16[256,2048]{1,0:T(8,128)(2,1)} %collective-permute-done.13.one, bf16[256,2048]{1,0:T(8,128)(2,1)} %collective-permute-done.14.two, bf16[256,2048]{1,0:T(8,128)(2,1)} %get-tuple-element.51.rest, ...), custom_call_target="tpu_custom_call" | custom-call | flops 1000 | bytes 1 | tf_op jit(solution)/shard_map/pallas_call | solution.py:220
Async XLA Ops:
  0.6 6.6 %collective-permute-start = (bf16[256,2048]{1,0:T(8,128)(2,1)}, bf16[256,2048]{1,0:T(8,128)(2,1)}, u32[]{:S(2)}, u32[]{:S(2)}) collective-permute-start(bf16[256,2048]{1,0:T(8,128)(2,1)} %refs_0_), channel_id=1, source_target_pairs={{0,4},{4,0},{8,12},{12,8},{16,20},{20,16},{24,28},{28,24},{1,5},{5... | collective-permute-start | bytes 3145736 | tf_op jit(solution)/shard_map/ppermute | solution.py:23
  1.1 6.1 %collective-permute-start.1 = (bf16[256,2048]{1,0:T(8,128)(2,1)}, bf16[256,2048]{1,0:T(8,128)(2,1)}, u32[]{:S(2)}, u32[]{:S(2)}) collective-permute-start(bf16[256,2048]{1,0:T(8,128)(2,1)} %refs_6_.1), channel_id=1, source_target_pairs={{0,4},{4,0},{8,12},{12,8},{16,20},{20,16},{24,28},{28,24},{1,5},{5... | collective-permute-start | bytes 3145736 | tf_op jit(solution)/shard_map/ppermute | solution.py:23
  1.2 6.0 %collective-permute-start.2 = (s32[256,1]{0,1:T(1,128)}, s32[256,1]{0,1:T(1,128)S(1)}, u32[]{:S(2)}, u32[]{:S(2)}) collective-permute-start(s32[256,1]{0,1:T(1,128)} %param.12), channel_id=1, source_target_pairs={{0,4},{4,0},{8,12},{12,8},{16,20},{20,16},{24,28},{28,24},{1,5},{5... | collective-permute-start | bytes 3080 | tf_op jit(solution)/shard_map/ppermute | solution.py:23
  1.7 23.3 %collective-permute-start.4 = (bf16[256,2048]{1,0:T(8,128)(2,1)}, bf16[256,2048]{1,0:T(8,128)(2,1)}, u32[]{:S(2)}, u32[]{:S(2)}) collective-permute-start(bf16[256,2048]{1,0:T(8,128)(2,1)} %refs_0_), channel_id=1, source_target_pairs={{0,1},{1,2},{2,3},{5,4},{6,5},{7,6},{8,9},{9,10},{10,11},{13,12},{... | collective-permute-start | bytes 3145736 | tf_op jit(solution)/shard_map/ppermute | solution.py:414
  7.2 3.7 %copy-start.1 = (s32[256,1]{0,1:T(1,128)}, s32[256,1]{0,1:T(1,128)S(1)}, u32[]{:S(2)}) copy-start(s32[256,1]{0,1:T(1,128)S(1)} %collective-permute-done.2) | copy-start | bytes 3076
  9.6 23.0 %collective-permute-start.3 = (bf16[256,2048]{1,0:T(8,128)(2,1)}, bf16[256,2048]{1,0:T(8,128)(2,1)}, u32[]{:S(2)}, u32[]{:S(2)}) collective-permute-start(bf16[256,2048]{1,0:T(8,128)(2,1)} %refs_0_), channel_id=1, source_target_pairs={{1,0},{2,1},{3,2},{4,5},{5,6},{6,7},{9,8},{10,9},{11,10},{12,13},{... | collective-permute-start | bytes 3145736 | tf_op jit(solution)/shard_map/ppermute | solution.py:414
  10.9 31.0 %all-to-all-start = ((bf16[4,128,2048]{2,1,0:T(8,128)(2,1)}), bf16[4,128,2048]{2,1,0:T(8,128)(2,1)}, u32[]{:S(2)}, u32[]{:S(2)}) async-start(bf16[4,128,2048]{2,1,0:T(8,128)(2,1)} %shard_map.102), calls=%async_computation | async-start | bytes 4194304 | tf_op jit(solution)/shard_map/all_to_all | solution.py:27
  27.3 27.2 %collective-permute-start.6 = (bf16[256,2048]{1,0:T(8,128)(2,1)}, bf16[256,2048]{1,0:T(8,128)(2,1)}, u32[]{:S(2)}, u32[]{:S(2)}) collective-permute-start(bf16[256,2048]{1,0:T(8,128)(2,1)} %shard_map.104), channel_id=1, source_target_pairs={{0,1},{1,2},{2,3},{5,4},{6,5},{7,6},{8,9},{9,10},{10,11},{13,12},{... | collective-permute-start | bytes 3145736 | tf_op jit(solution)/shard_map/ppermute | solution.py:414
  34.6 32.6 %collective-permute-start.5 = (bf16[256,2048]{1,0:T(8,128)(2,1)}, bf16[256,2048]{1,0:T(8,128)(2,1)}, u32[]{:S(2)}, u32[]{:S(2)}) collective-permute-start(bf16[256,2048]{1,0:T(8,128)(2,1)} %shard_map.105), channel_id=1, source_target_pairs={{1,0},{2,1},{3,2},{4,5},{5,6},{6,7},{9,8},{10,9},{11,10},{12,13},{... | collective-permute-start | bytes 3145736 | tf_op jit(solution)/shard_map/ppermute | solution.py:414
  48.7 21.9 %collective-permute-start.11 = (bf16[512,128]{1,0:T(8,128)(2,1)}, bf16[512,128]{1,0:T(8,128)(2,1)S(1)}, u32[]{:S(2)}, u32[]{:S(2)}) collective-permute-start(bf16[512,128]{1,0:T(8,128)(2,1)} %shard_map.107.refs_0_), channel_id=1, source_target_pairs={{0,3},{1,2},{2,1},{3,0},{4,7},{5,6},{6,5},{7,4},{8,11},{9,10},{10,... | collective-permute-start | bytes 393224 | tf_op jit(solution)/shard_map/ppermute | solution.py:23
  53.9 17.4 %collective-permute-start.10 = (bf16[512,128]{1,0:T(8,128)(2,1)}, bf16[512,128]{1,0:T(8,128)(2,1)S(1)}, u32[]{:S(2)}, u32[]{:S(2)}) collective-permute-start(bf16[512,128]{1,0:T(8,128)(2,1)} %shard_map.107.refs_0_), channel_id=1, source_target_pairs={{0,2},{1,3},{2,0},{3,1},{4,6},{5,7},{6,4},{7,5},{8,10},{9,11},{10,... | collective-permute-start | bytes 393224 | tf_op jit(solution)/shard_map/ppermute | solution.py:23
  53.9 17.4 %collective-permute-start.9 = (bf16[512,128]{1,0:T(8,128)(2,1)}, bf16[512,128]{1,0:T(8,128)(2,1)S(1)}, u32[]{:S(2)}, u32[]{:S(2)}) collective-permute-start(bf16[512,128]{1,0:T(8,128)(2,1)} %shard_map.107.refs_0_), channel_id=1, source_target_pairs={{0,1},{1,0},{2,3},{3,2},{4,5},{5,4},{6,7},{7,6},{8,9},{9,8},{10,11... | collective-permute-start | bytes 393224 | tf_op jit(solution)/shard_map/ppermute | solution.py:23
  56.9 26.3 %collective-permute-start.8 = (bf16[256,2048]{1,0:T(8,128)(2,1)}, bf16[256,2048]{1,0:T(8,128)(2,1)}, u32[]{:S(2)}, u32[]{:S(2)}) collective-permute-start(bf16[256,2048]{1,0:T(8,128)(2,1)} %shard_map.108), channel_id=1, source_target_pairs={{0,1},{1,2},{2,3},{5,4},{6,5},{7,6},{8,9},{9,10},{10,11},{13,12},{... | collective-permute-start | bytes 3145736 | tf_op jit(solution)/shard_map/ppermute | solution.py:414
  67.2 4.0 %copy-start = (bf16[512,128]{1,0:T(8,128)(2,1)S(1)}, bf16[512,128]{1,0:T(8,128)(2,1)}, u32[]{:S(2)}) copy-start(bf16[512,128]{1,0:T(8,128)(2,1)} %shard_map.107.refs_0_) | copy-start | bytes 393220
  69.3 21.9 %collective-permute-start.7 = (bf16[256,2048]{1,0:T(8,128)(2,1)}, bf16[256,2048]{1,0:T(8,128)(2,1)}, u32[]{:S(2)}, u32[]{:S(2)}) collective-permute-start(bf16[256,2048]{1,0:T(8,128)(2,1)} %shard_map.110), channel_id=1, source_target_pairs={{1,0},{2,1},{3,2},{4,5},{5,6},{6,7},{9,8},{10,9},{11,10},{12,13},{... | collective-permute-start | bytes 3145736 | tf_op jit(solution)/shard_map/ppermute | solution.py:414
  78.7 31.4 %all-to-all-start.1 = ((bf16[4,128,2048]{2,1,0:T(8,128)(2,1)}), bf16[4,128,2048]{2,1,0:T(8,128)(2,1)}, u32[]{:S(2)}, u32[]{:S(2)}) async-start(bf16[4,128,2048]{2,1,0:T(8,128)(2,1)} %get-tuple-element.52), calls=%async_computation.1 | async-start | bytes 4194304 | tf_op jit(solution)/shard_map/all_to_all | solution.py:27
  83.1 11.6 %collective-permute-start.12 = (bf16[512,2048]{1,0:T(8,128)(2,1)}, bf16[512,2048]{1,0:T(8,128)(2,1)}, u32[]{:S(2)}, u32[]{:S(2)}) collective-permute-start(bf16[512,2048]{1,0:T(8,128)(2,1)} %get-tuple-element.44), channel_id=1, source_target_pairs={{0,4},{4,0},{8,12},{12,8},{16,20},{20,16},{24,28},{28,24},{1,5},{5... | collective-permute-start | bytes 6291464 | tf_op jit(solution)/shard_map/ppermute | solution.py:23
  85.6 25.0 %collective-permute-start.13 = (bf16[256,2048]{1,0:T(8,128)(2,1)}, bf16[256,2048]{1,0:T(8,128)(2,1)}, u32[]{:S(2)}, u32[]{:S(2)}) collective-permute-start(bf16[256,2048]{1,0:T(8,128)(2,1)} %shard_map.112), channel_id=1, source_target_pairs={{0,1},{1,2},{2,3},{5,4},{6,5},{7,6},{8,9},{9,10},{10,11},{13,12},{... | collective-permute-start | bytes 3145736 | tf_op jit(solution)/shard_map/ppermute | solution.py:414
  93.2 20.4 %collective-permute-start.14 = (bf16[256,2048]{1,0:T(8,128)(2,1)}, bf16[256,2048]{1,0:T(8,128)(2,1)}, u32[]{:S(2)}, u32[]{:S(2)}) collective-permute-start(bf16[256,2048]{1,0:T(8,128)(2,1)} %shard_map.113), channel_id=1, source_target_pairs={{1,0},{2,1},{3,2},{4,5},{5,6},{6,7},{9,8},{10,9},{11,10},{12,13},{... | collective-permute-start | bytes 3145736 | tf_op jit(solution)/shard_map/ppermute | solution.py:414

commit v9 on v7

--- a/solution.py
+++ b/solution.py
@@ -82,11 +82,15 @@
     rank, width = B.shape
 
     def kernel(A, B, out, both, sem):
-        wait(fetch([(A, both.at[pl.ds(0, rank)]), (B, both.at[pl.ds(rank, rank)])], sem))
-        wait(fetch([(both, out.at[j]) for j in range(half)], sem, 2))
-
-    return call(
-        kernel, (1,), 0, [HBM, HBM], HBM, array(half, 2 * rank, width), [vmem(2 * rank, width), sems(2 + half)], mib=4
+        outs = []
+        for k, c in enumerate(fetch([(A, both.at[pl.ds(0, rank)]), (B, both.at[pl.ds(rank, rank)])], sem)):
+            c.wait()
+            span = pl.ds(k * rank, rank)
+            outs += fetch([(both.at[span], out.at[j, span]) for j in range(half)], sem, 2 + k * half)
+        wait(outs)
+
+    return call(
+        kernel, (1,), 0, [HBM, HBM], HBM, array(half, 2 * rank, width), [vmem(2 * rank, width), sems(2 + 2 * half)], mib=4
     )(*far(A, B))
 
 
@@ -151,7 +155,7 @@
 
 def add_on(spot, table, at, arrived, backs, cost):
     rows, width = arrived.shape
-    steps = 4
+    steps = 2
     size = rows // steps
     count = backs[0].shape[0]
 

time: 118 us -> 119 us (level)
  transfers between devices with their start and end apart: 17 -> 17, of which waited for: 2 -> 2; matrix products, arithmetic and copies ran while one was open for 0% -> 0% of each run, Pallas kernels for 59% -> 60%
where the time goes in v9:
time: 119 us; the launch traced here: 117 us
  Pallas kernels  72.5 us (61%)
  starting transfers between devices  41.8 us (35%)
  waiting for transfers between devices  1.57 us (1%)
    ppermute x8, starting transfers between devices, along(): return lax.ppermute(x, ('dp', 'tensor'), pairs[k])  25.7 us
    pallas_call x3, Pallas kernels, backward(): call(kernel, (1,), 1, [HBM, HBM], HBM, array(blocks, rows, size), [vmem(r...  21.6 us
    pallas_call x1, Pallas kernels, forward(): call(kernel, (1,), 1, [HBM] * (len(arrays) + 5), [HBM] * 2, [array(rows,...  15.3 us
    pallas_call x6, Pallas kernels, add_on(): call(kernel, (1,), 1, [HBM] * (1 + len(backs)), HBM, array(rows, width),...  13.7 us
    all_to_all x2, starting transfers between devices, swap(): return lax.all_to_all(x, axis, 0, 0, axis_index_groups=groups, tiled=True)  8.93 us
    pallas_call x1, Pallas kernels, adapters(): call(kernel, (1,), 2, [ids_spec(rows)] * 2 + [pl.BlockSpec(memory_space=p...  7.43 us
    ppermute x7, starting transfers between devices, exchange(): return lax.ppermute(x, axis, [(i, i ^ offset) for i in range(size)])  7.15 us
    pallas_call x1, Pallas kernels, low_parts(): call(kernel, (1,), 2, [ids_spec(rows)] * 2 + [HBM] * 5, HBM, array(2 * ro...  6.73 us
  transfers between devices with their start and end apart: 17, of which 2 were waited for; matrix products, arithmetic and copies ran while one was open for 0% of the time, Pallas kernels for 60%

profile of v9, /device:TPU:0, one launch (start us, length us, event | category | flops | bytes accessed | tf_op | source)
XLA Modules:
  0.0 117.0 jit_solution(17894592184328351475)
XLA Ops:
  0.6 0.5 collective-permute-start
  1.1 0.1 collective-permute-start.1
  1.2 0.4 collective-permute-start.2
  1.7 5.5 %collective-permute-start.4 = (bf16[256,2048]{1,0:T(8,128)(2,1)}, bf16[256,2048]{1,0:T(8,128)(2,1)}, u32[]{:S(2)}, u32[]{:S(2)}) collective-permute-start(bf16[256,2048]{1,0:T(8,128)(2,1)} %refs_0_), channel_id=1, source_target_pairs={{0,1},{1,2},{2,3},{5,4},{6,5},{7,6},{8,9},{9,10},{10,11},{13,12},{... | collective-permute-start | bytes 3145736 | tf_op jit(solution)/shard_map/ppermute | solution.py:433
  7.2 0.0 collective-permute-done.2
  7.2 0.0 copy-start.1
  7.2 0.0 collective-permute-done.X_other.refs_5_
  7.2 0.0 collective-permute-done.1.dY_other.refs_7_
  7.2 2.4 %shard_map.102 = bf16[4,128,2048]{2,1,0:T(8,128)(2,1)} custom-call(bf16[64,2048]{1,0:T(8,128)(2,1)} %bitcast.11, bf16[64,2048]{1,0:T(8,128)(2,1)} %bitcast.12), custom_call_target="tpu_custom_call" | custom-call | flops 1000 | bytes 1 | tf_op jit(solution)/shard_map/pallas_call | solution.py:92
  9.6 1.3 %collective-permute-start.3 = (bf16[256,2048]{1,0:T(8,128)(2,1)}, bf16[256,2048]{1,0:T(8,128)(2,1)}, u32[]{:S(2)}, u32[]{:S(2)}) collective-permute-start(bf16[256,2048]{1,0:T(8,128)(2,1)} %refs_0_), channel_id=1, source_target_pairs={{1,0},{2,1},{3,2},{4,5},{5,6},{6,7},{9,8},{10,9},{11,10},{12,13},{... | collective-permute-start | bytes 3145736 | tf_op jit(solution)/shard_map/ppermute | solution.py:433
  10.9 0.0 copy-done.1
  10.9 4.5 %all-to-all-start = ((bf16[4,128,2048]{2,1,0:T(8,128)(2,1)}), bf16[4,128,2048]{2,1,0:T(8,128)(2,1)}, u32[]{:S(2)}, u32[]{:S(2)}) async-start(bf16[4,128,2048]{2,1,0:T(8,128)(2,1)} %shard_map.102), calls=%async_computation | async-start | bytes 4194304 | tf_op jit(solution)/shard_map/all_to_all | solution.py:27
  15.4 9.5 %shard_map.103.refs_0_ = bf16[2,256,2048]{2,1,0:T(8,128)(2,1)} custom-call(s32[1]{0:T(128)} %bitcast.spot, bf16[256,2048]{1,0:T(8,128)(2,1)} %refs_6_.1, bf16[8192,2048]{1,0:T(8,128)(2,1)} %refs_7_.1), custom_call_target="tpu_custom_call" | custom-call | flops 1000 | bytes 1 | tf_op jit(solution)/shard_map/pallas_call | solution.py:145
  24.9 0.0 collective-permute-done.4.arrived.refs_1_
  24.9 2.5 %shard_map.104 = bf16[256,2048]{1,0:T(8,128)(2,1)} custom-call(s32[1]{0:T(128)} %bitcast.spot, bf16[256,2048]{1,0:T(8,128)(2,1)} %collective-permute-done.4.arrived.refs_1_, bf16[2,256,2048]{2,1,0:T(8,128)(2,1)} %shard_map.103.refs_0_), custom_call_target="tpu_custom_call" | custom-call | flops 1000 | bytes 1 | tf_op jit(solution)/shard_map/pallas_call | solution.py:187
  27.4 5.2 %collective-permute-start.6 = (bf16[256,2048]{1,0:T(8,128)(2,1)}, bf16[256,2048]{1,0:T(8,128)(2,1)}, u32[]{:S(2)}, u32[]{:S(2)}) collective-permute-start(bf16[256,2048]{1,0:T(8,128)(2,1)} %shard_map.104), channel_id=1, source_target_pairs={{0,1},{1,2},{2,3},{5,4},{6,5},{7,6},{8,9},{9,10},{10,11},{13,12},{... | collective-permute-start | bytes 3145736 | tf_op jit(solution)/shard_map/ppermute | solution.py:433
  32.6 0.0 collective-permute-done.3.arrived.refs_6_
  32.6 2.1 %shard_map.105 = bf16[256,2048]{1,0:T(8,128)(2,1)} custom-call(s32[1]{0:T(128)} %bitcast.spot, bf16[256,2048]{1,0:T(8,128)(2,1)} %collective-permute-done.3.arrived.refs_6_, bf16[2,256,2048]{2,1,0:T(8,128)(2,1)} %shard_map.103.refs_0_), custom_call_target="tpu_custom_call" | custom-call | flops 10000000000 | bytes 1 | tf_op jit(solution)/shard_map/pallas_call | solution.py:187
  34.7 1.3 %collective-permute-start.5 = (bf16[256,2048]{1,0:T(8,128)(2,1)}, bf16[256,2048]{1,0:T(8,128)(2,1)}, u32[]{:S(2)}, u32[]{:S(2)}) collective-permute-start(bf16[256,2048]{1,0:T(8,128)(2,1)} %shard_map.105), channel_id=1, source_target_pairs={{1,0},{2,1},{3,2},{4,5},{5,6},{6,7},{9,8},{10,9},{11,10},{12,13},{... | collective-permute-start | bytes 3145736 | tf_op jit(solution)/shard_map/ppermute | solution.py:433
  36.0 6.0 %shard_map.106.refs_1_ = bf16[1,256,2048]{2,1,0:T(8,128)(2,1)} custom-call(s32[1]{0:T(128)} %bitcast.spot, bf16[256,2048]{1,0:T(8,128)(2,1)} %refs_6_.1, bf16[8192,2048]{1,0:T(8,128)(2,1)} %refs_7_.1), custom_call_target="tpu_custom_call" | custom-call | flops 1000 | bytes 1 | tf_op jit(solution)/shard_map/pallas_call | solution.py:145
  42.0 0.0 all-to-all-done.gathered.refs_8_
  42.1 6.7 %shard_map.107.refs_0_ = bf16[512,128]{1,0:T(8,128)(2,1)} custom-call(s32[1]{0:T(128)} %bitcast.spot, s32[8]{0:T(128)} %slots.3, s32[1,256]{1,0:T(1,128)} %bitcast.13, s32[1,256]{1,0:T(1,128)} %bitcast.15, bf16[256,2048]{1,0:T(8,128)(2,1)} %refs_0_, bf16[256,2048]{1,0:T(8,128)(2,1)} %collective-permute-done.X_other.refs_5_, bf16[256,2048]{1,0:T(8,128)(2,1)} %refs_6_.1, ...), custom_call_target="tpu_custom_call" | custom-call | flops 1000 | bytes 1 | tf_op jit(solution)/shard_map/pallas_call | solution.py:360
  48.8 5.2 %collective-permute-start.11 = (bf16[512,128]{1,0:T(8,128)(2,1)}, bf16[512,128]{1,0:T(8,128)(2,1)S(1)}, u32[]{:S(2)}, u32[]{:S(2)}) collective-permute-start(bf16[512,128]{1,0:T(8,128)(2,1)} %shard_map.107.refs_0_), channel_id=1, source_target_pairs={{0,3},{1,2},{2,1},{3,0},{4,7},{5,6},{6,5},{7,4},{8,11},{9,10},{10,... | collective-permute-start | bytes 393224 | tf_op jit(solution)/shard_map/ppermute | solution.py:23
  54.0 0.0 collective-permute-start.10
  54.0 0.6 collective-permute-start.9
  54.6 0.0 collective-permute-done.6.arrived.refs_3_
  54.6 2.5 %shard_map.108 = bf16[256,2048]{1,0:T(8,128)(2,1)} custom-call(s32[1]{0:T(128)} %bitcast.spot, bf16[256,2048]{1,0:T(8,128)(2,1)} %collective-permute-done.6.arrived.refs_3_, bf16[2,256,2048]{2,1,0:T(8,128)(2,1)} %shard_map.103.refs_0_, bf16[1,256,2048]{2,1,0:T(8,128)(2,1)} %shard_map.106.refs_1_), custom_call_target="tpu_custom_call" | custom-call | flops 1000 | bytes 1 | tf_op jit(solution)/shard_map/pallas_call | solution.py:187
  57.1 4.3 %collective-permute-start.8 = (bf16[256,2048]{1,0:T(8,128)(2,1)}, bf16[256,2048]{1,0:T(8,128)(2,1)}, u32[]{:S(2)}, u32[]{:S(2)}) collective-permute-start(bf16[256,2048]{1,0:T(8,128)(2,1)} %shard_map.108), channel_id=1, source_target_pairs={{0,1},{1,2},{2,3},{5,4},{6,5},{7,6},{8,9},{9,10},{10,11},{13,12},{... | collective-permute-start | bytes 3145736 | tf_op jit(solution)/shard_map/ppermute | solution.py:433
  61.4 6.0 %shard_map.109.refs_11_ = bf16[1,256,2048]{2,1,0:T(8,128)(2,1)} custom-call(s32[1]{0:T(128)} %bitcast.spot, bf16[256,2048]{1,0:T(8,128)(2,1)} %refs_6_.1, bf16[8192,2048]{1,0:T(8,128)(2,1)} %refs_7_.1), custom_call_target="tpu_custom_call" | custom-call | flops 1000 | bytes 1 | tf_op jit(solution)/shard_map/pallas_call | solution.py:145
  67.4 0.0 copy-start
  67.4 0.0 collective-permute-done.5.arrived.refs_4_
  67.4 2.1 %shard_map.110 = bf16[256,2048]{1,0:T(8,128)(2,1)} custom-call(s32[1]{0:T(128)} %bitcast.spot, bf16[256,2048]{1,0:T(8,128)(2,1)} %collective-permute-done.5.arrived.refs_4_, bf16[2,256,2048]{2,1,0:T(8,128)(2,1)} %shard_map.103.refs_0_, bf16[1,256,2048]{2,1,0:T(8,128)(2,1)} %shard_map.106.refs_1_), custom_call_target="tpu_custom_call" | custom-call | flops 1000 | bytes 1 | tf_op jit(solution)/shard_map/pallas_call | solution.py:187
  69.5 1.3 %collective-permute-start.7 = (bf16[256,2048]{1,0:T(8,128)(2,1)}, bf16[256,2048]{1,0:T(8,128)(2,1)}, u32[]{:S(2)}, u32[]{:S(2)}) collective-permute-start(bf16[256,2048]{1,0:T(8,128)(2,1)} %shard_map.110), channel_id=1, source_target_pairs={{1,0},{2,1},{3,2},{4,5},{5,6},{6,7},{9,8},{10,9},{11,10},{12,13},{... | collective-permute-start | bytes 3145736 | tf_op jit(solution)/shard_map/ppermute | solution.py:433
  70.8 0.0 collective-permute-done.11.refs_3_
  70.8 0.4 collective-permute-done.10.refs_2_
  71.2 0.0 collective-permute-done.9.refs_1_
  71.3 0.0 copy-done
  71.3 7.4 %shard_map.111 = (bf16[4,128,2048]{2,1,0:T(8,128)(2,1)}, bf16[256,2048]{1,0:T(8,128)(2,1)}, bf16[256,2048]{1,0:T(8,128)(2,1)}, bf16[512,2048]{1,0:T(8,128)(2,1)}) custom-call(s32[1]{0:T(128)} %bitcast.spot, s32[8]{0:T(128)} %slots.3, s32[1,256]{1,0:T(1,128)} %bitcast.14, s32[1,256]{1,0:T(1,128)} %bitcast.16, bf16[512,128]{1,0:T(8,128)(2,1)S(1)} %copy-done, ...), custom_call_target="tpu_custom_call" | custom-call | flops 10000000000 | bytes 1 | tf_op jit(solution)/shard_map/pallas_call | solution.py:405
  78.7 4.5 %all-to-all-start.1 = ((bf16[4,128,2048]{2,1,0:T(8,128)(2,1)}), bf16[4,128,2048]{2,1,0:T(8,128)(2,1)}, u32[]{:S(2)}, u32[]{:S(2)}) async-start(bf16[4,128,2048]{2,1,0:T(8,128)(2,1)} %get-tuple-element.53), calls=%async_computation.1 | async-start | bytes 4194304 | tf_op jit(solution)/shard_map/all_to_all | solution.py:27
  83.2 0.3 collective-permute-start.12
  83.5 0.0 collective-permute-done.8.arrived.refs_5_
  83.5 2.5 %shard_map.112 = bf16[256,2048]{1,0:T(8,128)(2,1)} custom-call(s32[1]{0:T(128)} %bitcast.spot, bf16[256,2048]{1,0:T(8,128)(2,1)} %collective-permute-done.8.arrived.refs_5_, bf16[2,256,2048]{2,1,0:T(8,128)(2,1)} %shard_map.103.refs_0_, bf16[1,256,2048]{2,1,0:T(8,128)(2,1)} %shard_map.106.refs_1_), custom_call_target="tpu_custom_call" | custom-call | flops 999999995904 | bytes 1 | tf_op jit(solution)/shard_map/pallas_call | solution.py:187
  86.0 5.3 %collective-permute-start.13 = (bf16[256,2048]{1,0:T(8,128)(2,1)}, bf16[256,2048]{1,0:T(8,128)(2,1)}, u32[]{:S(2)}, u32[]{:S(2)}) collective-permute-start(bf16[256,2048]{1,0:T(8,128)(2,1)} %shard_map.112), channel_id=1, source_target_pairs={{0,1},{1,2},{2,3},{5,4},{6,5},{7,6},{8,9},{9,10},{10,11},{13,12},{... | collective-permute-start | bytes 3145736 | tf_op jit(solution)/shard_map/ppermute | solution.py:433
  91.3 0.0 collective-permute-done.7.arrived.refs_2_
  91.3 2.1 %shard_map.113 = bf16[256,2048]{1,0:T(8,128)(2,1)} custom-call(s32[1]{0:T(128)} %bitcast.spot, bf16[256,2048]{1,0:T(8,128)(2,1)} %collective-permute-done.7.arrived.refs_2_, bf16[2,256,2048]{2,1,0:T(8,128)(2,1)} %shard_map.103.refs_0_, bf16[1,256,2048]{2,1,0:T(8,128)(2,1)} %shard_map.106.refs_1_), custom_call_target="tpu_custom_call" | custom-call | flops 999999995904 | bytes 1 | tf_op jit(solution)/shard_map/pallas_call | solution.py:187
  93.3 1.5 %collective-permute-start.14 = (bf16[256,2048]{1,0:T(8,128)(2,1)}, bf16[256,2048]{1,0:T(8,128)(2,1)}, u32[]{:S(2)}, u32[]{:S(2)}) collective-permute-start(bf16[256,2048]{1,0:T(8,128)(2,1)} %shard_map.113), channel_id=1, source_target_pairs={{1,0},{2,1},{3,2},{4,5},{5,6},{6,7},{9,8},{10,9},{11,10},{12,13},{... | collective-permute-start | bytes 3145736 | tf_op jit(solution)/shard_map/ppermute | solution.py:433
  94.9 0.0 collective-permute-done.12.refs_10_
  94.9 15.3 %shard_map.114 = (bf16[256,2048]{1,0:T(8,128)(2,1)}, bf16[256,2048]{1,0:T(8,128)(2,1)}) custom-call(s32[1]{0:T(128)} %bitcast.spot, bf16[256,2048]{1,0:T(8,128)(2,1)} %refs_0_, bf16[256,2048]{1,0:T(8,128)(2,1)} %collective-permute-done.4.arrived.refs_1_, bf16[256,2048]{1,0:T(8,128)(2,1)} %collective-permute-done.7.arrived.refs_2_, ...), custom_call_target="tpu_custom_call" | custom-call | flops 1000 | bytes 1 | tf_op jit(solution)/shard_map/pallas_call | solution.py:296
  110.2 0.0 all-to-all-done.1.blocks
  110.2 2.7 %shard_map.115 = (bf16[64,2048]{1,0:T(8,128)(2,1)}, bf16[64,2048]{1,0:T(8,128)(2,1)}) custom-call(bf16[4,128,2048]{2,1,0:T(8,128)(2,1)} %all-to-all-done.1.blocks), custom_call_target="tpu_custom_call" | custom-call | flops 1000 | bytes 1 | tf_op jit(solution)/shard_map/pallas_call | solution.py:239
  112.9 0.0 collective-permute-done.13.one
  112.9 1.1 collective-permute-done.14.two
  114.0 2.8 %shard_map.116 = bf16[256,2048]{1,0:T(8,128)(2,1)} custom-call(bf16[256,2048]{1,0:T(8,128)(2,1)} %collective-permute-done.13.one, bf16[256,2048]{1,0:T(8,128)(2,1)} %collective-permute-done.14.two, bf16[256,2048]{1,0:T(8,128)(2,1)} %get-tuple-element.56.rest), custom_call_target="tpu_custom_call" | custom-call | flops 1000 | bytes 1 | tf_op jit(solution)/shard_map/pallas_call | solution.py:219
Async XLA Ops:
  0.6 6.6 %collective-permute-start = (bf16[256,2048]{1,0:T(8,128)(2,1)}, bf16[256,2048]{1,0:T(8,128)(2,1)}, u32[]{:S(2)}, u32[]{:S(2)}) collective-permute-start(bf16[256,2048]{1,0:T(8,128)(2,1)} %refs_0_), channel_id=1, source_target_pairs={{0,4},{4,0},{8,12},{12,8},{16,20},{20,16},{24,28},{28,24},{1,5},{5... | collective-permute-start | bytes 3145736 | tf_op jit(solution)/shard_map/ppermute | solution.py:23
  1.1 6.1 %collective-permute-start.1 = (bf16[256,2048]{1,0:T(8,128)(2,1)}, bf16[256,2048]{1,0:T(8,128)(2,1)}, u32[]{:S(2)}, u32[]{:S(2)}) collective-permute-start(bf16[256,2048]{1,0:T(8,128)(2,1)} %refs_6_.1), channel_id=1, source_target_pairs={{0,4},{4,0},{8,12},{12,8},{16,20},{20,16},{24,28},{28,24},{1,5},{5... | collective-permute-start | bytes 3145736 | tf_op jit(solution)/shard_map/ppermute | solution.py:23
  1.2 6.0 %collective-permute-start.2 = (s32[256,1]{0,1:T(1,128)}, s32[256,1]{0,1:T(1,128)S(1)}, u32[]{:S(2)}, u32[]{:S(2)}) collective-permute-start(s32[256,1]{0,1:T(1,128)} %param.12), channel_id=1, source_target_pairs={{0,4},{4,0},{8,12},{12,8},{16,20},{20,16},{24,28},{28,24},{1,5},{5... | collective-permute-start | bytes 3080 | tf_op jit(solution)/shard_map/ppermute | solution.py:23
  1.7 23.3 %collective-permute-start.4 = (bf16[256,2048]{1,0:T(8,128)(2,1)}, bf16[256,2048]{1,0:T(8,128)(2,1)}, u32[]{:S(2)}, u32[]{:S(2)}) collective-permute-start(bf16[256,2048]{1,0:T(8,128)(2,1)} %refs_0_), channel_id=1, source_target_pairs={{0,1},{1,2},{2,3},{5,4},{6,5},{7,6},{8,9},{9,10},{10,11},{13,12},{... | collective-permute-start | bytes 3145736 | tf_op jit(solution)/shard_map/ppermute | solution.py:433
  7.2 3.7 %copy-start.1 = (s32[256,1]{0,1:T(1,128)}, s32[256,1]{0,1:T(1,128)S(1)}, u32[]{:S(2)}) copy-start(s32[256,1]{0,1:T(1,128)S(1)} %collective-permute-done.2) | copy-start | bytes 3076
  9.6 23.1 %collective-permute-start.3 = (bf16[256,2048]{1,0:T(8,128)(2,1)}, bf16[256,2048]{1,0:T(8,128)(2,1)}, u32[]{:S(2)}, u32[]{:S(2)}) collective-permute-start(bf16[256,2048]{1,0:T(8,128)(2,1)} %refs_0_), channel_id=1, source_target_pairs={{1,0},{2,1},{3,2},{4,5},{5,6},{6,7},{9,8},{10,9},{11,10},{12,13},{... | collective-permute-start | bytes 3145736 | tf_op jit(solution)/shard_map/ppermute | solution.py:433
  10.9 31.2 %all-to-all-start = ((bf16[4,128,2048]{2,1,0:T(8,128)(2,1)}), bf16[4,128,2048]{2,1,0:T(8,128)(2,1)}, u32[]{:S(2)}, u32[]{:S(2)}) async-start(bf16[4,128,2048]{2,1,0:T(8,128)(2,1)} %shard_map.102), calls=%async_computation | async-start | bytes 4194304 | tf_op jit(solution)/shard_map/all_to_all | solution.py:27
  27.4 27.2 %collective-permute-start.6 = (bf16[256,2048]{1,0:T(8,128)(2,1)}, bf16[256,2048]{1,0:T(8,128)(2,1)}, u32[]{:S(2)}, u32[]{:S(2)}) collective-permute-start(bf16[256,2048]{1,0:T(8,128)(2,1)} %shard_map.104), channel_id=1, source_target_pairs={{0,1},{1,2},{2,3},{5,4},{6,5},{7,6},{8,9},{9,10},{10,11},{13,12},{... | collective-permute-start | bytes 3145736 | tf_op jit(solution)/shard_map/ppermute | solution.py:433
  34.7 32.7 %collective-permute-start.5 = (bf16[256,2048]{1,0:T(8,128)(2,1)}, bf16[256,2048]{1,0:T(8,128)(2,1)}, u32[]{:S(2)}, u32[]{:S(2)}) collective-permute-start(bf16[256,2048]{1,0:T(8,128)(2,1)} %shard_map.105), channel_id=1, source_target_pairs={{1,0},{2,1},{3,2},{4,5},{5,6},{6,7},{9,8},{10,9},{11,10},{12,13},{... | collective-permute-start | bytes 3145736 | tf_op jit(solution)/shard_map/ppermute | solution.py:433
  48.8 22.0 %collective-permute-start.11 = (bf16[512,128]{1,0:T(8,128)(2,1)}, bf16[512,128]{1,0:T(8,128)(2,1)S(1)}, u32[]{:S(2)}, u32[]{:S(2)}) collective-permute-start(bf16[512,128]{1,0:T(8,128)(2,1)} %shard_map.107.refs_0_), channel_id=1, source_target_pairs={{0,3},{1,2},{2,1},{3,0},{4,7},{5,6},{6,5},{7,4},{8,11},{9,10},{10,... | collective-permute-start | bytes 393224 | tf_op jit(solution)/shard_map/ppermute | solution.py:23
  54.0 17.3 %collective-permute-start.10 = (bf16[512,128]{1,0:T(8,128)(2,1)}, bf16[512,128]{1,0:T(8,128)(2,1)S(1)}, u32[]{:S(2)}, u32[]{:S(2)}) collective-permute-start(bf16[512,128]{1,0:T(8,128)(2,1)} %shard_map.107.refs_0_), channel_id=1, source_target_pairs={{0,2},{1,3},{2,0},{3,1},{4,6},{5,7},{6,4},{7,5},{8,10},{9,11},{10,... | collective-permute-start | bytes 393224 | tf_op jit(solution)/shard_map/ppermute | solution.py:23
  54.0 17.3 %collective-permute-start.9 = (bf16[512,128]{1,0:T(8,128)(2,1)}, bf16[512,128]{1,0:T(8,128)(2,1)S(1)}, u32[]{:S(2)}, u32[]{:S(2)}) collective-permute-start(bf16[512,128]{1,0:T(8,128)(2,1)} %shard_map.107.refs_0_), channel_id=1, source_target_pairs={{0,1},{1,0},{2,3},{3,2},{4,5},{5,4},{6,7},{7,6},{8,9},{9,8},{10,11... | collective-permute-start | bytes 393224 | tf_op jit(solution)/shard_map/ppermute | solution.py:23
  57.1 26.4 %collective-permute-start.8 = (bf16[256,2048]{1,0:T(8,128)(2,1)}, bf16[256,2048]{1,0:T(8,128)(2,1)}, u32[]{:S(2)}, u32[]{:S(2)}) collective-permute-start(bf16[256,2048]{1,0:T(8,128)(2,1)} %shard_map.108), channel_id=1, source_target_pairs={{0,1},{1,2},{2,3},{5,4},{6,5},{7,6},{8,9},{9,10},{10,11},{13,12},{... | collective-permute-start | bytes 3145736 | tf_op jit(solution)/shard_map/ppermute | solution.py:433
  67.4 3.9 %copy-start = (bf16[512,128]{1,0:T(8,128)(2,1)S(1)}, bf16[512,128]{1,0:T(8,128)(2,1)}, u32[]{:S(2)}) copy-start(bf16[512,128]{1,0:T(8,128)(2,1)} %shard_map.107.refs_0_) | copy-start | bytes 393220
  69.5 21.7 %collective-permute-start.7 = (bf16[256,2048]{1,0:T(8,128)(2,1)}, bf16[256,2048]{1,0:T(8,128)(2,1)}, u32[]{:S(2)}, u32[]{:S(2)}) collective-permute-start(bf16[256,2048]{1,0:T(8,128)(2,1)} %shard_map.110), channel_id=1, source_target_pairs={{1,0},{2,1},{3,2},{4,5},{5,6},{6,7},{9,8},{10,9},{11,10},{12,13},{... | collective-permute-start | bytes 3145736 | tf_op jit(solution)/shard_map/ppermute | solution.py:433
  78.7 31.5 %all-to-all-start.1 = ((bf16[4,128,2048]{2,1,0:T(8,128)(2,1)}), bf16[4,128,2048]{2,1,0:T(8,128)(2,1)}, u32[]{:S(2)}, u32[]{:S(2)}) async-start(bf16[4,128,2048]{2,1,0:T(8,128)(2,1)} %get-tuple-element.53), calls=%async_computation.1 | async-start | bytes 4194304 | tf_op jit(solution)/shard_map/all_to_all | solution.py:27
  83.2 11.7 %collective-permute-start.12 = (bf16[512,2048]{1,0:T(8,128)(2,1)}, bf16[512,2048]{1,0:T(8,128)(2,1)}, u32[]{:S(2)}, u32[]{:S(2)}) collective-permute-start(bf16[512,2048]{1,0:T(8,128)(2,1)} %get-tuple-element.45), channel_id=1, source_target_pairs={{0,4},{4,0},{8,12},{12,8},{16,20},{20,16},{24,28},{28,24},{1,5},{5... | collective-permute-start | bytes 6291464 | tf_op jit(solution)/shard_map/ppermute | solution.py:23
  86.0 26.9 %collective-permute-start.13 = (bf16[256,2048]{1,0:T(8,128)(2,1)}, bf16[256,2048]{1,0:T(8,128)(2,1)}, u32[]{:S(2)}, u32[]{:S(2)}) collective-permute-start(bf16[256,2048]{1,0:T(8,128)(2,1)} %shard_map.112), channel_id=1, source_target_pairs={{0,1},{1,2},{2,3},{5,4},{6,5},{7,6},{8,9},{9,10},{10,11},{13,12},{... | collective-permute-start | bytes 3145736 | tf_op jit(solution)/shard_map/ppermute | solution.py:433
  93.3 20.7 %collective-permute-start.14 = (bf16[256,2048]{1,0:T(8,128)(2,1)}, bf16[256,2048]{1,0:T(8,128)(2,1)}, u32[]{:S(2)}, u32[]{:S(2)}) collective-permute-start(bf16[256,2048]{1,0:T(8,128)(2,1)} %shard_map.113), channel_id=1, source_target_pairs={{1,0},{2,1},{3,2},{4,5},{5,6},{6,7},{9,8},{10,9},{11,10},{12,13},{... | collective-permute-start | bytes 3145736 | tf_op jit(solution)/shard_map/ppermute | solution.py:433
